TPU v7x, 512 devices: a whole 4x4x16 slice. The times are simulated.
512 devices in a mesh: row: 32 (over z_lo, y), col: 16 (over x, z_hi, core).
Axes of the slice: x: 4, y: 4, z: 16 (z_hi: 2, z_lo: 8; z = z_hi * 8 + z_lo), core: 2. Of those that a mesh axis runs over, the one named last changes fastest.
Arguments:
- split_at: int32 [1], replicated, may hold values from 65536 to 196607
- slab: float32 [1536, 262144], P('row', 'col'), may hold values from -6 to 6
- vectors: float32 [262144, 256], P(('col', 'row')), may hold values from -0.046875 to 0.046875
Outputs:
- eigvecs: float32 [1536, 512], P('row', 'col')
All inputs are finite; a program needn't handle non-finite values.
Results may differ from a plain program's by a relative error of at most 0.0003.
Values sent between devices are 32-bit elements; how exact they have to be, the bound alone decides.
No kernel may reach another device: no remote copies, remote signals or barrier semaphores. Data moves between devices by JAX's collectives and lax.ppermute only.
A program may use at most 64 MiB of HBM per device.

v0:
```python
import jax
import jax.numpy as jnp
from jax import lax
from jax.sharding import PartitionSpec as P


def keep_mask(offset, count, split_at):
    positions = offset + jnp.arange(count, dtype=jnp.int32)
    return (positions < split_at[0]).astype(jnp.float32)


def both_children(basis, rows_piece, offset, split_at):
    keep = keep_mask(offset, basis.shape[1], split_at)
    left = basis * keep[None, :]
    first_add = jnp.dot(
        left, rows_piece, precision=lax.Precision.HIGHEST, preferred_element_type=jnp.float32
    )
    second_add = jnp.dot(
        basis - left,
        rows_piece,
        precision=lax.Precision.HIGHEST,
        preferred_element_type=jnp.float32,
    )
    return jnp.concatenate([first_add, second_add], axis=1)


def local(split_at, slab, vectors):
    cols_local = slab.shape[1]
    first_col = lax.axis_index("col") * cols_local
    partial_sum = both_children(
        slab, lax.all_gather(vectors, "row", axis=0, tiled=True), first_col, split_at
    )
    return lax.psum_scatter(partial_sum, "col", scatter_dimension=1, tiled=True)


def solution(mesh):
    placed = (P(), P("row", "col"), P(("col", "row"), None))
    return jax.shard_map(
        local, mesh=mesh, in_specs=placed, out_specs=P("row", "col"), check_vma=False
    )
```

profile of v0, /device:TPU:1, one launch (start us, length us, event | category | flops | bytes accessed | tf_op | source)
XLA Modules:
  0.0 392.0 jit_solution(17618077848149503565)
XLA Ops:
  6.5 0.0 all-gather.2.cloned.1.call-start
  6.5 0.7 all-gather.2.cloned.1.call-update
  7.3 0.0 reduce-scatter.4.cloned.1.call-start
  8.0 0.0 copy-start.1
  8.0 246.6 %all-gather.2.cloned.1.call-done = f32[16384,256]{1,0:T(8,128)} async-done(((f32[512,256]{1,0:T(8,128)}), f32[16384,256]{1,0:T(8,128)}) %all-gather.2.cloned.1.call-update) | async-done | bytes 16777232 | tf_op jit(solution)/shard_map/all_gather | solution.py:31
  254.6 0.0 copy-start
  254.6 14.9 %fusion.2 = f32[48,256]{1,0:T(8,128)S(1)} fusion(f32[16384,256]{1,0:T(8,128)} %all-gather.2.cloned.1.call-done, f32[48,16384]{1,0:T(8,128)} %param.4, f32[16384]{0:T(1024)S(1)} %fusion.5), kind=kOutput, calls=%fused_computation.3 | convolution fusion | flops 2417491968 | bytes 20037632 | tf_op jit(solution)/shard_map/dot_general | solution.py:18
  269.5 0.0 copy-done.1
  269.5 0.0 copy-done
  269.6 8.5 %fusion = f32[48,256]{1,0:T(8,128)S(1)} fusion(f32[16384,256]{1,0:T(8,128)S(1)} %copy-done, f32[48,16384]{1,0:T(8,128)S(1)} %copy-done.1, f32[16384]{0:T(1024)S(1)} %fusion.5), kind=kOutput, calls=%fused_computation.1 | convolution fusion | flops 2416705536 | bytes 20037632 | tf_op jit(solution)/shard_map/dot_general | solution.py:15
  278.1 0.8 copy.6
  278.9 0.0 reduce-scatter.4.cloned.1.call-update
  278.9 106.2 %reduce-scatter.4.cloned.1.call-done = f32[32,48]{1,0:T(8,128)} async-done(((f32[512,48]{1,0:T(8,128)}), f32[32,48]{1,0:T(8,128)}) %reduce-scatter.4.cloned.1.call-update) | async-done | bytes 6160
  (2 shorter events, 0.0 us)
Async XLA Ops:
  6.5 248.1 %all-gather.2.cloned.1.call-start = ((), (), s32[]{:S(2)}) async-start(), calls=%async_computation.1 | async-start | bytes 17301504 | tf_op jit(solution)/shard_map/all_gather | solution.py:31
  7.3 377.9 %reduce-scatter.4.cloned.1.call-start = ((), (), s32[]{:S(2)}) async-start(), calls=%async_computation.2 | async-start | bytes 278528
  8.0 261.6 %copy-start.1 = (f32[48,16384]{1,0:T(8,128)S(1)}, f32[48,16384]{1,0:T(8,128)}, u32[]{:S(2)}) copy-start(f32[48,16384]{1,0:T(8,128)} %param.4) | copy-start | bytes 9437188
  254.6 14.9 %copy-start = (f32[16384,256]{1,0:T(8,128)S(1)}, f32[16384,256]{1,0:T(8,128)}, u32[]{:S(2)}) copy-start(f32[16384,256]{1,0:T(8,128)} %all-gather.2.cloned.1.call-done) | copy-start | bytes 50331652
Sparse Core Ops, SparseCore 0:
  9.4 245.1 all-gather.1
  279.1 106.0 reduce-scatter.3
where the time goes:
time: 393 us; the launch traced here: 392 us
  waiting for transfers between devices  354 us (90%)
  matrix products  23.4 us (6%)
  between operations  14.1 us (4%)
    all_gather x1, waiting for transfers between devices, local(): lax.all_gather(vectors, 'row', axis=0, tiled=True)  247 us
    unnamed x3, waiting for transfers between devices  107 us
    dot_general x1, matrix products, both_children(): jnp.dot(basis - left, rows_piece, precision=lax.Precision.HIGHEST, prefer...  14.9 us
    dot_general x1, matrix products, both_children(): jnp.dot(left, rows_piece, precision=lax.Precision.HIGHEST, preferred_elem...  8.5 us
  transfers between devices with their start and end apart: 2, of which 2 were waited for; matrix products, arithmetic and copies ran while one was open for 0% of the time, Pallas kernels for 0%

commit v1 on v0

v1 whole, which is shorter than its diff:
```python
import functools

import jax
import jax.numpy as jnp
from jax import lax
from jax.experimental import pallas as pl
from jax.experimental.pallas import tpu as pltpu
from jax.sharding import Mesh, PartitionSpec as P

AXES = ("z", "y", "x", "half", "core")
SIZES = (8, 4, 4, 2, 2)
Z, Y, X = SIZES[:3]
F32, BF16 = jnp.float32, jnp.bfloat16


def pack_kernel(chunk, slab, *refs):
    outs, sems = refs[:Y], refs[Y]
    y = lax.axis_index("y")
    copies = []
    for k in range(Y):
        to = lax.rem(y + k, Y)
        for z in range(Z):
            start = pl.multiple_of((z * Y + to) * chunk, chunk)
            copies.append(
                pltpu.make_async_copy(
                    slab.at[:, pl.ds(start, chunk)],
                    outs[k].at[:, pl.ds(z * chunk, chunk)],
                    sems.at[k, z],
                )
            )
    for copy in copies:
        copy.start()
    for copy in copies:
        copy.wait()


def pack(slab, chunk):
    rows = slab.shape[0]
    return pl.pallas_call(
        functools.partial(pack_kernel, chunk),
        out_shape=[jax.ShapeDtypeStruct((rows, Z * chunk), F32)] * Y,
        in_specs=[pl.BlockSpec(memory_space=pl.ANY)],
        out_specs=[pl.BlockSpec(memory_space=pl.ANY)] * Y,
        scratch_shapes=[pltpu.SemaphoreType.DMA((Y, Z))],
        name="pack_slab",
    )(slab)


def halves(a):
    high = a.astype(BF16)
    return high, (a - high.astype(F32)).astype(BF16)


def product(a, b):
    a_high, a_low = halves(a)
    b_high, b_low = halves(b)
    dot = functools.partial(jnp.dot, preferred_element_type=F32)
    return dot(a_high, b_high) + (dot(a_high, b_low) + dot(a_low, b_high))


def add_kernel(offsets, first, last, info, *refs):
    total = refs[-1]
    out = refs[-2] if last else total
    if first:
        total[...] = jnp.zeros_like(total)
    else:
        total[...] = refs[len(offsets) * (Y + 1)][...]
    split, z, y, col = (info[i] for i in range(4))
    for i, off in enumerate(offsets):
        basis, vec = refs[i * (Y + 1) : i * (Y + 1) + Y], refs[i * (Y + 1) + Y]
        chunk = vec.shape[0]
        valid = (z + off >= 0) & (z + off < Z)
        start = ((col * Z + z + off) * Y + y) * chunk
        one_side = (start + chunk <= split) | (start >= split)

        @pl.when(valid & one_side)
        def _():
            lhs = jnp.concatenate([b[...] for b in basis], axis=0)
            side = (start >= split).astype(jnp.int32)
            total[side] += product(lhs, vec[...])

        @pl.when(valid & jnp.logical_not(one_side))
        def _():
            lhs = jnp.concatenate([b[...] for b in basis], axis=0)
            at = start + lax.broadcasted_iota(jnp.int32, lhs.shape, 1)
            left = jnp.where(at < split, lhs, 0.0)
            right = jnp.where(at < split, 0.0, lhs)
            total[0] += product(left, vec[...])
            total[1] += product(right, vec[...])

    if last:
        rows, wide = out.shape[1:]
        for k in range(Y):
            to = lax.rem(y + Y - k, Y)
            for x in range(X):
                part = total[x // 2, k * rows : (k + 1) * rows, (x % 2) * wide : (x % 2 + 1) * wide]
                out[to * X + x] = part


def add_chunks(info, basis, pieces, total, last=False):
    rows, chunk, cols = basis[0].shape[0], pieces[0][0].shape[0], pieces[0][0].shape[1]
    specs, args = [], []
    for vec, off in pieces:
        specs += [
            pl.BlockSpec(
                (rows, chunk), functools.partial(lambda off, g, s: (0, jnp.clip(s[1] + off, 0, Z - 1)), off)
            )
        ] * Y
        specs.append(pl.BlockSpec((chunk, cols), lambda g, s: (0, 0)))
        args += [*basis, vec]
    shape = (2, Y * rows, cols)
    whole = pl.BlockSpec(shape, lambda g, s: (0, 0, 0))
    if total is not None:
        specs.append(whole)
        args.append(total)
    out = (Y * X, rows, cols // 2) if last else shape
    flops = len(pieces) * 6 * Y * rows * chunk * cols
    return pl.pallas_call(
        functools.partial(add_kernel, [off for _, off in pieces], total is None, last),
        out_shape=jax.ShapeDtypeStruct(out, F32),
        grid_spec=pltpu.PrefetchScalarGridSpec(
            num_scalar_prefetch=1,
            grid=(1,),
            in_specs=specs,
            out_specs=pl.BlockSpec(out, lambda g, s: (0, 0, 0)),
            scratch_shapes=[pltpu.VMEM(shape, F32)] if last else [],
        ),
        input_output_aliases={} if total is None or last else {len(args): 0},
        compiler_params=pltpu.CompilerParams(vmem_limit_bytes=32 << 20),
        cost_estimate=pl.CostEstimate(flops=flops, bytes_accessed=4 << 20, transcendentals=0),
        name="add_chunks",
    )(info, *args)


def shift(a, axis, size, by):
    return lax.ppermute(a, axis, [(i, (i + by) % size) for i in range(size)])


def local(split_at, slab, vectors):
    chunk = vectors.shape[0]
    rows = slab.shape[0]
    at = {axis: lax.axis_index(axis) for axis in AXES}
    col = (at["x"] * 2 + at["half"]) * 2 + at["core"]
    info = jnp.stack([split_at[0], at["z"], at["y"], col])
    up = [(i, i + 1) for i in range(Z - 1)]
    down = [(i + 1, i) for i in range(Z - 1)]

    with jax.named_scope("basis_by_y"):
        packed = pack(slab, chunk)
    below, above = [vectors], [vectors]
    basis = [packed[0], None, None, None]
    for step in range(1, Z):
        if step == 2:
            below[-1], above[-1], packed = lax.optimization_barrier((below[-1], above[-1], packed))
        ready = {3: (1,), 4: (3,), 5: (2,)}.get(step, ())
        for k in ready:
            with jax.named_scope("basis_along_y"):
                basis[k] = shift(packed[k], "y", Y, k)
        if ready:
            below[-1], above[-1], basis = lax.optimization_barrier((below[-1], above[-1], basis))
        with jax.named_scope("vectors_along_z"):
            below.append(lax.ppermute(below[-1], "z", up))
            above.append(lax.ppermute(above[-1], "z", down))

    total = add_chunks(info, basis, [(vectors, 0)], None)
    for step in range(1, Z):
        pieces = [(below[step], -step), (above[step], step)]
        total = add_chunks(info, basis, pieces, total, step == Z - 1)

    with jax.named_scope("sum_over_columns"):
        got = lax.all_to_all(total, ("y", "x"), 0, 0, tiled=True)
        mine = jnp.sum(got, axis=0)
        mine = mine + shift(mine, "core", 2, 1)
        mine = mine + shift(mine, "half", 2, 1)
        wide = mine.shape[1] // 4
        return lax.dynamic_slice(mine, (0, (at["half"] * 2 + at["core"]) * wide), (rows, wide))


def solution(mesh):
    split_mesh = Mesh(mesh.devices.reshape(SIZES), AXES)
    placed = (P(), P(("z", "y"), ("x", "half", "core")), P(("x", "half", "core", "z", "y"), None))
    return jax.shard_map(
        local, mesh=split_mesh, in_specs=placed,
        out_specs=P(("z", "y"), ("x", "half", "core")), check_vma=False,
    )
```

time: 393 us -> 244 us (0.62)
  waiting for transfers between devices: 354 us -> 34.2 us
  Pallas kernels: 0 us -> 107 us
  starting transfers between devices: 0.04 us -> 77.2 us
  matrix products: 23.4 us -> 0 us
  blocking collectives: 0 us -> 13.1 us
  between operations: 14.1 us -> 1.01 us
  local copies, waits for them, and re-layouts: 0.84 us -> 9.85 us
    all_gather x1 -> x0, waiting for transfers between devices: 247 us -> none  [local(): lax.all_gather(vectors, 'row', axis=0, tiled=True)]
    unnamed x3 -> x0, waiting for transfers between devices: 107 us -> none
    pallas_call x0 -> x9, Pallas kernels: none -> 107 us  [the longest x1 96.7 us: pack(): pl.pallas_call(functools.partial(pack_kernel, chunk), out_shape=[jax.Shap...]
    ppermute x0 -> x19, starting transfers between devices: none -> 77.2 us  [the longest x7 34.4 us: local(): below.append(lax.ppermute(below[-1], 'z', up))]
    ppermute x0 -> x19, waiting for transfers between devices: none -> 34.2 us  [the longest x7 14.7 us: local(): above.append(lax.ppermute(above[-1], 'z', down))]
    dot_general x2 -> x0, matrix products: 23.4 us -> none  [the longest x1 14.9 us: both_children(): jnp.dot(basis - left, rows_piece, precision=lax.Precision.HIGHEST, prefer...]
    all_to_all x0 -> x1, blocking collectives: none -> 13.1 us  [local(): got = lax.all_to_all(total, ('y', 'x'), 0, 0, tiled=True)]
    unnamed x5 -> x40, local copies, waits for them, and re-layouts: 0.84 us -> 9.16 us
  transfers between devices with their start and end apart: 2 -> 19, of which waited for: 2 -> 12; matrix products, arithmetic and copies ran while one was open for 0% -> 0% of each run, Pallas kernels for 0% -> 43%
where the time goes in v1:
time: 244 us; the launch traced here: 242 us
  Pallas kernels  107 us (44%)
  starting transfers between devices  77.2 us (32%)
  waiting for transfers between devices  34.2 us (14%)
  blocking collectives  13.1 us (5%)
  local copies, waits for them, and re-layouts  9.85 us (4%)
    pallas_call x1, Pallas kernels, pack(): pl.pallas_call(functools.partial(pack_kernel, chunk), out_shape=[jax.Shap...  96.7 us
    ppermute x7, starting transfers between devices, local(): below.append(lax.ppermute(below[-1], 'z', up))  34.4 us
    ppermute x5, starting transfers between devices, shift(): return lax.ppermute(a, axis, [(i, (i + by) % size) for i in range(size)])  33.8 us
    ppermute x7, waiting for transfers between devices, local(): above.append(lax.ppermute(above[-1], 'z', down))  14.7 us
    ppermute x7, waiting for transfers between devices, local(): below.append(lax.ppermute(below[-1], 'z', up))  14.3 us
    all_to_all x1, blocking collectives, local(): got = lax.all_to_all(total, ('y', 'x'), 0, 0, tiled=True)  13.1 us
    pallas_call x8, Pallas kernels, add_chunks(): pl.pallas_call(functools.partial(add_kernel, [off for _, off in pieces],...  10.2 us
    unnamed x40, local copies, waits for them, and re-layouts  9.16 us
  transfers between devices with their start and end apart: 19, of which 12 were waited for; matrix products, arithmetic and copies ran while one was open for 0% of the time, Pallas kernels for 43%

profile of v1, /device:TPU:1, one launch (start us, length us, event | category | flops | bytes accessed | tf_op | source)
XLA Modules:
  0.0 242.4 jit_solution(1668709047107100616)
XLA Ops:
  0.0 4.5 %collective-permute-start = (f32[512,256]{1,0:T(8,128)}, f32[512,256]{1,0:T(8,128)S(1)}, u32[]{:S(2)}, u32[]{:S(2)}) collective-permute-start(f32[512,256]{1,0:T(8,128)} %refs_4_.1), channel_id=1, source_target_pairs={{0,64},{64,128},{128,192},{192,256},{256,320},{320,384},{384,448},... | collective-permute-start | bytes 1572872 | tf_op jit(solution)/shard_map/vectors_along_z/ppermute | solution.py:162
  4.5 1.3 collective-permute-start.1
  5.8 96.7 %pack_slab.1 = (f32[48,4096]{1,0:T(8,128)}, f32[48,4096]{1,0:T(8,128)}, f32[48,4096]{1,0:T(8,128)}, f32[48,4096]{1,0:T(8,128)}) custom-call(f32[48,16384]{1,0:T(8,128)} %slab.1), custom_call_target="tpu_custom_call" | custom-call | tf_op jit(solution)/shard_map/basis_by_y/pack_slab/pallas_call | solution.py:39
  102.6 3.2 %collective-permute-start.4 = (f32[48,4096]{1,0:T(8,128)}, f32[48,4096]{1,0:T(8,128)S(1)}, u32[]{:S(2)}, u32[]{:S(2)}) collective-permute-start(f32[48,4096]{1,0:T(8,128)} %get-tuple-element.35), channel_id=1, source_target_pairs={{0,16},{16,32},{32,48},{48,0},{1,17},{17,33},{33,49},{49,1},{2,18}... | collective-permute-start | bytes 2359304 | tf_op jit(solution)/shard_map/basis_along_y/ppermute | solution.py:136
  105.8 4.2 %collective-permute-start.2 = (f32[512,256]{1,0:T(8,128)S(1)}, f32[512,256]{1,0:T(8,128)S(1)}, u32[]{:S(2)}, u32[]{:S(2)}) collective-permute-start(f32[512,256]{1,0:T(8,128)S(1)} %collective-permute-done.refs_4_), channel_id=1, source_target_pairs={{0,64},{64,128},{128,192},{192,256},{256,320},{320,384},{384,448},... | collective-permute-start | bytes 1572872 | tf_op jit(solution)/shard_map/vectors_along_z/ppermute | solution.py:162
  109.9 1.3 collective-permute-start.3
  112.0 3.3 %collective-permute-start.7 = (f32[48,4096]{1,0:T(8,128)}, f32[48,4096]{1,0:T(8,128)S(1)}, u32[]{:S(2)}, u32[]{:S(2)}) collective-permute-start(f32[48,4096]{1,0:T(8,128)} %get-tuple-element.40), channel_id=1, source_target_pairs={{0,48},{16,0},{32,16},{48,32},{1,49},{17,1},{33,17},{49,33},{2,50}... | collective-permute-start | bytes 2359304 | tf_op jit(solution)/shard_map/basis_along_y/ppermute | solution.py:136
  115.4 3.1 %collective-permute-done.2.refs_4_ = f32[512,256]{1,0:T(8,128)S(1)} collective-permute-done((f32[512,256]{1,0:T(8,128)S(1)}, f32[512,256]{1,0:T(8,128)S(1)}, u32[]{:S(2)}, u32[]{:S(2)}) %collective-permute-start.2) | collective-permute-done | bytes 524320 | tf_op jit(solution)/shard_map/vectors_along_z/ppermute | solution.py:162
  118.5 4.2 %collective-permute-done.3.refs_9_ = f32[512,256]{1,0:T(8,128)S(1)} collective-permute-done((f32[512,256]{1,0:T(8,128)S(1)}, f32[512,256]{1,0:T(8,128)S(1)}, u32[]{:S(2)}, u32[]{:S(2)}) %collective-permute-start.3) | collective-permute-done | bytes 524320 | tf_op jit(solution)/shard_map/vectors_along_z/ppermute | solution.py:163
  122.7 6.3 %collective-permute-start.5 = (f32[512,256]{1,0:T(8,128)S(1)}, f32[512,256]{1,0:T(8,128)S(1)}, u32[]{:S(2)}, u32[]{:S(2)}) collective-permute-start(f32[512,256]{1,0:T(8,128)S(1)} %collective-permute-done.2.refs_4_), channel_id=1, source_target_pairs={{0,64},{64,128},{128,192},{192,256},{256,320},{320,384},{384,448},... | collective-permute-start | bytes 1572872 | tf_op jit(solution)/shard_map/vectors_along_z/ppermute | solution.py:162
  129.8 1.3 collective-permute-start.6
  131.8 4.5 %collective-permute-start.10 = (f32[48,4096]{1,0:T(8,128)}, f32[48,4096]{1,0:T(8,128)S(1)}, u32[]{:S(2)}, u32[]{:S(2)}) collective-permute-start(f32[48,4096]{1,0:T(8,128)} %get-tuple-element.45), channel_id=1, source_target_pairs={{0,32},{16,48},{32,0},{48,16},{1,33},{17,49},{33,1},{49,17},{2,34}... | collective-permute-start | bytes 2359304 | tf_op jit(solution)/shard_map/basis_along_y/ppermute | solution.py:136
  136.4 1.6 collective-permute-done.5.refs_4_
  138.0 5.5 %collective-permute-done.6.refs_9_ = f32[512,256]{1,0:T(8,128)S(1)} collective-permute-done((f32[512,256]{1,0:T(8,128)S(1)}, f32[512,256]{1,0:T(8,128)S(1)}, u32[]{:S(2)}, u32[]{:S(2)}) %collective-permute-start.6) | collective-permute-done | bytes 524320 | tf_op jit(solution)/shard_map/vectors_along_z/ppermute | solution.py:163
  143.5 4.0 %collective-permute-start.8 = (f32[512,256]{1,0:T(8,128)S(1)}, f32[512,256]{1,0:T(8,128)S(1)}, u32[]{:S(2)}, u32[]{:S(2)}) collective-permute-start(f32[512,256]{1,0:T(8,128)S(1)} %collective-permute-done.5.refs_4_), channel_id=1, source_target_pairs={{0,64},{64,128},{128,192},{192,256},{256,320},{320,384},{384,448},... | collective-permute-start | bytes 1572872 | tf_op jit(solution)/shard_map/vectors_along_z/ppermute | solution.py:162
  148.3 1.3 collective-permute-start.9
  150.4 1.6 collective-permute-done.10.refs_2_.refs_7_
  152.0 3.0 %collective-permute-done.8.refs_4_ = f32[512,256]{1,0:T(8,128)S(1)} collective-permute-done((f32[512,256]{1,0:T(8,128)S(1)}, f32[512,256]{1,0:T(8,128)S(1)}, u32[]{:S(2)}, u32[]{:S(2)}) %collective-permute-start.8) | collective-permute-done | bytes 524320 | tf_op jit(solution)/shard_map/vectors_along_z/ppermute | solution.py:162
  155.1 4.6 %collective-permute-done.9.refs_9_ = f32[512,256]{1,0:T(8,128)S(1)} collective-permute-done((f32[512,256]{1,0:T(8,128)S(1)}, f32[512,256]{1,0:T(8,128)S(1)}, u32[]{:S(2)}, u32[]{:S(2)}) %collective-permute-start.9) | collective-permute-done | bytes 524320 | tf_op jit(solution)/shard_map/vectors_along_z/ppermute | solution.py:163
  159.7 5.5 %collective-permute-start.11 = (f32[512,256]{1,0:T(8,128)S(1)}, f32[512,256]{1,0:T(8,128)S(1)}, u32[]{:S(2)}, u32[]{:S(2)}) collective-permute-start(f32[512,256]{1,0:T(8,128)S(1)} %collective-permute-done.8.refs_4_), channel_id=1, source_target_pairs={{0,64},{64,128},{128,192},{192,256},{256,320},{320,384},{384,448},... | collective-permute-start | bytes 1572872 | tf_op jit(solution)/shard_map/vectors_along_z/ppermute | solution.py:162
  168.1 4.1 %collective-permute-done.11.refs_4_ = f32[512,256]{1,0:T(8,128)S(1)} collective-permute-done((f32[512,256]{1,0:T(8,128)S(1)}, f32[512,256]{1,0:T(8,128)S(1)}, u32[]{:S(2)}, u32[]{:S(2)}) %collective-permute-start.11) | collective-permute-done | bytes 524320 | tf_op jit(solution)/shard_map/vectors_along_z/ppermute | solution.py:162
  172.2 4.9 %collective-permute-start.12 = (f32[512,256]{1,0:T(8,128)S(1)}, f32[512,256]{1,0:T(8,128)}, u32[]{:S(2)}, u32[]{:S(2)}) collective-permute-start(f32[512,256]{1,0:T(8,128)S(1)} %collective-permute-done.11.refs_4_), channel_id=1, source_target_pairs={{0,64},{64,128},{128,192},{192,256},{256,320},{320,384},{384,448},... | collective-permute-start | bytes 1572872 | tf_op jit(solution)/shard_map/vectors_along_z/ppermute | solution.py:162
  177.9 1.3 collective-permute-start.15
  180.0 2.5 %collective-permute-done.12.refs_4_ = f32[512,256]{1,0:T(8,128)} collective-permute-done((f32[512,256]{1,0:T(8,128)S(1)}, f32[512,256]{1,0:T(8,128)}, u32[]{:S(2)}, u32[]{:S(2)}) %collective-permute-start.12) | collective-permute-done | bytes 524320 | tf_op jit(solution)/shard_map/vectors_along_z/ppermute | solution.py:162
  182.5 5.0 %collective-permute-start.13 = (f32[512,256]{1,0:T(8,128)}, f32[512,256]{1,0:T(8,128)}, u32[]{:S(2)}, u32[]{:S(2)}) collective-permute-start(f32[512,256]{1,0:T(8,128)} %collective-permute-done.12.refs_4_), channel_id=1, source_target_pairs={{0,64},{64,128},{128,192},{192,256},{256,320},{320,384},{384,448},... | collective-permute-start | bytes 1572872 | tf_op jit(solution)/shard_map/vectors_along_z/ppermute | solution.py:162
  187.9 1.3 collective-permute-start.16
  197.9 2.2 add_chunks.14.refs_10_
  200.1 2.2 add_chunks.15
  202.3 13.1 %all_to_all.5 = f32[16,48,128]{2,1,0:T(8,128)S(1)} all-to-all(f32[16,48,128]{2,1,0:T(8,128)S(1)} %add_chunks.15), channel_id=1, replica_groups=mesh['z'=8,'y'=4,'x'=4,'half'=2,'core'=2] {'y','x'}, dimensions={0} | all-to-all | bytes 786432 | tf_op jit(solution)/shard_map/sum_over_columns/all_to_all | solution.py:171
  215.3 12.1 %collective-permute-start.17 = (f32[48,128]{1,0:T(8,128)S(1)}, f32[48,128]{1,0:T(8,128)S(1)}, u32[]{:S(2)}, u32[]{:S(2)}) collective-permute-start(f32[48,128]{1,0:T(8,128)S(1)} %reduce_sum.9), channel_id=1, source_target_pairs={{0,1},{1,0},{2,3},{3,2},{4,5},{5,4},{6,7},{7,6},{8,9},{9,8},{10,11... | collective-permute-start | bytes 73736 | tf_op jit(solution)/shard_map/sum_over_columns/ppermute | solution.py:136
  228.3 10.6 %collective-permute-start.18 = (f32[48,128]{1,0:T(8,128)S(1)}, f32[48,128]{1,0:T(8,128)S(1)}, u32[]{:S(2)}, u32[]{:S(2)}) collective-permute-start(f32[48,128]{1,0:T(8,128)S(1)} %add.20), channel_id=1, source_target_pairs={{0,2},{2,0},{1,3},{3,1},{4,6},{6,4},{5,7},{7,5},{8,10},{10,8},{9,1... | collective-permute-start | bytes 73736 | tf_op jit(solution)/shard_map/sum_over_columns/ppermute | solution.py:136
  238.9 2.7 %collective-permute-done.18 = f32[48,128]{1,0:T(8,128)S(1)} collective-permute-done((f32[48,128]{1,0:T(8,128)S(1)}, f32[48,128]{1,0:T(8,128)S(1)}, u32[]{:S(2)}, u32[]{:S(2)}) %collective-permute-start.18) | collective-permute-done | bytes 24608 | tf_op jit(solution)/shard_map/sum_over_columns/ppermute | solution.py:136
  (61 shorter events, 18.4 us)
Async XLA Ops:
  0.0 189.9 %copy-start.1 = (f32[512,256]{1,0:T(8,128)S(1)}, f32[512,256]{1,0:T(8,128)}, u32[]{:S(2)}) copy-start(f32[512,256]{1,0:T(8,128)} %refs_4_.1) | copy-start | bytes 1572868
  0.0 102.5 %collective-permute-start = (f32[512,256]{1,0:T(8,128)}, f32[512,256]{1,0:T(8,128)S(1)}, u32[]{:S(2)}, u32[]{:S(2)}) collective-permute-start(f32[512,256]{1,0:T(8,128)} %refs_4_.1), channel_id=1, source_target_pairs={{0,64},{64,128},{128,192},{192,256},{256,320},{320,384},{384,448},... | collective-permute-start | bytes 1572872 | tf_op jit(solution)/shard_map/vectors_along_z/ppermute | solution.py:162
  4.5 98.0 %collective-permute-start.1 = (f32[512,256]{1,0:T(8,128)}, f32[512,256]{1,0:T(8,128)S(1)}, u32[]{:S(2)}, u32[]{:S(2)}) collective-permute-start(f32[512,256]{1,0:T(8,128)} %refs_4_.1), channel_id=1, source_target_pairs={{64,0},{128,64},{192,128},{256,192},{320,256},{384,320},{448,384},... | collective-permute-start | bytes 1572872 | tf_op jit(solution)/shard_map/vectors_along_z/ppermute | solution.py:163
  102.6 20.1 %collective-permute-start.4 = (f32[48,4096]{1,0:T(8,128)}, f32[48,4096]{1,0:T(8,128)S(1)}, u32[]{:S(2)}, u32[]{:S(2)}) collective-permute-start(f32[48,4096]{1,0:T(8,128)} %get-tuple-element.35), channel_id=1, source_target_pairs={{0,16},{16,32},{32,48},{48,0},{1,17},{17,33},{33,49},{49,1},{2,18}... | collective-permute-start | bytes 2359304 | tf_op jit(solution)/shard_map/basis_along_y/ppermute | solution.py:136
  105.8 12.7 %collective-permute-start.2 = (f32[512,256]{1,0:T(8,128)S(1)}, f32[512,256]{1,0:T(8,128)S(1)}, u32[]{:S(2)}, u32[]{:S(2)}) collective-permute-start(f32[512,256]{1,0:T(8,128)S(1)} %collective-permute-done.refs_4_), channel_id=1, source_target_pairs={{0,64},{64,128},{128,192},{192,256},{256,320},{320,384},{384,448},... | collective-permute-start | bytes 1572872 | tf_op jit(solution)/shard_map/vectors_along_z/ppermute | solution.py:162
  109.9 12.7 %collective-permute-start.3 = (f32[512,256]{1,0:T(8,128)S(1)}, f32[512,256]{1,0:T(8,128)S(1)}, u32[]{:S(2)}, u32[]{:S(2)}) collective-permute-start(f32[512,256]{1,0:T(8,128)S(1)} %collective-permute-done.1.refs_9_), channel_id=1, source_target_pairs={{64,0},{128,64},{192,128},{256,192},{320,256},{384,320},{448,384},... | collective-permute-start | bytes 1572872 | tf_op jit(solution)/shard_map/vectors_along_z/ppermute | solution.py:163
  112.0 24.3 %collective-permute-start.7 = (f32[48,4096]{1,0:T(8,128)}, f32[48,4096]{1,0:T(8,128)S(1)}, u32[]{:S(2)}, u32[]{:S(2)}) collective-permute-start(f32[48,4096]{1,0:T(8,128)} %get-tuple-element.40), channel_id=1, source_target_pairs={{0,48},{16,0},{32,16},{48,32},{1,49},{17,1},{33,17},{49,33},{2,50}... | collective-permute-start | bytes 2359304 | tf_op jit(solution)/shard_map/basis_along_y/ppermute | solution.py:136
  122.7 15.3 %collective-permute-start.5 = (f32[512,256]{1,0:T(8,128)S(1)}, f32[512,256]{1,0:T(8,128)S(1)}, u32[]{:S(2)}, u32[]{:S(2)}) collective-permute-start(f32[512,256]{1,0:T(8,128)S(1)} %collective-permute-done.2.refs_4_), channel_id=1, source_target_pairs={{0,64},{64,128},{128,192},{192,256},{256,320},{320,384},{384,448},... | collective-permute-start | bytes 1572872 | tf_op jit(solution)/shard_map/vectors_along_z/ppermute | solution.py:162
  129.8 13.8 %collective-permute-start.6 = (f32[512,256]{1,0:T(8,128)S(1)}, f32[512,256]{1,0:T(8,128)S(1)}, u32[]{:S(2)}, u32[]{:S(2)}) collective-permute-start(f32[512,256]{1,0:T(8,128)S(1)} %collective-permute-done.3.refs_9_), channel_id=1, source_target_pairs={{64,0},{128,64},{192,128},{256,192},{320,256},{384,320},{448,384},... | collective-permute-start | bytes 1572872 | tf_op jit(solution)/shard_map/vectors_along_z/ppermute | solution.py:163
  131.8 20.2 %collective-permute-start.10 = (f32[48,4096]{1,0:T(8,128)}, f32[48,4096]{1,0:T(8,128)S(1)}, u32[]{:S(2)}, u32[]{:S(2)}) collective-permute-start(f32[48,4096]{1,0:T(8,128)} %get-tuple-element.45), channel_id=1, source_target_pairs={{0,32},{16,48},{32,0},{48,16},{1,33},{17,49},{33,1},{49,17},{2,34}... | collective-permute-start | bytes 2359304 | tf_op jit(solution)/shard_map/basis_along_y/ppermute | solution.py:136
  143.5 11.6 %collective-permute-start.8 = (f32[512,256]{1,0:T(8,128)S(1)}, f32[512,256]{1,0:T(8,128)S(1)}, u32[]{:S(2)}, u32[]{:S(2)}) collective-permute-start(f32[512,256]{1,0:T(8,128)S(1)} %collective-permute-done.5.refs_4_), channel_id=1, source_target_pairs={{0,64},{64,128},{128,192},{192,256},{256,320},{320,384},{384,448},... | collective-permute-start | bytes 1572872 | tf_op jit(solution)/shard_map/vectors_along_z/ppermute | solution.py:162
  148.3 11.4 %collective-permute-start.9 = (f32[512,256]{1,0:T(8,128)S(1)}, f32[512,256]{1,0:T(8,128)S(1)}, u32[]{:S(2)}, u32[]{:S(2)}) collective-permute-start(f32[512,256]{1,0:T(8,128)S(1)} %collective-permute-done.6.refs_9_), channel_id=1, source_target_pairs={{64,0},{128,64},{192,128},{256,192},{320,256},{384,320},{448,384},... | collective-permute-start | bytes 1572872 | tf_op jit(solution)/shard_map/vectors_along_z/ppermute | solution.py:163
  159.7 12.4 %collective-permute-start.11 = (f32[512,256]{1,0:T(8,128)S(1)}, f32[512,256]{1,0:T(8,128)S(1)}, u32[]{:S(2)}, u32[]{:S(2)}) collective-permute-start(f32[512,256]{1,0:T(8,128)S(1)} %collective-permute-done.8.refs_4_), channel_id=1, source_target_pairs={{0,64},{64,128},{128,192},{192,256},{256,320},{320,384},{384,448},... | collective-permute-start | bytes 1572872 | tf_op jit(solution)/shard_map/vectors_along_z/ppermute | solution.py:162
  165.2 0.8 copy-start.12
  166.0 11.9 %collective-permute-start.14 = (f32[512,256]{1,0:T(8,128)S(1)}, f32[512,256]{1,0:T(8,128)S(1)}, u32[]{:S(2)}, u32[]{:S(2)}) collective-permute-start(f32[512,256]{1,0:T(8,128)S(1)} %collective-permute-done.9.refs_9_), channel_id=1, source_target_pairs={{64,0},{128,64},{192,128},{256,192},{320,256},{384,320},{448,384},... | collective-permute-start | bytes 1572872 | tf_op jit(solution)/shard_map/vectors_along_z/ppermute | solution.py:163
  172.2 10.4 %collective-permute-start.12 = (f32[512,256]{1,0:T(8,128)S(1)}, f32[512,256]{1,0:T(8,128)}, u32[]{:S(2)}, u32[]{:S(2)}) collective-permute-start(f32[512,256]{1,0:T(8,128)S(1)} %collective-permute-done.11.refs_4_), channel_id=1, source_target_pairs={{0,64},{64,128},{128,192},{192,256},{256,320},{320,384},{384,448},... | collective-permute-start | bytes 1572872 | tf_op jit(solution)/shard_map/vectors_along_z/ppermute | solution.py:162
  177.9 10.0 %collective-permute-start.15 = (f32[512,256]{1,0:T(8,128)S(1)}, f32[512,256]{1,0:T(8,128)}, u32[]{:S(2)}, u32[]{:S(2)}) collective-permute-start(f32[512,256]{1,0:T(8,128)S(1)} %collective-permute-done.14.refs_9_), channel_id=1, source_target_pairs={{64,0},{128,64},{192,128},{256,192},{320,256},{384,320},{448,384},... | collective-permute-start | bytes 1572872 | tf_op jit(solution)/shard_map/vectors_along_z/ppermute | solution.py:163
  179.2 0.8 copy-start.18
  182.5 17.6 %collective-permute-start.13 = (f32[512,256]{1,0:T(8,128)}, f32[512,256]{1,0:T(8,128)}, u32[]{:S(2)}, u32[]{:S(2)}) collective-permute-start(f32[512,256]{1,0:T(8,128)} %collective-permute-done.12.refs_4_), channel_id=1, source_target_pairs={{0,64},{64,128},{128,192},{192,256},{256,320},{320,384},{384,448},... | collective-permute-start | bytes 1572872 | tf_op jit(solution)/shard_map/vectors_along_z/ppermute | solution.py:162
  187.9 12.2 %collective-permute-start.16 = (f32[512,256]{1,0:T(8,128)}, f32[512,256]{1,0:T(8,128)}, u32[]{:S(2)}, u32[]{:S(2)}) collective-permute-start(f32[512,256]{1,0:T(8,128)} %collective-permute-done.15.refs_9_), channel_id=1, source_target_pairs={{64,0},{128,64},{192,128},{256,192},{320,256},{384,320},{448,384},... | collective-permute-start | bytes 1572872 | tf_op jit(solution)/shard_map/vectors_along_z/ppermute | solution.py:163
  189.9 1.1 copy-start
  191.1 1.0 copy-start.3
  192.1 1.0 copy-start.5
  192.1 1.2 copy-start.7
  193.3 1.0 copy-start.9
  193.3 1.2 copy-start.11
  194.5 1.0 copy-start.13
  194.5 1.2 copy-start.15
  195.7 1.0 copy-start.17
  195.7 1.2 copy-start.19
  215.3 12.9 %collective-permute-start.17 = (f32[48,128]{1,0:T(8,128)S(1)}, f32[48,128]{1,0:T(8,128)S(1)}, u32[]{:S(2)}, u32[]{:S(2)}) collective-permute-start(f32[48,128]{1,0:T(8,128)S(1)} %reduce_sum.9), channel_id=1, source_target_pairs={{0,1},{1,0},{2,3},{3,2},{4,5},{5,4},{6,7},{7,6},{8,9},{9,8},{10,11... | collective-permute-start | bytes 73736 | tf_op jit(solution)/shard_map/sum_over_columns/ppermute | solution.py:136
  228.3 13.3 %collective-permute-start.18 = (f32[48,128]{1,0:T(8,128)S(1)}, f32[48,128]{1,0:T(8,128)S(1)}, u32[]{:S(2)}, u32[]{:S(2)}) collective-permute-start(f32[48,128]{1,0:T(8,128)S(1)} %add.20), channel_id=1, source_target_pairs={{0,2},{2,0},{1,3},{3,1},{4,6},{6,4},{5,7},{7,5},{8,10},{10,8},{9,1... | collective-permute-start | bytes 73736 | tf_op jit(solution)/shard_map/sum_over_columns/ppermute | solution.py:136
  (7 other events, 5.6 us)

commit v2 on v1

--- a/solution.py
+++ b/solution.py
@@ -13,25 +13,13 @@
 F32, BF16 = jnp.float32, jnp.bfloat16
 
 
-def pack_kernel(chunk, slab, *refs):
-    outs, sems = refs[:Y], refs[Y]
+def pack_kernel(chunk, slab, *outs):
     y = lax.axis_index("y")
-    copies = []
     for k in range(Y):
         to = lax.rem(y + k, Y)
         for z in range(Z):
             start = pl.multiple_of((z * Y + to) * chunk, chunk)
-            copies.append(
-                pltpu.make_async_copy(
-                    slab.at[:, pl.ds(start, chunk)],
-                    outs[k].at[:, pl.ds(z * chunk, chunk)],
-                    sems.at[k, z],
-                )
-            )
-    for copy in copies:
-        copy.start()
-    for copy in copies:
-        copy.wait()
+            outs[k][:, z * chunk : (z + 1) * chunk] = slab[:, pl.ds(start, chunk)]
 
 
 def pack(slab, chunk):
@@ -39,9 +27,9 @@
     return pl.pallas_call(
         functools.partial(pack_kernel, chunk),
         out_shape=[jax.ShapeDtypeStruct((rows, Z * chunk), F32)] * Y,
-        in_specs=[pl.BlockSpec(memory_space=pl.ANY)],
-        out_specs=[pl.BlockSpec(memory_space=pl.ANY)] * Y,
-        scratch_shapes=[pltpu.SemaphoreType.DMA((Y, Z))],
+        in_specs=[pl.BlockSpec(memory_space=pltpu.VMEM)],
+        out_specs=[pl.BlockSpec(memory_space=pltpu.VMEM)] * Y,
+        compiler_params=pltpu.CompilerParams(vmem_limit_bytes=14 << 20),
         name="pack_slab",
     )(slab)
 
@@ -89,12 +77,17 @@
             total[1] += product(right, vec[...])
 
     if last:
-        rows, wide = out.shape[1:]
+        rows, wide = total.shape[1] // Y, out.shape[2]
+        low = lax.broadcasted_iota(jnp.int32, out.shape[1:], 1) % (wide // 2) < wide // 4
         for k in range(Y):
             to = lax.rem(y + Y - k, Y)
             for x in range(X):
-                part = total[x // 2, k * rows : (k + 1) * rows, (x % 2) * wide : (x % 2 + 1) * wide]
-                out[to * X + x] = part
+                cols = slice((x % 2) * wide, (x % 2 + 1) * wide)
+                top = total[x // 2, k * rows : k * rows + rows // 2, cols]
+                bottom = total[x // 2, k * rows + rows // 2 : (k + 1) * rows, cols]
+                at = (to * X + x) * 2
+                out[at] = jnp.where(low, top, pltpu.roll(bottom, wide // 4, 1))
+                out[at + 1] = jnp.where(low, pltpu.roll(top, wide - wide // 4, 1), bottom)
 
 
 def add_chunks(info, basis, pieces, total, last=False):
@@ -113,7 +106,7 @@
     if total is not None:
         specs.append(whole)
         args.append(total)
-    out = (Y * X, rows, cols // 2) if last else shape
+    out = (Y * X * 2, rows // 2, cols // 2) if last else shape
     flops = len(pieces) * 6 * Y * rows * chunk * cols
     return pl.pallas_call(
         functools.partial(add_kernel, [off for _, off in pieces], total is None, last),
@@ -126,7 +119,7 @@
             scratch_shapes=[pltpu.VMEM(shape, F32)] if last else [],
         ),
         input_output_aliases={} if total is None or last else {len(args): 0},
-        compiler_params=pltpu.CompilerParams(vmem_limit_bytes=32 << 20),
+        compiler_params=pltpu.CompilerParams(vmem_limit_bytes=12 << 20),
         cost_estimate=pl.CostEstimate(flops=flops, bytes_accessed=4 << 20, transcendentals=0),
         name="add_chunks",
     )(info, *args)
@@ -157,7 +150,7 @@
             with jax.named_scope("basis_along_y"):
                 basis[k] = shift(packed[k], "y", Y, k)
         if ready:
-            below[-1], above[-1], basis = lax.optimization_barrier((below[-1], above[-1], basis))
+            above[-1], basis = lax.optimization_barrier((above[-1], basis))
         with jax.named_scope("vectors_along_z"):
             below.append(lax.ppermute(below[-1], "z", up))
             above.append(lax.ppermute(above[-1], "z", down))
@@ -168,12 +161,12 @@
         total = add_chunks(info, basis, pieces, total, step == Z - 1)
 
     with jax.named_scope("sum_over_columns"):
-        got = lax.all_to_all(total, ("y", "x"), 0, 0, tiled=True)
+        got = lax.all_to_all(total, ("y", "x", "core"), 0, 0, tiled=True)
         mine = jnp.sum(got, axis=0)
-        mine = mine + shift(mine, "core", 2, 1)
         mine = mine + shift(mine, "half", 2, 1)
         wide = mine.shape[1] // 4
-        return lax.dynamic_slice(mine, (0, (at["half"] * 2 + at["core"]) * wide), (rows, wide))
+        mine = lax.dynamic_slice(mine, (0, at["half"] * 2 * wide), (rows // 2, 2 * wide))
+        return jnp.concatenate([mine[:, :wide], mine[:, wide:]], axis=0)
 
 
 def solution(mesh):

time: 244 us -> 160 us (0.66)
  the two profiles are of different devices: /device:TPU:1 before, /device:TPU:128 now
where the time goes in v2:
time: 160 us; the launch traced here: 159 us
  starting transfers between devices  71.4 us (45%)
  waiting for transfers between devices  32.8 us (20%)
  blocking collectives  31.3 us (20%)
  local copies, waits for them, and re-layouts  12 us (8%)
  Pallas kernels  10.6 us (7%)
    ppermute x7, starting transfers between devices, local(): above.append(lax.ppermute(above[-1], 'z', down))  31.9 us
    all_to_all x1, blocking collectives, local(): got = lax.all_to_all(total, ('y', 'x', 'core'), 0, 0, tiled=True)  31.3 us
    ppermute x7, waiting for transfers between devices, local(): below.append(lax.ppermute(below[-1], 'z', up))  25.2 us
    ppermute x4, starting transfers between devices, shift(): return lax.ppermute(a, axis, [(i, (i + by) % size) for i in range(size)])  21.6 us
    ppermute x7, starting transfers between devices, local(): below.append(lax.ppermute(below[-1], 'z', up))  17.9 us
    unnamed x44, local copies, waits for them, and re-layouts  11.3 us
    pallas_call x8, Pallas kernels, add_chunks(): pl.pallas_call(functools.partial(add_kernel, [off for _, off in pieces],...  10.4 us
    ppermute x4, waiting for transfers between devices, shift(): return lax.ppermute(a, axis, [(i, (i + by) % size) for i in range(size)])  4.55 us
  transfers between devices with their start and end apart: 18, of which 9 were waited for; matrix products, arithmetic and copies ran while one was open for 0% of the time, Pallas kernels for 5%

profile of v2, /device:TPU:128, one launch (start us, length us, event | category | flops | bytes accessed | tf_op | source)
XLA Modules:
  0.0 159.4 jit_solution(5646102071837660706)
XLA Ops:
  0.0 3.8 %collective-permute-start = (f32[512,256]{1,0:T(8,128)}, f32[512,256]{1,0:T(8,128)S(1)}, u32[]{:S(2)}, u32[]{:S(2)}) collective-permute-start(f32[512,256]{1,0:T(8,128)} %refs_4_.1), channel_id=1, source_target_pairs={{0,64},{64,128},{128,192},{192,256},{256,320},{320,384},{384,448},... | collective-permute-start | bytes 1572872 | tf_op jit(solution)/shard_map/vectors_along_z/ppermute | solution.py:155
  3.8 3.2 %collective-permute-start.1 = (f32[512,256]{1,0:T(8,128)}, f32[512,256]{1,0:T(8,128)S(1)}, u32[]{:S(2)}, u32[]{:S(2)}) collective-permute-start(f32[512,256]{1,0:T(8,128)} %refs_4_.1), channel_id=1, source_target_pairs={{64,0},{128,64},{192,128},{256,192},{320,256},{384,320},{448,384},... | collective-permute-start | bytes 1572872 | tf_op jit(solution)/shard_map/vectors_along_z/ppermute | solution.py:156
  7.1 1.9 %copy-done = f32[48,16384]{1,0:T(8,128)S(1)} copy-done((f32[48,16384]{1,0:T(8,128)S(1)}, f32[48,16384]{1,0:T(8,128)}, u32[]{:S(2)}) %copy-start) | copy-done | bytes 3145752
  9.2 7.8 %collective-permute-done.refs_4_ = f32[512,256]{1,0:T(8,128)S(1)} collective-permute-done((f32[512,256]{1,0:T(8,128)}, f32[512,256]{1,0:T(8,128)S(1)}, u32[]{:S(2)}, u32[]{:S(2)}) %collective-permute-start) | collective-permute-done | bytes 524320 | tf_op jit(solution)/shard_map/vectors_along_z/ppermute | solution.py:155
  17.0 2.5 %collective-permute-done.1.refs_9_ = f32[512,256]{1,0:T(8,128)S(1)} collective-permute-done((f32[512,256]{1,0:T(8,128)}, f32[512,256]{1,0:T(8,128)S(1)}, u32[]{:S(2)}, u32[]{:S(2)}) %collective-permute-start.1) | collective-permute-done | bytes 524320 | tf_op jit(solution)/shard_map/vectors_along_z/ppermute | solution.py:156
  19.5 3.5 %collective-permute-start.3 = (f32[48,4096]{1,0:T(8,128)S(1)}, f32[48,4096]{1,0:T(8,128)S(1)}, u32[]{:S(2)}, u32[]{:S(2)}) collective-permute-start(f32[48,4096]{1,0:T(8,128)S(1)} %get-tuple-element.31), channel_id=1, source_target_pairs={{0,16},{16,32},{32,48},{48,0},{1,17},{17,33},{33,49},{49,1},{2,18}... | collective-permute-start | bytes 2359304 | tf_op jit(solution)/shard_map/basis_along_y/ppermute | solution.py:129
  23.0 3.8 %collective-permute-start.8 = (f32[512,256]{1,0:T(8,128)S(1)}, f32[512,256]{1,0:T(8,128)S(1)}, u32[]{:S(2)}, u32[]{:S(2)}) collective-permute-start(f32[512,256]{1,0:T(8,128)S(1)} %collective-permute-done.refs_4_), channel_id=1, source_target_pairs={{0,64},{64,128},{128,192},{192,256},{256,320},{320,384},{384,448},... | collective-permute-start | bytes 1572872 | tf_op jit(solution)/shard_map/vectors_along_z/ppermute | solution.py:155
  27.6 3.2 %collective-permute-start.2 = (f32[512,256]{1,0:T(8,128)S(1)}, f32[512,256]{1,0:T(8,128)S(1)}, u32[]{:S(2)}, u32[]{:S(2)}) collective-permute-start(f32[512,256]{1,0:T(8,128)S(1)} %collective-permute-done.1.refs_9_), channel_id=1, source_target_pairs={{64,0},{128,64},{192,128},{256,192},{320,256},{384,320},{448,384},... | collective-permute-start | bytes 1572872 | tf_op jit(solution)/shard_map/vectors_along_z/ppermute | solution.py:156
  31.6 3.6 %collective-permute-start.5 = (f32[48,4096]{1,0:T(8,128)S(1)}, f32[48,4096]{1,0:T(8,128)S(1)}, u32[]{:S(2)}, u32[]{:S(2)}) collective-permute-start(f32[48,4096]{1,0:T(8,128)S(1)} %get-tuple-element.35), channel_id=1, source_target_pairs={{0,48},{16,0},{32,16},{48,32},{1,49},{17,1},{33,17},{49,33},{2,50}... | collective-permute-start | bytes 2359304 | tf_op jit(solution)/shard_map/basis_along_y/ppermute | solution.py:129
  35.2 3.3 %collective-permute-done.8.refs_4_ = f32[512,256]{1,0:T(8,128)S(1)} collective-permute-done((f32[512,256]{1,0:T(8,128)S(1)}, f32[512,256]{1,0:T(8,128)S(1)}, u32[]{:S(2)}, u32[]{:S(2)}) %collective-permute-start.8) | collective-permute-done | bytes 524320 | tf_op jit(solution)/shard_map/vectors_along_z/ppermute | solution.py:155
  38.5 2.6 %collective-permute-start.9 = (f32[512,256]{1,0:T(8,128)S(1)}, f32[512,256]{1,0:T(8,128)S(1)}, u32[]{:S(2)}, u32[]{:S(2)}) collective-permute-start(f32[512,256]{1,0:T(8,128)S(1)} %collective-permute-done.8.refs_4_), channel_id=1, source_target_pairs={{0,64},{64,128},{128,192},{192,256},{256,320},{320,384},{384,448},... | collective-permute-start | bytes 1572872 | tf_op jit(solution)/shard_map/vectors_along_z/ppermute | solution.py:155
  41.9 4.4 %collective-permute-start.4 = (f32[512,256]{1,0:T(8,128)S(1)}, f32[512,256]{1,0:T(8,128)S(1)}, u32[]{:S(2)}, u32[]{:S(2)}) collective-permute-start(f32[512,256]{1,0:T(8,128)S(1)} %collective-permute-done.2.refs_9_), channel_id=1, source_target_pairs={{64,0},{128,64},{192,128},{256,192},{320,256},{384,320},{448,384},... | collective-permute-start | bytes 1572872 | tf_op jit(solution)/shard_map/vectors_along_z/ppermute | solution.py:156
  47.2 4.8 %collective-permute-start.7 = (f32[48,4096]{1,0:T(8,128)S(1)}, f32[48,4096]{1,0:T(8,128)S(1)}, u32[]{:S(2)}, u32[]{:S(2)}) collective-permute-start(f32[48,4096]{1,0:T(8,128)S(1)} %get-tuple-element.39), channel_id=1, source_target_pairs={{0,32},{16,48},{32,0},{48,16},{1,33},{17,49},{33,1},{49,17},{2,34}... | collective-permute-start | bytes 2359304 | tf_op jit(solution)/shard_map/basis_along_y/ppermute | solution.py:129
  53.1 1.9 %collective-permute-start.10 = (f32[512,256]{1,0:T(8,128)S(1)}, f32[512,256]{1,0:T(8,128)S(1)}, u32[]{:S(2)}, u32[]{:S(2)}) collective-permute-start(f32[512,256]{1,0:T(8,128)S(1)} %collective-permute-done.9.refs_4_), channel_id=1, source_target_pairs={{0,64},{64,128},{128,192},{192,256},{256,320},{320,384},{384,448},... | collective-permute-start | bytes 1572872 | tf_op jit(solution)/shard_map/vectors_along_z/ppermute | solution.py:155
  55.8 5.1 %collective-permute-start.6 = (f32[512,256]{1,0:T(8,128)S(1)}, f32[512,256]{1,0:T(8,128)S(1)}, u32[]{:S(2)}, u32[]{:S(2)}) collective-permute-start(f32[512,256]{1,0:T(8,128)S(1)} %collective-permute-done.4.refs_9_), channel_id=1, source_target_pairs={{64,0},{128,64},{192,128},{256,192},{320,256},{384,320},{448,384},... | collective-permute-start | bytes 1572872 | tf_op jit(solution)/shard_map/vectors_along_z/ppermute | solution.py:156
  61.7 5.0 %collective-permute-done.10.refs_4_ = f32[512,256]{1,0:T(8,128)S(1)} collective-permute-done((f32[512,256]{1,0:T(8,128)S(1)}, f32[512,256]{1,0:T(8,128)S(1)}, u32[]{:S(2)}, u32[]{:S(2)}) %collective-permute-start.10) | collective-permute-done | bytes 524320 | tf_op jit(solution)/shard_map/vectors_along_z/ppermute | solution.py:155
  66.7 1.9 %collective-permute-start.11 = (f32[512,256]{1,0:T(8,128)S(1)}, f32[512,256]{1,0:T(8,128)S(1)}, u32[]{:S(2)}, u32[]{:S(2)}) collective-permute-start(f32[512,256]{1,0:T(8,128)S(1)} %collective-permute-done.10.refs_4_), channel_id=1, source_target_pairs={{0,64},{64,128},{128,192},{192,256},{256,320},{320,384},{384,448},... | collective-permute-start | bytes 1572872 | tf_op jit(solution)/shard_map/vectors_along_z/ppermute | solution.py:155
  69.4 5.1 %collective-permute-start.14 = (f32[512,256]{1,0:T(8,128)S(1)}, f32[512,256]{1,0:T(8,128)S(1)}, u32[]{:S(2)}, u32[]{:S(2)}) collective-permute-start(f32[512,256]{1,0:T(8,128)S(1)} %collective-permute-done.6.refs_9_), channel_id=1, source_target_pairs={{64,0},{128,64},{192,128},{256,192},{320,256},{384,320},{448,384},... | collective-permute-start | bytes 1572872 | tf_op jit(solution)/shard_map/vectors_along_z/ppermute | solution.py:156
  75.4 4.1 %collective-permute-done.11.refs_4_ = f32[512,256]{1,0:T(8,128)S(1)} collective-permute-done((f32[512,256]{1,0:T(8,128)S(1)}, f32[512,256]{1,0:T(8,128)S(1)}, u32[]{:S(2)}, u32[]{:S(2)}) %collective-permute-start.11) | collective-permute-done | bytes 524320 | tf_op jit(solution)/shard_map/vectors_along_z/ppermute | solution.py:155
  79.4 1.9 %collective-permute-start.12 = (f32[512,256]{1,0:T(8,128)S(1)}, f32[512,256]{1,0:T(8,128)}, u32[]{:S(2)}, u32[]{:S(2)}) collective-permute-start(f32[512,256]{1,0:T(8,128)S(1)} %collective-permute-done.11.refs_4_), channel_id=1, source_target_pairs={{0,64},{64,128},{128,192},{192,256},{256,320},{320,384},{384,448},... | collective-permute-start | bytes 1572872 | tf_op jit(solution)/shard_map/vectors_along_z/ppermute | solution.py:155
  82.2 5.1 %collective-permute-start.15 = (f32[512,256]{1,0:T(8,128)S(1)}, f32[512,256]{1,0:T(8,128)}, u32[]{:S(2)}, u32[]{:S(2)}) collective-permute-start(f32[512,256]{1,0:T(8,128)S(1)} %collective-permute-done.14.refs_9_), channel_id=1, source_target_pairs={{64,0},{128,64},{192,128},{256,192},{320,256},{384,320},{448,384},... | collective-permute-start | bytes 1572872 | tf_op jit(solution)/shard_map/vectors_along_z/ppermute | solution.py:156
  88.1 3.9 %collective-permute-done.12.refs_4_ = f32[512,256]{1,0:T(8,128)} collective-permute-done((f32[512,256]{1,0:T(8,128)S(1)}, f32[512,256]{1,0:T(8,128)}, u32[]{:S(2)}, u32[]{:S(2)}) %collective-permute-start.12) | collective-permute-done | bytes 524320 | tf_op jit(solution)/shard_map/vectors_along_z/ppermute | solution.py:155
  92.0 1.9 %collective-permute-start.13 = (f32[512,256]{1,0:T(8,128)}, f32[512,256]{1,0:T(8,128)}, u32[]{:S(2)}, u32[]{:S(2)}) collective-permute-start(f32[512,256]{1,0:T(8,128)} %collective-permute-done.12.refs_4_), channel_id=1, source_target_pairs={{0,64},{64,128},{128,192},{192,256},{256,320},{320,384},{384,448},... | collective-permute-start | bytes 1572872 | tf_op jit(solution)/shard_map/vectors_along_z/ppermute | solution.py:155
  94.4 5.7 %collective-permute-start.16 = (f32[512,256]{1,0:T(8,128)}, f32[512,256]{1,0:T(8,128)}, u32[]{:S(2)}, u32[]{:S(2)}) collective-permute-start(f32[512,256]{1,0:T(8,128)} %collective-permute-done.15.refs_9_), channel_id=1, source_target_pairs={{64,0},{128,64},{192,128},{256,192},{320,256},{384,320},{448,384},... | collective-permute-start | bytes 1572872 | tf_op jit(solution)/shard_map/vectors_along_z/ppermute | solution.py:156
  103.1 1.3 add_chunks.9.refs_10_
  104.5 1.3 add_chunks.10.refs_10_
  105.9 1.3 add_chunks.11.refs_10_
  109.1 1.8 %add_chunks.14.refs_10_ = f32[2,192,256]{2,1,0:T(8,128)S(1)} custom-call(s32[4]{0:T(128)S(1)} %pad_add_fusion.info, f32[48,4096]{1,0:T(8,128)S(1)} %get-tuple-element.41.refs_0_.refs_5_, f32[48,4096]{1,0:T(8,128)S(1)} %collective-permute-done.3.refs_1_.refs_6_, ...), custom_call_target="tpu_custom_call", output_to_operand_aliasing={{}: (11, {})} | custom-call | flops 301989888 | bytes 4194304 | tf_op jit(solution)/shard_map/add_chunks/pallas_call | solution.py:111
  111.0 2.0 %add_chunks.15 = f32[32,24,128]{2,1,0:T(8,128)S(1)} custom-call(s32[4]{0:T(128)S(1)} %pad_add_fusion.info, f32[48,4096]{1,0:T(8,128)S(1)} %get-tuple-element.41.refs_0_.refs_5_, f32[48,4096]{1,0:T(8,128)S(1)} %collective-permute-done.3.refs_1_.refs_6_, f32[48,4096]{1,0:T(8,128)S(1)} %collective-permute-done.7.refs_2_.refs_7_, ...), custom_call_target="tpu_custom_call" | custom-call | flops 301989888 | bytes 4194304 | tf_op jit(solution)/shard_map/add_chunks/pallas_call | solution.py:111
  112.9 31.3 %all_to_all.5 = f32[32,24,128]{2,1,0:T(8,128)S(1)} all-to-all(f32[32,24,128]{2,1,0:T(8,128)S(1)} %add_chunks.15), channel_id=1, replica_groups=mesh['z'=8,'y'=4,'x'=4,'half'=2,'core'=2] {'y','x','core'}, dimensions={0} | all-to-all | bytes 786432 | tf_op jit(solution)/shard_map/sum_over_columns/all_to_all | solution.py:164
  144.2 9.7 %collective-permute-start.17 = (f32[24,128]{1,0:T(8,128)S(1)}, f32[24,128]{1,0:T(8,128)S(1)}, u32[]{:S(2)}, u32[]{:S(2)}) collective-permute-start(f32[24,128]{1,0:T(8,128)S(1)} %reduce_sum.9), channel_id=1, source_target_pairs={{0,2},{2,0},{1,3},{3,1},{4,6},{6,4},{5,7},{7,5},{8,10},{10,8},{9,1... | collective-permute-start | bytes 36872 | tf_op jit(solution)/shard_map/sum_over_columns/ppermute | solution.py:129
  154.0 4.5 %collective-permute-done.17 = f32[24,128]{1,0:T(8,128)S(1)} collective-permute-done((f32[24,128]{1,0:T(8,128)S(1)}, f32[24,128]{1,0:T(8,128)S(1)}, u32[]{:S(2)}, u32[]{:S(2)}) %collective-permute-start.17) | collective-permute-done | bytes 12320 | tf_op jit(solution)/shard_map/sum_over_columns/ppermute | solution.py:129
  (64 shorter events, 14.8 us)
Async XLA Ops:
  0.0 17.0 %collective-permute-start = (f32[512,256]{1,0:T(8,128)}, f32[512,256]{1,0:T(8,128)S(1)}, u32[]{:S(2)}, u32[]{:S(2)}) collective-permute-start(f32[512,256]{1,0:T(8,128)} %refs_4_.1), channel_id=1, source_target_pairs={{0,64},{64,128},{128,192},{192,256},{256,320},{320,384},{384,448},... | collective-permute-start | bytes 1572872 | tf_op jit(solution)/shard_map/vectors_along_z/ppermute | solution.py:155
  3.8 15.7 %collective-permute-start.1 = (f32[512,256]{1,0:T(8,128)}, f32[512,256]{1,0:T(8,128)S(1)}, u32[]{:S(2)}, u32[]{:S(2)}) collective-permute-start(f32[512,256]{1,0:T(8,128)} %refs_4_.1), channel_id=1, source_target_pairs={{64,0},{128,64},{192,128},{256,192},{320,256},{384,320},{448,384},... | collective-permute-start | bytes 1572872 | tf_op jit(solution)/shard_map/vectors_along_z/ppermute | solution.py:156
  7.1 1.9 %copy-start = (f32[48,16384]{1,0:T(8,128)S(1)}, f32[48,16384]{1,0:T(8,128)}, u32[]{:S(2)}) copy-start(f32[48,16384]{1,0:T(8,128)} %slab.1) | copy-start | bytes 9437188
  19.5 22.4 %collective-permute-start.3 = (f32[48,4096]{1,0:T(8,128)S(1)}, f32[48,4096]{1,0:T(8,128)S(1)}, u32[]{:S(2)}, u32[]{:S(2)}) collective-permute-start(f32[48,4096]{1,0:T(8,128)S(1)} %get-tuple-element.31), channel_id=1, source_target_pairs={{0,16},{16,32},{32,48},{48,0},{1,17},{17,33},{33,49},{49,1},{2,18}... | collective-permute-start | bytes 2359304 | tf_op jit(solution)/shard_map/basis_along_y/ppermute | solution.py:129
  23.0 15.5 %collective-permute-start.8 = (f32[512,256]{1,0:T(8,128)S(1)}, f32[512,256]{1,0:T(8,128)S(1)}, u32[]{:S(2)}, u32[]{:S(2)}) collective-permute-start(f32[512,256]{1,0:T(8,128)S(1)} %collective-permute-done.refs_4_), channel_id=1, source_target_pairs={{0,64},{64,128},{128,192},{192,256},{256,320},{320,384},{384,448},... | collective-permute-start | bytes 1572872 | tf_op jit(solution)/shard_map/vectors_along_z/ppermute | solution.py:155
  27.6 14.3 %collective-permute-start.2 = (f32[512,256]{1,0:T(8,128)S(1)}, f32[512,256]{1,0:T(8,128)S(1)}, u32[]{:S(2)}, u32[]{:S(2)}) collective-permute-start(f32[512,256]{1,0:T(8,128)S(1)} %collective-permute-done.1.refs_9_), channel_id=1, source_target_pairs={{64,0},{128,64},{192,128},{256,192},{320,256},{384,320},{448,384},... | collective-permute-start | bytes 1572872 | tf_op jit(solution)/shard_map/vectors_along_z/ppermute | solution.py:156
  30.8 0.8 copy-start.4
  31.6 24.1 %collective-permute-start.5 = (f32[48,4096]{1,0:T(8,128)S(1)}, f32[48,4096]{1,0:T(8,128)S(1)}, u32[]{:S(2)}, u32[]{:S(2)}) collective-permute-start(f32[48,4096]{1,0:T(8,128)S(1)} %get-tuple-element.35), channel_id=1, source_target_pairs={{0,48},{16,0},{32,16},{48,32},{1,49},{17,1},{33,17},{49,33},{2,50}... | collective-permute-start | bytes 2359304 | tf_op jit(solution)/shard_map/basis_along_y/ppermute | solution.py:129
  38.5 14.6 %collective-permute-start.9 = (f32[512,256]{1,0:T(8,128)S(1)}, f32[512,256]{1,0:T(8,128)S(1)}, u32[]{:S(2)}, u32[]{:S(2)}) collective-permute-start(f32[512,256]{1,0:T(8,128)S(1)} %collective-permute-done.8.refs_4_), channel_id=1, source_target_pairs={{0,64},{64,128},{128,192},{192,256},{256,320},{320,384},{384,448},... | collective-permute-start | bytes 1572872 | tf_op jit(solution)/shard_map/vectors_along_z/ppermute | solution.py:155
  41.9 13.9 %collective-permute-start.4 = (f32[512,256]{1,0:T(8,128)S(1)}, f32[512,256]{1,0:T(8,128)S(1)}, u32[]{:S(2)}, u32[]{:S(2)}) collective-permute-start(f32[512,256]{1,0:T(8,128)S(1)} %collective-permute-done.2.refs_9_), channel_id=1, source_target_pairs={{64,0},{128,64},{192,128},{256,192},{320,256},{384,320},{448,384},... | collective-permute-start | bytes 1572872 | tf_op jit(solution)/shard_map/vectors_along_z/ppermute | solution.py:156
  46.3 0.8 copy-start.8
  47.2 22.3 %collective-permute-start.7 = (f32[48,4096]{1,0:T(8,128)S(1)}, f32[48,4096]{1,0:T(8,128)S(1)}, u32[]{:S(2)}, u32[]{:S(2)}) collective-permute-start(f32[48,4096]{1,0:T(8,128)S(1)} %get-tuple-element.39), channel_id=1, source_target_pairs={{0,32},{16,48},{32,0},{48,16},{1,33},{17,49},{33,1},{49,17},{2,34}... | collective-permute-start | bytes 2359304 | tf_op jit(solution)/shard_map/basis_along_y/ppermute | solution.py:129
  53.1 13.7 %collective-permute-start.10 = (f32[512,256]{1,0:T(8,128)S(1)}, f32[512,256]{1,0:T(8,128)S(1)}, u32[]{:S(2)}, u32[]{:S(2)}) collective-permute-start(f32[512,256]{1,0:T(8,128)S(1)} %collective-permute-done.9.refs_4_), channel_id=1, source_target_pairs={{0,64},{64,128},{128,192},{192,256},{256,320},{320,384},{384,448},... | collective-permute-start | bytes 1572872 | tf_op jit(solution)/shard_map/vectors_along_z/ppermute | solution.py:155
  55.8 13.7 %collective-permute-start.6 = (f32[512,256]{1,0:T(8,128)S(1)}, f32[512,256]{1,0:T(8,128)S(1)}, u32[]{:S(2)}, u32[]{:S(2)}) collective-permute-start(f32[512,256]{1,0:T(8,128)S(1)} %collective-permute-done.4.refs_9_), channel_id=1, source_target_pairs={{64,0},{128,64},{192,128},{256,192},{320,256},{384,320},{448,384},... | collective-permute-start | bytes 1572872 | tf_op jit(solution)/shard_map/vectors_along_z/ppermute | solution.py:156
  66.7 12.7 %collective-permute-start.11 = (f32[512,256]{1,0:T(8,128)S(1)}, f32[512,256]{1,0:T(8,128)S(1)}, u32[]{:S(2)}, u32[]{:S(2)}) collective-permute-start(f32[512,256]{1,0:T(8,128)S(1)} %collective-permute-done.10.refs_4_), channel_id=1, source_target_pairs={{0,64},{64,128},{128,192},{192,256},{256,320},{320,384},{384,448},... | collective-permute-start | bytes 1572872 | tf_op jit(solution)/shard_map/vectors_along_z/ppermute | solution.py:155
  69.4 12.7 %collective-permute-start.14 = (f32[512,256]{1,0:T(8,128)S(1)}, f32[512,256]{1,0:T(8,128)S(1)}, u32[]{:S(2)}, u32[]{:S(2)}) collective-permute-start(f32[512,256]{1,0:T(8,128)S(1)} %collective-permute-done.6.refs_9_), channel_id=1, source_target_pairs={{64,0},{128,64},{192,128},{256,192},{320,256},{384,320},{448,384},... | collective-permute-start | bytes 1572872 | tf_op jit(solution)/shard_map/vectors_along_z/ppermute | solution.py:156
  79.4 12.6 %collective-permute-start.12 = (f32[512,256]{1,0:T(8,128)S(1)}, f32[512,256]{1,0:T(8,128)}, u32[]{:S(2)}, u32[]{:S(2)}) collective-permute-start(f32[512,256]{1,0:T(8,128)S(1)} %collective-permute-done.11.refs_4_), channel_id=1, source_target_pairs={{0,64},{64,128},{128,192},{192,256},{256,320},{320,384},{384,448},... | collective-permute-start | bytes 1572872 | tf_op jit(solution)/shard_map/vectors_along_z/ppermute | solution.py:155
  82.2 12.3 %collective-permute-start.15 = (f32[512,256]{1,0:T(8,128)S(1)}, f32[512,256]{1,0:T(8,128)}, u32[]{:S(2)}, u32[]{:S(2)}) collective-permute-start(f32[512,256]{1,0:T(8,128)S(1)} %collective-permute-done.14.refs_9_), channel_id=1, source_target_pairs={{64,0},{128,64},{192,128},{256,192},{320,256},{384,320},{448,384},... | collective-permute-start | bytes 1572872 | tf_op jit(solution)/shard_map/vectors_along_z/ppermute | solution.py:156
  92.0 18.9 %collective-permute-start.13 = (f32[512,256]{1,0:T(8,128)}, f32[512,256]{1,0:T(8,128)}, u32[]{:S(2)}, u32[]{:S(2)}) collective-permute-start(f32[512,256]{1,0:T(8,128)} %collective-permute-done.12.refs_4_), channel_id=1, source_target_pairs={{0,64},{64,128},{128,192},{192,256},{256,320},{320,384},{384,448},... | collective-permute-start | bytes 1572872 | tf_op jit(solution)/shard_map/vectors_along_z/ppermute | solution.py:155
  94.4 16.5 %collective-permute-start.16 = (f32[512,256]{1,0:T(8,128)}, f32[512,256]{1,0:T(8,128)}, u32[]{:S(2)}, u32[]{:S(2)}) collective-permute-start(f32[512,256]{1,0:T(8,128)} %collective-permute-done.15.refs_9_), channel_id=1, source_target_pairs={{64,0},{128,64},{192,128},{256,192},{320,256},{384,320},{448,384},... | collective-permute-start | bytes 1572872 | tf_op jit(solution)/shard_map/vectors_along_z/ppermute | solution.py:156
  100.9 1.0 copy-start.1
  101.9 1.0 copy-start.3
  101.9 1.2 copy-start.5
  103.1 1.3 copy-start.7
  103.1 1.3 copy-start.9
  104.5 1.4 copy-start.11
  104.5 1.4 copy-start.13
  105.9 1.4 copy-start.15
  105.9 1.4 copy-start.17
  107.2 1.0 copy-start.19
  107.3 1.2 copy-start.21
  144.2 14.3 %collective-permute-start.17 = (f32[24,128]{1,0:T(8,128)S(1)}, f32[24,128]{1,0:T(8,128)S(1)}, u32[]{:S(2)}, u32[]{:S(2)}) collective-permute-start(f32[24,128]{1,0:T(8,128)S(1)} %reduce_sum.9), channel_id=1, source_target_pairs={{0,2},{2,0},{1,3},{3,1},{4,6},{6,4},{5,7},{7,5},{8,10},{10,8},{9,1... | collective-permute-start | bytes 36872 | tf_op jit(solution)/shard_map/sum_over_columns/ppermute | solution.py:129
  (8 other events, 6.3 us)

commit v3 on v2

v3 whole, which is shorter than its diff:
```python
import functools

import jax
import jax.numpy as jnp
from jax import lax
from jax.experimental import pallas as pl
from jax.experimental.pallas import tpu as pltpu
from jax.sharding import Mesh, PartitionSpec as P

AXES = ("z", "y", "x", "half", "core")
SIZES = (8, 4, 4, 2, 2)
Z, Y, X = SIZES[:3]
F32, BF16 = jnp.float32, jnp.bfloat16


def pack_kernel(chunk, slab, *outs):
    y = lax.axis_index("y")
    for k in range(Y):
        to = lax.rem(y + k, Y)
        for z in range(Z):
            start = pl.multiple_of((z * Y + to) * chunk, chunk)
            at = z % (Z // 2) * chunk
            outs[2 * k + z // (Z // 2)][:, at : at + chunk] = slab[:, pl.ds(start, chunk)]


def pack(slab, chunk):
    rows = slab.shape[0]
    parts = pl.pallas_call(
        functools.partial(pack_kernel, chunk),
        out_shape=[jax.ShapeDtypeStruct((rows, Z // 2 * chunk), F32)] * (2 * Y),
        in_specs=[pl.BlockSpec(memory_space=pltpu.VMEM)],
        out_specs=[pl.BlockSpec(memory_space=pltpu.VMEM)] * (2 * Y),
        compiler_params=pltpu.CompilerParams(vmem_limit_bytes=14 << 20),
        name="pack_slab",
    )(slab)
    return [list(parts[2 * k : 2 * k + 2]) for k in range(Y)]


def halves(a):
    high = a.astype(BF16)
    return high, (a - high.astype(F32)).astype(BF16)


def product(a, b):
    a_high, a_low = halves(a)
    b_high, b_low = halves(b)
    dot = functools.partial(jnp.dot, preferred_element_type=F32)
    return dot(a_high, b_high) + (dot(a_high, b_low) + dot(a_low, b_high))


def add_product(total, split, start, lhs, vec):
    chunk = vec.shape[0]
    one_side = (start + chunk <= split) | (start >= split)

    @pl.when(one_side)
    def _():
        side = (start >= split).astype(jnp.int32)
        total[side] += product(lhs(), vec[...])

    @pl.when(jnp.logical_not(one_side))
    def _():
        basis = lhs()
        at = start + lax.broadcasted_iota(jnp.int32, basis.shape, 1)
        total[0] += product(jnp.where(at < split, basis, 0.0), vec[...])
        total[1] += product(jnp.where(at < split, 0.0, basis), vec[...])


def add_kernel(offsets, first, last, info, *refs):
    total = refs[-1]
    out = refs[-2] if last else total
    n = 2 * Y + 1
    rest = refs[len(offsets) * n :]
    split, z, y, col, core = (info[i] for i in range(5))
    if first:
        total[...] = jnp.zeros_like(total)
    else:
        total[...] = rest[0][...]
    if last:
        total[core] += rest[1][...]
    for i, off in enumerate(offsets):
        lower, upper, vec = refs[i * n : i * n + Y], refs[i * n + Y : i * n + 2 * Y], refs[i * n + 2 * Y]
        chunk = vec.shape[0]
        at = z + off

        def lhs(at=at, lower=lower, upper=upper):
            return jnp.concatenate([jnp.where(at < Z // 2, a[...], b[...]) for a, b in zip(lower, upper)], axis=0)

        @pl.when((at >= 0) & (at < Z))
        def _(at=at, lhs=lhs, vec=vec, chunk=chunk):
            add_product(total, split, ((col * Z + at) * Y + y) * chunk, lhs, vec)

    if last:
        rows, wide = total.shape[1] // Y, out.shape[2]
        low = lax.broadcasted_iota(jnp.int32, out.shape[1:], 1) % (wide // 2) < wide // 4
        for k in range(Y):
            to = lax.rem(y + Y - k, Y)
            for x in range(X):
                cols = slice((x % 2) * wide, (x % 2 + 1) * wide)
                top = total[x // 2, k * rows : k * rows + rows // 2, cols]
                bottom = total[x // 2, k * rows + rows // 2 : (k + 1) * rows, cols]
                at = (to * X + x) * 2
                out[at] = jnp.where(low, top, pltpu.roll(bottom, wide // 4, 1))
                out[at + 1] = jnp.where(low, pltpu.roll(top, wide - wide // 4, 1), bottom)


def add_chunks(info, basis, pieces, total, extra=None):
    rows, chunk, cols = basis[0][0].shape[0], pieces[0][0].shape[0], pieces[0][0].shape[1]
    last = extra is not None
    specs, args = [], []
    for vec, off in pieces:
        for half in range(2):
            def index(g, s, off=off, half=half):
                return 0, jnp.clip(s[1] + off - half * (Z // 2), 0, Z // 2 - 1)

            specs += [pl.BlockSpec((rows, chunk), index)] * Y
            args += [b[half] for b in basis]
        specs.append(pl.BlockSpec((chunk, cols), lambda g, s: (0, 0)))
        args.append(vec)
    shape = (2, Y * rows, cols)
    for whole in [] if total is None else [total, extra] if last else [total]:
        specs.append(pl.BlockSpec(whole.shape, lambda g, s, n=whole.ndim: (0,) * n))
        args.append(whole)
    out = (Y * X * 2, rows // 2, cols // 2) if last else shape
    flops = len(pieces) * 6 * Y * rows * chunk * cols
    return pl.pallas_call(
        functools.partial(add_kernel, [off for _, off in pieces], total is None, last),
        out_shape=jax.ShapeDtypeStruct(out, F32),
        grid_spec=pltpu.PrefetchScalarGridSpec(
            num_scalar_prefetch=1,
            grid=(1,),
            in_specs=specs,
            out_specs=pl.BlockSpec(out, lambda g, s: (0, 0, 0)),
            scratch_shapes=[pltpu.VMEM(shape, F32)] if last else [],
        ),
        input_output_aliases={} if total is None or last else {len(args): 0},
        compiler_params=pltpu.CompilerParams(vmem_limit_bytes=16 << 20),
        cost_estimate=pl.CostEstimate(flops=flops, bytes_accessed=4 << 20, transcendentals=0),
        name="add_chunks",
    )(info, *args)


def help_kernel(info, basis, below, above, keep, send, total):
    split, z, y, col, core = (info[i] for i in range(5))
    chunk = below.shape[0]
    total[...] = jnp.zeros_like(total)
    for vec, mine, at in ((above, Z // 2 - 1, Z - 1), (below, Z // 2, 0)):

        @pl.when(z == mine)
        def _(vec=vec, at=at):
            add_product(total, split, ((col * Z + at) * Y + y) * chunk, lambda: basis[...], vec)

    keep[...] = total[core]
    send[...] = total[1 - core]


def help_ends(info, basis, below, above):
    shape = (basis.shape[0], below.shape[1])
    vmem = pl.BlockSpec(memory_space=pltpu.VMEM)
    return pl.pallas_call(
        help_kernel,
        out_shape=[jax.ShapeDtypeStruct(shape, F32)] * 2,
        in_specs=[pl.BlockSpec(memory_space=pltpu.SMEM), vmem, vmem, vmem],
        out_specs=[vmem, vmem],
        scratch_shapes=[pltpu.VMEM((2, *shape), F32)],
        compiler_params=pltpu.CompilerParams(vmem_limit_bytes=16 << 20),
        cost_estimate=pl.CostEstimate(flops=6 * shape[0] * below.size, bytes_accessed=3 << 20, transcendentals=0),
        name="help_ends",
    )(info, basis, below, above)


def shift(a, axis, size, by):
    return lax.ppermute(a, axis, [(i, (i + by) % size) for i in range(size)])


def local(split_at, slab, vectors):
    chunk = vectors.shape[0]
    rows = slab.shape[0]
    at = {axis: lax.axis_index(axis) for axis in AXES}
    col = (at["x"] * 2 + at["half"]) * 2 + at["core"]
    info = jnp.stack([split_at[0], at["z"], at["y"], col, at["core"]])
    up = [(i, i + 1) for i in range(Z - 1)]
    down = [(i + 1, i) for i in range(Z - 1)]
    middle = Z // 2 - 1

    with jax.named_scope("basis_by_y"):
        packed = pack(slab, chunk)
    below, above = [vectors], [vectors]
    basis = [list(parts) for parts in packed]
    ended = None
    for step in range(1, Z - 1):
        ready = {2: ((1, 0), (3, 0)), 3: ((1, 1), (3, 1)), 4: ((2, 0),), 5: ((2, 1),)}.get(step, ())
        for k, half in ready:
            with jax.named_scope("basis_along_y"):
                basis[k][half] = shift(packed[k][half], "y", Y, k)
        if ready:
            above[-1], basis = lax.optimization_barrier((above[-1], basis))
        with jax.named_scope("vectors_along_z"):
            below.append(lax.ppermute(below[-1], "z", up))
            above.append(lax.ppermute(above[-1], "z", down))
        if step == 5:
            with jax.named_scope("ends_to_middle"):
                lower = jnp.concatenate([b[0][:, :chunk] for b in basis], axis=0)
                upper = jnp.concatenate([b[1][:, -chunk:] for b in basis], axis=0)
                ends = jnp.where(at["z"] < Z // 2, upper, lower)
                ends = lax.ppermute(ends, "z", [(0, middle), (Z - 1, Z - 1 - middle)])
                keep, send = help_ends(info, ends, below[4], above[4])
                ended = keep + shift(send, "core", 2, 1)
                ended = lax.ppermute(ended, "z", [(middle, 0), (Z - 1 - middle, Z - 1)])

    total = add_chunks(info, basis, [(vectors, 0)], None)
    for step in range(1, Z - 1):
        pieces = [(below[step], -step), (above[step], step)]
        total = add_chunks(info, basis, pieces, total, ended if step == Z - 2 else None)

    with jax.named_scope("sum_over_columns"):
        got = lax.all_to_all(total, ("y", "x", "core"), 0, 0, tiled=True)
        mine = jnp.sum(got, axis=0)
        mine = mine + shift(mine, "half", 2, 1)
        wide = mine.shape[1] // 4
        mine = lax.dynamic_slice(mine, (0, at["half"] * 2 * wide), (rows // 2, 2 * wide))
        return jnp.concatenate([mine[:, :wide], mine[:, wide:]], axis=0)


def solution(mesh):
    split_mesh = Mesh(mesh.devices.reshape(SIZES), AXES)
    placed = (P(), P(("z", "y"), ("x", "half", "core")), P(("x", "half", "core", "z", "y"), None))
    return jax.shard_map(
        local, mesh=split_mesh, in_specs=placed,
        out_specs=P(("z", "y"), ("x", "half", "core")), check_vma=False,
    )
```

time: 160 us -> 168 us (1.050)
  the two profiles are of different devices: /device:TPU:128 before, /device:TPU:1 now
where the time goes in v3:
time: 168 us; the launch traced here: 166 us
  starting transfers between devices  95.4 us (57%)
  waiting for transfers between devices  29.7 us (18%)
  blocking collectives  17.7 us (11%)
  Pallas kernels  12.2 us (7%)
  local copies, waits for them, and re-layouts  8.86 us (5%)
    ppermute x8, starting transfers between devices, shift(): return lax.ppermute(a, axis, [(i, (i + by) % size) for i in range(size)])  47.1 us
    ppermute x6, starting transfers between devices, local(): below.append(lax.ppermute(below[-1], 'z', up))  30.7 us
    ppermute x8, waiting for transfers between devices, shift(): return lax.ppermute(a, axis, [(i, (i + by) % size) for i in range(size)])  26 us
    all_to_all x1, blocking collectives, local(): got = lax.all_to_all(total, ('y', 'x', 'core'), 0, 0, tiled=True)  17.7 us
    pallas_call x7, Pallas kernels, add_chunks(): pl.pallas_call(functools.partial(add_kernel, [off for _, off in pieces],...  10.8 us
    ppermute x1, starting transfers between devices, local(): ends = lax.ppermute(ends, 'z', [(0, middle), (Z - 1, Z - 1 - middle)])  8.58 us
    unnamed x28, local copies, waits for them, and re-layouts  7.95 us
    ppermute x6, starting transfers between devices, local(): above.append(lax.ppermute(above[-1], 'z', down))  7.7 us
  transfers between devices with their start and end apart: 22, of which 10 were waited for; matrix products, arithmetic and copies ran while one was open for 1% of the time, Pallas kernels for 6%

profile of v3, /device:TPU:1, one launch (start us, length us, event | category | flops | bytes accessed | tf_op | source)
XLA Modules:
  0.0 165.9 jit_solution(9989637456353943098)
XLA Ops:
  1.3 5.0 %collective-permute-start.10 = (f32[512,256]{1,0:T(8,128)}, f32[512,256]{1,0:T(8,128)S(1)}, u32[]{:S(2)}, u32[]{:S(2)}) collective-permute-start(f32[512,256]{1,0:T(8,128)} %refs_8_.1), channel_id=1, source_target_pairs={{0,64},{64,128},{128,192},{192,256},{256,320},{320,384},{384,448},... | collective-permute-start | bytes 1572872 | tf_op jit(solution)/shard_map/vectors_along_z/ppermute | solution.py:198
  6.3 1.9 %copy-done = f32[48,16384]{1,0:T(8,128)S(1)} copy-done((f32[48,16384]{1,0:T(8,128)S(1)}, f32[48,16384]{1,0:T(8,128)}, u32[]{:S(2)}) %copy-start) | copy-done | bytes 3145752
  8.4 3.2 %collective-permute-start.1 = (f32[48,2048]{1,0:T(8,128)S(1)}, f32[48,2048]{1,0:T(8,128)S(1)}, u32[]{:S(2)}, u32[]{:S(2)}) collective-permute-start(f32[48,2048]{1,0:T(8,128)S(1)} %get-tuple-element.46), channel_id=1, source_target_pairs={{0,16},{16,32},{32,48},{48,0},{1,17},{17,33},{33,49},{49,1},{2,18}... | collective-permute-start | bytes 1179656 | tf_op jit(solution)/shard_map/basis_along_y/ppermute | solution.py:172
  11.6 3.4 %collective-permute-start.2 = (f32[48,2048]{1,0:T(8,128)S(1)}, f32[48,2048]{1,0:T(8,128)S(1)}, u32[]{:S(2)}, u32[]{:S(2)}) collective-permute-start(f32[48,2048]{1,0:T(8,128)S(1)} %get-tuple-element.50), channel_id=1, source_target_pairs={{0,48},{16,0},{32,16},{48,32},{1,49},{17,1},{33,17},{49,33},{2,50}... | collective-permute-start | bytes 1179656 | tf_op jit(solution)/shard_map/basis_along_y/ppermute | solution.py:172
  15.0 3.2 %collective-permute-done.1.refs_1_.refs_10_ = f32[48,2048]{1,0:T(8,128)S(1)} collective-permute-done((f32[48,2048]{1,0:T(8,128)S(1)}, f32[48,2048]{1,0:T(8,128)S(1)}, u32[]{:S(2)}, u32[]{:S(2)}) %collective-permute-start.1) | collective-permute-done | bytes 393248 | tf_op jit(solution)/shard_map/basis_along_y/ppermute | solution.py:172
  18.2 1.9 %collective-permute-done.2.refs_3_.refs_12_ = f32[48,2048]{1,0:T(8,128)S(1)} collective-permute-done((f32[48,2048]{1,0:T(8,128)S(1)}, f32[48,2048]{1,0:T(8,128)S(1)}, u32[]{:S(2)}, u32[]{:S(2)}) %collective-permute-start.2) | collective-permute-done | bytes 393248 | tf_op jit(solution)/shard_map/basis_along_y/ppermute | solution.py:172
  20.2 1.3 collective-permute-start.3
  22.3 4.9 %collective-permute-start.11 = (f32[512,256]{1,0:T(8,128)S(1)}, f32[512,256]{1,0:T(8,128)S(1)}, u32[]{:S(2)}, u32[]{:S(2)}) collective-permute-start(f32[512,256]{1,0:T(8,128)S(1)} %collective-permute-done.10.refs_8_), channel_id=1, source_target_pairs={{0,64},{64,128},{128,192},{192,256},{256,320},{320,384},{384,448},... | collective-permute-start | bytes 1572872 | tf_op jit(solution)/shard_map/vectors_along_z/ppermute | solution.py:198
  28.0 5.1 %collective-permute-start.4 = (f32[48,2048]{1,0:T(8,128)S(1)}, f32[48,2048]{1,0:T(8,128)S(1)}, u32[]{:S(2)}, u32[]{:S(2)}) collective-permute-start(f32[48,2048]{1,0:T(8,128)S(1)} %get-tuple-element.47), channel_id=1, source_target_pairs={{0,16},{16,32},{32,48},{48,0},{1,17},{17,33},{33,49},{49,1},{2,18}... | collective-permute-start | bytes 1179656 | tf_op jit(solution)/shard_map/basis_along_y/ppermute | solution.py:172
  33.1 1.9 %collective-permute-start.5 = (f32[48,2048]{1,0:T(8,128)S(1)}, f32[48,2048]{1,0:T(8,128)S(1)}, u32[]{:S(2)}, u32[]{:S(2)}) collective-permute-start(f32[48,2048]{1,0:T(8,128)S(1)} %get-tuple-element.51), channel_id=1, source_target_pairs={{0,48},{16,0},{32,16},{48,32},{1,49},{17,1},{33,17},{49,33},{2,50}... | collective-permute-start | bytes 1179656 | tf_op jit(solution)/shard_map/basis_along_y/ppermute | solution.py:172
  35.0 3.2 %collective-permute-done.4.refs_5_.refs_14_ = f32[48,2048]{1,0:T(8,128)S(1)} collective-permute-done((f32[48,2048]{1,0:T(8,128)S(1)}, f32[48,2048]{1,0:T(8,128)S(1)}, u32[]{:S(2)}, u32[]{:S(2)}) %collective-permute-start.4) | collective-permute-done | bytes 393248 | tf_op jit(solution)/shard_map/basis_along_y/ppermute | solution.py:172
  38.3 3.8 %collective-permute-done.5.refs_7_.refs_16_ = f32[48,2048]{1,0:T(8,128)S(1)} collective-permute-done((f32[48,2048]{1,0:T(8,128)S(1)}, f32[48,2048]{1,0:T(8,128)S(1)}, u32[]{:S(2)}, u32[]{:S(2)}) %collective-permute-start.5) | collective-permute-done | bytes 393248 | tf_op jit(solution)/shard_map/basis_along_y/ppermute | solution.py:172
  42.1 1.3 collective-permute-start.6
  44.2 4.8 %collective-permute-start.12 = (f32[512,256]{1,0:T(8,128)S(1)}, f32[512,256]{1,0:T(8,128)S(1)}, u32[]{:S(2)}, u32[]{:S(2)}) collective-permute-start(f32[512,256]{1,0:T(8,128)S(1)} %collective-permute-done.11.refs_8_), channel_id=1, source_target_pairs={{0,64},{64,128},{128,192},{192,256},{256,320},{320,384},{384,448},... | collective-permute-start | bytes 1572872 | tf_op jit(solution)/shard_map/vectors_along_z/ppermute | solution.py:198
  49.7 3.7 %collective-permute-start.7 = (f32[48,2048]{1,0:T(8,128)S(1)}, f32[48,2048]{1,0:T(8,128)S(1)}, u32[]{:S(2)}, u32[]{:S(2)}) collective-permute-start(f32[48,2048]{1,0:T(8,128)S(1)} %get-tuple-element.48), channel_id=1, source_target_pairs={{0,32},{16,48},{32,0},{48,16},{1,33},{17,49},{33,1},{49,17},{2,34}... | collective-permute-start | bytes 1179656 | tf_op jit(solution)/shard_map/basis_along_y/ppermute | solution.py:172
  53.5 6.3 %collective-permute-done.7.refs_2_.refs_11_ = f32[48,2048]{1,0:T(8,128)S(1)} collective-permute-done((f32[48,2048]{1,0:T(8,128)S(1)}, f32[48,2048]{1,0:T(8,128)S(1)}, u32[]{:S(2)}, u32[]{:S(2)}) %collective-permute-start.7) | collective-permute-done | bytes 393248 | tf_op jit(solution)/shard_map/basis_along_y/ppermute | solution.py:172
  59.8 1.3 collective-permute-start.8
  61.8 6.3 %collective-permute-start.13 = (f32[512,256]{1,0:T(8,128)S(1)}, f32[512,256]{1,0:T(8,128)}, u32[]{:S(2)}, u32[]{:S(2)}) collective-permute-start(f32[512,256]{1,0:T(8,128)S(1)} %collective-permute-done.12.refs_8_), channel_id=1, source_target_pairs={{0,64},{64,128},{128,192},{192,256},{256,320},{320,384},{384,448},... | collective-permute-start | bytes 1572872 | tf_op jit(solution)/shard_map/vectors_along_z/ppermute | solution.py:198
  68.9 4.6 %collective-permute-start.9 = (f32[48,2048]{1,0:T(8,128)S(1)}, f32[48,2048]{1,0:T(8,128)S(1)}, u32[]{:S(2)}, u32[]{:S(2)}) collective-permute-start(f32[48,2048]{1,0:T(8,128)S(1)} %get-tuple-element.49), channel_id=1, source_target_pairs={{0,32},{16,48},{32,0},{48,16},{1,33},{17,49},{33,1},{49,17},{2,34}... | collective-permute-start | bytes 1179656 | tf_op jit(solution)/shard_map/basis_along_y/ppermute | solution.py:172
  73.5 5.4 %collective-permute-done.9.refs_6_.refs_15_ = f32[48,2048]{1,0:T(8,128)S(1)} collective-permute-done((f32[48,2048]{1,0:T(8,128)S(1)}, f32[48,2048]{1,0:T(8,128)S(1)}, u32[]{:S(2)}, u32[]{:S(2)}) %collective-permute-start.9) | collective-permute-done | bytes 393248 | tf_op jit(solution)/shard_map/basis_along_y/ppermute | solution.py:172
  80.2 4.9 %collective-permute-start.14 = (f32[512,256]{1,0:T(8,128)}, f32[512,256]{1,0:T(8,128)}, u32[]{:S(2)}, u32[]{:S(2)}) collective-permute-start(f32[512,256]{1,0:T(8,128)} %collective-permute-done.13.refs_8_.below), channel_id=1, source_target_pairs={{0,64},{64,128},{128,192},{192,256},{256,320},{320,384},{384,448},... | collective-permute-start | bytes 1572872 | tf_op jit(solution)/shard_map/vectors_along_z/ppermute | solution.py:198
  86.1 8.6 %collective-permute-start.18 = (f32[192,512]{1,0:T(8,128)}, f32[192,512]{1,0:T(8,128)S(1)}, u32[]{:S(2)}, u32[]{:S(2)}) collective-permute-start(f32[192,512]{1,0:T(8,128)} %maximum_select_fusion), channel_id=1, source_target_pairs={{0,192},{448,256},{1,193},{449,257},{2,194},{450,258},{3,195},{451... | collective-permute-start | bytes 1179656 | tf_op jit(solution)/shard_map/ends_to_middle/ppermute | solution.py:205
  94.7 1.3 collective-permute-start.17
  96.0 4.8 %collective-permute-start.15 = (f32[512,256]{1,0:T(8,128)}, f32[512,256]{1,0:T(8,128)}, u32[]{:S(2)}, u32[]{:S(2)}) collective-permute-start(f32[512,256]{1,0:T(8,128)} %collective-permute-done.14.refs_8_), channel_id=1, source_target_pairs={{0,64},{64,128},{128,192},{192,256},{256,320},{320,384},{384,448},... | collective-permute-start | bytes 1572872 | tf_op jit(solution)/shard_map/vectors_along_z/ppermute | solution.py:198
  103.9 12.9 %collective-permute-start.19 = (f32[192,256]{1,0:T(8,128)S(1)}, f32[192,256]{1,0:T(8,128)S(1)}, u32[]{:S(2)}, u32[]{:S(2)}) collective-permute-start(f32[192,256]{1,0:T(8,128)S(1)} %get-tuple-element.82), channel_id=1, source_target_pairs={{0,1},{1,0},{2,3},{3,2},{4,5},{5,4},{6,7},{7,6},{8,9},{9,8},{10,11... | collective-permute-start | bytes 589832 | tf_op jit(solution)/shard_map/ends_to_middle/ppermute | solution.py:172
  117.9 1.3 collective-permute-start.20
  124.7 2.2 %add_chunks.11.refs_18_ = f32[2,192,256]{2,1,0:T(8,128)S(1)} custom-call(s32[5]{0:T(128)S(1)} %stack.19.info, f32[48,2048]{1,0:T(8,128)S(1)} %get-tuple-element.72.refs_0_.refs_9_, f32[48,2048]{1,0:T(8,128)S(1)} %collective-permute-done.1.refs_1_.refs_10_, f32[48,2048]{1,0:T(8,128)S(1)} %collective-permute-done.7.refs_2_.refs_11_, ...), custom_call_target="tpu_custom_call", output_to_operand_aliasing={{}: (19, {})} | custom-call | flops 301989888 | bytes 4194304 | tf_op jit(solution)/shard_map/add_chunks/pallas_call | solution.py:125
  126.9 2.2 %add_chunks.12.refs_18_ = f32[2,192,256]{2,1,0:T(8,128)S(1)} custom-call(s32[5]{0:T(128)S(1)} %stack.19.info, f32[48,2048]{1,0:T(8,128)S(1)} %get-tuple-element.72.refs_0_.refs_9_, f32[48,2048]{1,0:T(8,128)S(1)} %collective-permute-done.1.refs_1_.refs_10_, f32[48,2048]{1,0:T(8,128)S(1)} %collective-permute-done.7.refs_2_.refs_11_, ...), custom_call_target="tpu_custom_call", output_to_operand_aliasing={{}: (19, {})} | custom-call | flops 301989888 | bytes 4194304 | tf_op jit(solution)/shard_map/add_chunks/pallas_call | solution.py:125
  129.0 2.6 %collective-permute-done.20.refs_19_ = f32[192,256]{1,0:T(8,128)S(1)} collective-permute-done((f32[192,256]{1,0:T(8,128)S(1)}, f32[192,256]{1,0:T(8,128)S(1)}, u32[]{:S(2)}, u32[]{:S(2)}) %collective-permute-start.20) | collective-permute-done | bytes 196640 | tf_op jit(solution)/shard_map/ends_to_middle/ppermute | solution.py:208
  131.6 2.3 %add_chunks.13 = f32[32,24,128]{2,1,0:T(8,128)S(1)} custom-call(s32[5]{0:T(128)S(1)} %stack.19.info, f32[48,2048]{1,0:T(8,128)S(1)} %get-tuple-element.72.refs_0_.refs_9_, f32[48,2048]{1,0:T(8,128)S(1)} %collective-permute-done.1.refs_1_.refs_10_, f32[48,2048]{1,0:T(8,128)S(1)} %collective-permute-done.7.refs_2_.refs_11_, ...), custom_call_target="tpu_custom_call" | custom-call | flops 301989888 | bytes 4194304 | tf_op jit(solution)/shard_map/add_chunks/pallas_call | solution.py:125
  133.9 17.7 %all_to_all.5 = f32[32,24,128]{2,1,0:T(8,128)S(1)} all-to-all(f32[32,24,128]{2,1,0:T(8,128)S(1)} %add_chunks.13), channel_id=1, replica_groups=mesh['z'=8,'y'=4,'x'=4,'half'=2,'core'=2] {'y','x','core'}, dimensions={0} | all-to-all | bytes 786432 | tf_op jit(solution)/shard_map/sum_over_columns/all_to_all | solution.py:216
  151.7 12.4 %collective-permute-start.21 = (f32[24,128]{1,0:T(8,128)S(1)}, f32[24,128]{1,0:T(8,128)S(1)}, u32[]{:S(2)}, u32[]{:S(2)}) collective-permute-start(f32[24,128]{1,0:T(8,128)S(1)} %reduce_sum.9), channel_id=1, source_target_pairs={{0,2},{2,0},{1,3},{3,1},{4,6},{6,4},{5,7},{7,5},{8,10},{10,8},{9,1... | collective-permute-start | bytes 36872 | tf_op jit(solution)/shard_map/sum_over_columns/ppermute | solution.py:172
  (66 shorter events, 19.4 us)
Async XLA Ops:
  0.0 20.2 %collective-permute-start = (f32[512,256]{1,0:T(8,128)}, f32[512,256]{1,0:T(8,128)S(1)}, u32[]{:S(2)}, u32[]{:S(2)}) collective-permute-start(f32[512,256]{1,0:T(8,128)} %refs_8_.1), channel_id=1, source_target_pairs={{64,0},{128,64},{192,128},{256,192},{320,256},{384,320},{448,384},... | collective-permute-start | bytes 1572872 | tf_op jit(solution)/shard_map/vectors_along_z/ppermute | solution.py:199
  1.3 21.0 %collective-permute-start.10 = (f32[512,256]{1,0:T(8,128)}, f32[512,256]{1,0:T(8,128)S(1)}, u32[]{:S(2)}, u32[]{:S(2)}) collective-permute-start(f32[512,256]{1,0:T(8,128)} %refs_8_.1), channel_id=1, source_target_pairs={{0,64},{64,128},{128,192},{192,256},{256,320},{320,384},{384,448},... | collective-permute-start | bytes 1572872 | tf_op jit(solution)/shard_map/vectors_along_z/ppermute | solution.py:198
  6.3 1.9 %copy-start = (f32[48,16384]{1,0:T(8,128)S(1)}, f32[48,16384]{1,0:T(8,128)}, u32[]{:S(2)}) copy-start(f32[48,16384]{1,0:T(8,128)} %slab.1) | copy-start | bytes 9437188
  8.4 9.8 %collective-permute-start.1 = (f32[48,2048]{1,0:T(8,128)S(1)}, f32[48,2048]{1,0:T(8,128)S(1)}, u32[]{:S(2)}, u32[]{:S(2)}) collective-permute-start(f32[48,2048]{1,0:T(8,128)S(1)} %get-tuple-element.46), channel_id=1, source_target_pairs={{0,16},{16,32},{32,48},{48,0},{1,17},{17,33},{33,49},{49,1},{2,18}... | collective-permute-start | bytes 1179656 | tf_op jit(solution)/shard_map/basis_along_y/ppermute | solution.py:172
  11.6 8.5 %collective-permute-start.2 = (f32[48,2048]{1,0:T(8,128)S(1)}, f32[48,2048]{1,0:T(8,128)S(1)}, u32[]{:S(2)}, u32[]{:S(2)}) collective-permute-start(f32[48,2048]{1,0:T(8,128)S(1)} %get-tuple-element.50), channel_id=1, source_target_pairs={{0,48},{16,0},{32,16},{48,32},{1,49},{17,1},{33,17},{49,33},{2,50}... | collective-permute-start | bytes 1179656 | tf_op jit(solution)/shard_map/basis_along_y/ppermute | solution.py:172
  20.2 21.9 %collective-permute-start.3 = (f32[512,256]{1,0:T(8,128)S(1)}, f32[512,256]{1,0:T(8,128)S(1)}, u32[]{:S(2)}, u32[]{:S(2)}) collective-permute-start(f32[512,256]{1,0:T(8,128)S(1)} %collective-permute-done.refs_17_), channel_id=1, source_target_pairs={{64,0},{128,64},{192,128},{256,192},{320,256},{384,320},{448,384},... | collective-permute-start | bytes 1572872 | tf_op jit(solution)/shard_map/vectors_along_z/ppermute | solution.py:199
  21.5 0.8 copy-start.2
  22.3 21.9 %collective-permute-start.11 = (f32[512,256]{1,0:T(8,128)S(1)}, f32[512,256]{1,0:T(8,128)S(1)}, u32[]{:S(2)}, u32[]{:S(2)}) collective-permute-start(f32[512,256]{1,0:T(8,128)S(1)} %collective-permute-done.10.refs_8_), channel_id=1, source_target_pairs={{0,64},{64,128},{128,192},{192,256},{256,320},{320,384},{384,448},... | collective-permute-start | bytes 1572872 | tf_op jit(solution)/shard_map/vectors_along_z/ppermute | solution.py:198
  28.0 10.3 %collective-permute-start.4 = (f32[48,2048]{1,0:T(8,128)S(1)}, f32[48,2048]{1,0:T(8,128)S(1)}, u32[]{:S(2)}, u32[]{:S(2)}) collective-permute-start(f32[48,2048]{1,0:T(8,128)S(1)} %get-tuple-element.47), channel_id=1, source_target_pairs={{0,16},{16,32},{32,48},{48,0},{1,17},{17,33},{33,49},{49,1},{2,18}... | collective-permute-start | bytes 1179656 | tf_op jit(solution)/shard_map/basis_along_y/ppermute | solution.py:172
  33.1 9.0 %collective-permute-start.5 = (f32[48,2048]{1,0:T(8,128)S(1)}, f32[48,2048]{1,0:T(8,128)S(1)}, u32[]{:S(2)}, u32[]{:S(2)}) collective-permute-start(f32[48,2048]{1,0:T(8,128)S(1)} %get-tuple-element.51), channel_id=1, source_target_pairs={{0,48},{16,0},{32,16},{48,32},{1,49},{17,1},{33,17},{49,33},{2,50}... | collective-permute-start | bytes 1179656 | tf_op jit(solution)/shard_map/basis_along_y/ppermute | solution.py:172
  42.1 17.7 %collective-permute-start.6 = (f32[512,256]{1,0:T(8,128)S(1)}, f32[512,256]{1,0:T(8,128)S(1)}, u32[]{:S(2)}, u32[]{:S(2)}) collective-permute-start(f32[512,256]{1,0:T(8,128)S(1)} %collective-permute-done.3.refs_17_), channel_id=1, source_target_pairs={{64,0},{128,64},{192,128},{256,192},{320,256},{384,320},{448,384},... | collective-permute-start | bytes 1572872 | tf_op jit(solution)/shard_map/vectors_along_z/ppermute | solution.py:199
  44.2 17.7 %collective-permute-start.12 = (f32[512,256]{1,0:T(8,128)S(1)}, f32[512,256]{1,0:T(8,128)S(1)}, u32[]{:S(2)}, u32[]{:S(2)}) collective-permute-start(f32[512,256]{1,0:T(8,128)S(1)} %collective-permute-done.11.refs_8_), channel_id=1, source_target_pairs={{0,64},{64,128},{128,192},{192,256},{256,320},{320,384},{384,448},... | collective-permute-start | bytes 1572872 | tf_op jit(solution)/shard_map/vectors_along_z/ppermute | solution.py:198
  49.7 10.0 %collective-permute-start.7 = (f32[48,2048]{1,0:T(8,128)S(1)}, f32[48,2048]{1,0:T(8,128)S(1)}, u32[]{:S(2)}, u32[]{:S(2)}) collective-permute-start(f32[48,2048]{1,0:T(8,128)S(1)} %get-tuple-element.48), channel_id=1, source_target_pairs={{0,32},{16,48},{32,0},{48,16},{1,33},{17,49},{33,1},{49,17},{2,34}... | collective-permute-start | bytes 1179656 | tf_op jit(solution)/shard_map/basis_along_y/ppermute | solution.py:172
  59.8 19.2 %collective-permute-start.8 = (f32[512,256]{1,0:T(8,128)S(1)}, f32[512,256]{1,0:T(8,128)}, u32[]{:S(2)}, u32[]{:S(2)}) collective-permute-start(f32[512,256]{1,0:T(8,128)S(1)} %collective-permute-done.6.refs_17_), channel_id=1, source_target_pairs={{64,0},{128,64},{192,128},{256,192},{320,256},{384,320},{448,384},... | collective-permute-start | bytes 1572872 | tf_op jit(solution)/shard_map/vectors_along_z/ppermute | solution.py:199
  61.8 18.4 %collective-permute-start.13 = (f32[512,256]{1,0:T(8,128)S(1)}, f32[512,256]{1,0:T(8,128)}, u32[]{:S(2)}, u32[]{:S(2)}) collective-permute-start(f32[512,256]{1,0:T(8,128)S(1)} %collective-permute-done.12.refs_8_), channel_id=1, source_target_pairs={{0,64},{64,128},{128,192},{192,256},{256,320},{320,384},{384,448},... | collective-permute-start | bytes 1572872 | tf_op jit(solution)/shard_map/vectors_along_z/ppermute | solution.py:198
  68.1 0.8 copy-start.12
  68.9 10.0 %collective-permute-start.9 = (f32[48,2048]{1,0:T(8,128)S(1)}, f32[48,2048]{1,0:T(8,128)S(1)}, u32[]{:S(2)}, u32[]{:S(2)}) collective-permute-start(f32[48,2048]{1,0:T(8,128)S(1)} %get-tuple-element.49), channel_id=1, source_target_pairs={{0,32},{16,48},{32,0},{48,16},{1,33},{17,49},{33,1},{49,17},{2,34}... | collective-permute-start | bytes 1179656 | tf_op jit(solution)/shard_map/basis_along_y/ppermute | solution.py:172
  78.9 15.7 %collective-permute-start.16 = (f32[512,256]{1,0:T(8,128)}, f32[512,256]{1,0:T(8,128)}, u32[]{:S(2)}, u32[]{:S(2)}) collective-permute-start(f32[512,256]{1,0:T(8,128)} %collective-permute-done.8.refs_17_.above), channel_id=1, source_target_pairs={{64,0},{128,64},{192,128},{256,192},{320,256},{384,320},{448,384},... | collective-permute-start | bytes 1572872 | tf_op jit(solution)/shard_map/vectors_along_z/ppermute | solution.py:199
  80.2 15.7 %collective-permute-start.14 = (f32[512,256]{1,0:T(8,128)}, f32[512,256]{1,0:T(8,128)}, u32[]{:S(2)}, u32[]{:S(2)}) collective-permute-start(f32[512,256]{1,0:T(8,128)} %collective-permute-done.13.refs_8_.below), channel_id=1, source_target_pairs={{0,64},{64,128},{128,192},{192,256},{256,320},{320,384},{384,448},... | collective-permute-start | bytes 1572872 | tf_op jit(solution)/shard_map/vectors_along_z/ppermute | solution.py:198
  86.1 16.6 %collective-permute-start.18 = (f32[192,512]{1,0:T(8,128)}, f32[192,512]{1,0:T(8,128)S(1)}, u32[]{:S(2)}, u32[]{:S(2)}) collective-permute-start(f32[192,512]{1,0:T(8,128)} %maximum_select_fusion), channel_id=1, source_target_pairs={{0,192},{448,256},{1,193},{449,257},{2,194},{450,258},{3,195},{451... | collective-permute-start | bytes 1179656 | tf_op jit(solution)/shard_map/ends_to_middle/ppermute | solution.py:205
  94.7 36.9 %collective-permute-start.17 = (f32[512,256]{1,0:T(8,128)}, f32[512,256]{1,0:T(8,128)}, u32[]{:S(2)}, u32[]{:S(2)}) collective-permute-start(f32[512,256]{1,0:T(8,128)} %collective-permute-done.16.refs_17_), channel_id=1, source_target_pairs={{64,0},{128,64},{192,128},{256,192},{320,256},{384,320},{448,384},... | collective-permute-start | bytes 1572872 | tf_op jit(solution)/shard_map/vectors_along_z/ppermute | solution.py:199
  96.0 35.6 %collective-permute-start.15 = (f32[512,256]{1,0:T(8,128)}, f32[512,256]{1,0:T(8,128)}, u32[]{:S(2)}, u32[]{:S(2)}) collective-permute-start(f32[512,256]{1,0:T(8,128)} %collective-permute-done.14.refs_8_), channel_id=1, source_target_pairs={{0,64},{64,128},{128,192},{192,256},{256,320},{320,384},{384,448},... | collective-permute-start | bytes 1572872 | tf_op jit(solution)/shard_map/vectors_along_z/ppermute | solution.py:198
  101.5 19.7 %copy-start.3 = (f32[512,256]{1,0:T(8,128)S(1)}, f32[512,256]{1,0:T(8,128)}, u32[]{:S(2)}) copy-start(f32[512,256]{1,0:T(8,128)} %copy-done.2) | copy-start | bytes 1572868
  101.5 19.7 %copy-start.5 = (f32[512,256]{1,0:T(8,128)S(1)}, f32[512,256]{1,0:T(8,128)}, u32[]{:S(2)}) copy-start(f32[512,256]{1,0:T(8,128)} %copy-done.4) | copy-start | bytes 1572868
  103.9 13.9 %collective-permute-start.19 = (f32[192,256]{1,0:T(8,128)S(1)}, f32[192,256]{1,0:T(8,128)S(1)}, u32[]{:S(2)}, u32[]{:S(2)}) collective-permute-start(f32[192,256]{1,0:T(8,128)S(1)} %get-tuple-element.82), channel_id=1, source_target_pairs={{0,1},{1,0},{2,3},{3,2},{4,5},{5,4},{6,7},{7,6},{8,9},{9,8},{10,11... | collective-permute-start | bytes 589832 | tf_op jit(solution)/shard_map/ends_to_middle/ppermute | solution.py:172
  117.9 13.7 %collective-permute-start.20 = (f32[192,256]{1,0:T(8,128)S(1)}, f32[192,256]{1,0:T(8,128)S(1)}, u32[]{:S(2)}, u32[]{:S(2)}) collective-permute-start(f32[192,256]{1,0:T(8,128)S(1)} %add.17), channel_id=1, source_target_pairs={{192,0},{256,448},{193,1},{257,449},{194,2},{258,450},{195,3},{259... | collective-permute-start | bytes 589832 | tf_op jit(solution)/shard_map/ends_to_middle/ppermute | solution.py:208
  119.2 1.0 copy-start.1
  121.2 1.1 copy-start.7
  121.2 1.2 copy-start.9
  122.4 1.1 copy-start.11
  122.4 1.2 copy-start.13
  151.7 13.4 %collective-permute-start.21 = (f32[24,128]{1,0:T(8,128)S(1)}, f32[24,128]{1,0:T(8,128)S(1)}, u32[]{:S(2)}, u32[]{:S(2)}) collective-permute-start(f32[24,128]{1,0:T(8,128)S(1)} %reduce_sum.9), channel_id=1, source_target_pairs={{0,2},{2,0},{1,3},{3,1},{4,6},{6,4},{5,7},{7,5},{8,10},{10,8},{9,1... | collective-permute-start | bytes 36872 | tf_op jit(solution)/shard_map/sum_over_columns/ppermute | solution.py:172
  (4 other events, 3.2 us)

commit v4 on v2

--- a/solution.py
+++ b/solution.py
@@ -145,7 +145,7 @@
     for step in range(1, Z):
         if step == 2:
             below[-1], above[-1], packed = lax.optimization_barrier((below[-1], above[-1], packed))
-        ready = {3: (1,), 4: (3,), 5: (2,)}.get(step, ())
+        ready = {4: (1,), 5: (3,), 7: (2,)}.get(step, ())
         for k in ready:
             with jax.named_scope("basis_along_y"):
                 basis[k] = shift(packed[k], "y", Y, k)

time: 160 us -> 146 us (0.912)
  the two profiles are of different devices: /device:TPU:128 before, /device:TPU:1 now
where the time goes in v4:
time: 146 us; the launch traced here: 143 us
  starting transfers between devices  68.7 us (47%)
  waiting for transfers between devices  27.2 us (19%)
  blocking collectives  23.1 us (16%)
  local copies, waits for them, and re-layouts  12.6 us (9%)
  Pallas kernels  10.5 us (7%)
    ppermute x7, starting transfers between devices, local(): below.append(lax.ppermute(below[-1], 'z', up))  36.4 us
    ppermute x4, starting transfers between devices, shift(): return lax.ppermute(a, axis, [(i, (i + by) % size) for i in range(size)])  23.3 us
    all_to_all x1, blocking collectives, local(): got = lax.all_to_all(total, ('y', 'x', 'core'), 0, 0, tiled=True)  23.1 us
    ppermute x4, waiting for transfers between devices, shift(): return lax.ppermute(a, axis, [(i, (i + by) % size) for i in range(size)])  12.8 us
    unnamed x44, local copies, waits for them, and re-layouts  11.9 us
    pallas_call x8, Pallas kernels, add_chunks(): pl.pallas_call(functools.partial(add_kernel, [off for _, off in pieces],...  10.3 us
    ppermute x7, waiting for transfers between devices, local(): above.append(lax.ppermute(above[-1], 'z', down))  9.78 us
    ppermute x7, starting transfers between devices, local(): above.append(lax.ppermute(above[-1], 'z', down))  8.99 us
  transfers between devices with their start and end apart: 18, of which 8 were waited for; matrix products, arithmetic and copies ran while one was open for 0% of the time, Pallas kernels for 6%

profile of v4, /device:TPU:1, one launch (start us, length us, event | category | flops | bytes accessed | tf_op | source)
XLA Modules:
  0.0 143.3 jit_solution(3300783627890007628)
XLA Ops:
  0.0 4.4 %collective-permute-start = (f32[512,256]{1,0:T(8,128)}, f32[512,256]{1,0:T(8,128)S(1)}, u32[]{:S(2)}, u32[]{:S(2)}) collective-permute-start(f32[512,256]{1,0:T(8,128)} %refs_4_.1), channel_id=1, source_target_pairs={{0,64},{64,128},{128,192},{192,256},{256,320},{320,384},{384,448},... | collective-permute-start | bytes 1572872 | tf_op jit(solution)/shard_map/vectors_along_z/ppermute | solution.py:155
  4.4 1.3 collective-permute-start.1
  5.7 1.9 %copy-done = f32[48,16384]{1,0:T(8,128)S(1)} copy-done((f32[48,16384]{1,0:T(8,128)S(1)}, f32[48,16384]{1,0:T(8,128)}, u32[]{:S(2)}) %copy-start) | copy-done | bytes 3145752
  7.8 4.6 %collective-permute-done.refs_4_ = f32[512,256]{1,0:T(8,128)S(1)} collective-permute-done((f32[512,256]{1,0:T(8,128)}, f32[512,256]{1,0:T(8,128)S(1)}, u32[]{:S(2)}, u32[]{:S(2)}) %collective-permute-start) | collective-permute-done | bytes 524320 | tf_op jit(solution)/shard_map/vectors_along_z/ppermute | solution.py:155
  12.4 4.1 %collective-permute-done.1.refs_9_ = f32[512,256]{1,0:T(8,128)S(1)} collective-permute-done((f32[512,256]{1,0:T(8,128)}, f32[512,256]{1,0:T(8,128)S(1)}, u32[]{:S(2)}, u32[]{:S(2)}) %collective-permute-start.1) | collective-permute-done | bytes 524320 | tf_op jit(solution)/shard_map/vectors_along_z/ppermute | solution.py:156
  16.4 1.3 collective-permute-start.2
  18.5 7.1 %collective-permute-start.10 = (f32[512,256]{1,0:T(8,128)S(1)}, f32[512,256]{1,0:T(8,128)S(1)}, u32[]{:S(2)}, u32[]{:S(2)}) collective-permute-start(f32[512,256]{1,0:T(8,128)S(1)} %collective-permute-done.refs_4_), channel_id=1, source_target_pairs={{0,64},{64,128},{128,192},{192,256},{256,320},{320,384},{384,448},... | collective-permute-start | bytes 1572872 | tf_op jit(solution)/shard_map/vectors_along_z/ppermute | solution.py:155
  26.4 3.2 %collective-permute-start.4 = (f32[48,4096]{1,0:T(8,128)S(1)}, f32[48,4096]{1,0:T(8,128)S(1)}, u32[]{:S(2)}, u32[]{:S(2)}) collective-permute-start(f32[48,4096]{1,0:T(8,128)S(1)} %get-tuple-element.31), channel_id=1, source_target_pairs={{0,16},{16,32},{32,48},{48,0},{1,17},{17,33},{33,49},{49,1},{2,18}... | collective-permute-start | bytes 2359304 | tf_op jit(solution)/shard_map/basis_along_y/ppermute | solution.py:129
  29.6 3.7 %collective-permute-done.2.refs_9_ = f32[512,256]{1,0:T(8,128)S(1)} collective-permute-done((f32[512,256]{1,0:T(8,128)S(1)}, f32[512,256]{1,0:T(8,128)S(1)}, u32[]{:S(2)}, u32[]{:S(2)}) %collective-permute-start.2) | collective-permute-done | bytes 524320 | tf_op jit(solution)/shard_map/vectors_along_z/ppermute | solution.py:156
  33.4 1.3 collective-permute-start.3
  35.4 5.7 %collective-permute-start.11 = (f32[512,256]{1,0:T(8,128)S(1)}, f32[512,256]{1,0:T(8,128)S(1)}, u32[]{:S(2)}, u32[]{:S(2)}) collective-permute-start(f32[512,256]{1,0:T(8,128)S(1)} %collective-permute-done.10.refs_4_), channel_id=1, source_target_pairs={{0,64},{64,128},{128,192},{192,256},{256,320},{320,384},{384,448},... | collective-permute-start | bytes 1572872 | tf_op jit(solution)/shard_map/vectors_along_z/ppermute | solution.py:155
  42.0 4.6 %collective-permute-start.6 = (f32[48,4096]{1,0:T(8,128)S(1)}, f32[48,4096]{1,0:T(8,128)S(1)}, u32[]{:S(2)}, u32[]{:S(2)}) collective-permute-start(f32[48,4096]{1,0:T(8,128)S(1)} %get-tuple-element.35), channel_id=1, source_target_pairs={{0,48},{16,0},{32,16},{48,32},{1,49},{17,1},{33,17},{49,33},{2,50}... | collective-permute-start | bytes 2359304 | tf_op jit(solution)/shard_map/basis_along_y/ppermute | solution.py:129
  46.7 1.8 %collective-permute-done.3.refs_9_ = f32[512,256]{1,0:T(8,128)S(1)} collective-permute-done((f32[512,256]{1,0:T(8,128)S(1)}, f32[512,256]{1,0:T(8,128)S(1)}, u32[]{:S(2)}, u32[]{:S(2)}) %collective-permute-start.3) | collective-permute-done | bytes 524320 | tf_op jit(solution)/shard_map/vectors_along_z/ppermute | solution.py:156
  48.5 1.3 collective-permute-start.5
  50.5 4.3 %collective-permute-start.12 = (f32[512,256]{1,0:T(8,128)S(1)}, f32[512,256]{1,0:T(8,128)S(1)}, u32[]{:S(2)}, u32[]{:S(2)}) collective-permute-start(f32[512,256]{1,0:T(8,128)S(1)} %collective-permute-done.11.refs_4_), channel_id=1, source_target_pairs={{0,64},{64,128},{128,192},{192,256},{256,320},{320,384},{384,448},... | collective-permute-start | bytes 1572872 | tf_op jit(solution)/shard_map/vectors_along_z/ppermute | solution.py:155
  55.6 5.3 %collective-permute-done.6.refs_3_.refs_8_ = f32[48,4096]{1,0:T(8,128)S(1)} collective-permute-done((f32[48,4096]{1,0:T(8,128)S(1)}, f32[48,4096]{1,0:T(8,128)S(1)}, u32[]{:S(2)}, u32[]{:S(2)}) %collective-permute-start.6) | collective-permute-done | bytes 786464 | tf_op jit(solution)/shard_map/basis_along_y/ppermute | solution.py:129
  61.1 1.3 collective-permute-start.7
  63.2 4.4 %collective-permute-start.13 = (f32[512,256]{1,0:T(8,128)S(1)}, f32[512,256]{1,0:T(8,128)S(1)}, u32[]{:S(2)}, u32[]{:S(2)}) collective-permute-start(f32[512,256]{1,0:T(8,128)S(1)} %collective-permute-done.12.refs_4_), channel_id=1, source_target_pairs={{0,64},{64,128},{128,192},{192,256},{256,320},{320,384},{384,448},... | collective-permute-start | bytes 1572872 | tf_op jit(solution)/shard_map/vectors_along_z/ppermute | solution.py:155
  68.4 4.8 %collective-permute-start.9 = (f32[48,4096]{1,0:T(8,128)S(1)}, f32[48,4096]{1,0:T(8,128)S(1)}, u32[]{:S(2)}, u32[]{:S(2)}) collective-permute-start(f32[48,4096]{1,0:T(8,128)S(1)} %get-tuple-element.39), channel_id=1, source_target_pairs={{0,32},{16,48},{32,0},{48,16},{1,33},{17,49},{33,1},{49,17},{2,34}... | collective-permute-start | bytes 2359304 | tf_op jit(solution)/shard_map/basis_along_y/ppermute | solution.py:129
  73.2 1.3 collective-permute-start.8
  75.3 5.4 %collective-permute-start.14 = (f32[512,256]{1,0:T(8,128)S(1)}, f32[512,256]{1,0:T(8,128)}, u32[]{:S(2)}, u32[]{:S(2)}) collective-permute-start(f32[512,256]{1,0:T(8,128)S(1)} %collective-permute-done.13.refs_4_), channel_id=1, source_target_pairs={{0,64},{64,128},{128,192},{192,256},{256,320},{320,384},{384,448},... | collective-permute-start | bytes 1572872 | tf_op jit(solution)/shard_map/vectors_along_z/ppermute | solution.py:155
  81.5 4.9 %collective-permute-done.9.refs_2_.refs_7_ = f32[48,4096]{1,0:T(8,128)S(1)} collective-permute-done((f32[48,4096]{1,0:T(8,128)S(1)}, f32[48,4096]{1,0:T(8,128)S(1)}, u32[]{:S(2)}, u32[]{:S(2)}) %collective-permute-start.9) | collective-permute-done | bytes 786464 | tf_op jit(solution)/shard_map/basis_along_y/ppermute | solution.py:129
  86.5 1.3 collective-permute-start.16
  87.8 5.1 %collective-permute-start.15 = (f32[512,256]{1,0:T(8,128)}, f32[512,256]{1,0:T(8,128)}, u32[]{:S(2)}, u32[]{:S(2)}) collective-permute-start(f32[512,256]{1,0:T(8,128)} %collective-permute-done.14.refs_4_), channel_id=1, source_target_pairs={{0,64},{64,128},{128,192},{192,256},{256,320},{320,384},{384,448},... | collective-permute-start | bytes 1572872 | tf_op jit(solution)/shard_map/vectors_along_z/ppermute | solution.py:155
  93.6 1.0 copy-done.1
  95.9 1.0 add_chunks.9.refs_10_
  98.3 1.0 add_chunks.11.refs_10_
  101.7 2.2 %add_chunks.14.refs_10_ = f32[2,192,256]{2,1,0:T(8,128)S(1)} custom-call(s32[4]{0:T(128)S(1)} %pad_add_fusion.info, f32[48,4096]{1,0:T(8,128)S(1)} %get-tuple-element.41.refs_0_.refs_5_, f32[48,4096]{1,0:T(8,128)S(1)} %collective-permute-done.4.refs_1_.refs_6_, ...), custom_call_target="tpu_custom_call", output_to_operand_aliasing={{}: (11, {})} | custom-call | flops 301989888 | bytes 4194304 | tf_op jit(solution)/shard_map/add_chunks/pallas_call | solution.py:111
  103.9 2.3 %add_chunks.15 = f32[32,24,128]{2,1,0:T(8,128)S(1)} custom-call(s32[4]{0:T(128)S(1)} %pad_add_fusion.info, f32[48,4096]{1,0:T(8,128)S(1)} %get-tuple-element.41.refs_0_.refs_5_, f32[48,4096]{1,0:T(8,128)S(1)} %collective-permute-done.4.refs_1_.refs_6_, f32[48,4096]{1,0:T(8,128)S(1)} %collective-permute-done.9.refs_2_.refs_7_, ...), custom_call_target="tpu_custom_call" | custom-call | flops 301989888 | bytes 4194304 | tf_op jit(solution)/shard_map/add_chunks/pallas_call | solution.py:111
  106.2 23.1 %all_to_all.5 = f32[32,24,128]{2,1,0:T(8,128)S(1)} all-to-all(f32[32,24,128]{2,1,0:T(8,128)S(1)} %add_chunks.15), channel_id=1, replica_groups=mesh['z'=8,'y'=4,'x'=4,'half'=2,'core'=2] {'y','x','core'}, dimensions={0} | all-to-all | bytes 786432 | tf_op jit(solution)/shard_map/sum_over_columns/all_to_all | solution.py:164
  129.3 10.6 %collective-permute-start.17 = (f32[24,128]{1,0:T(8,128)S(1)}, f32[24,128]{1,0:T(8,128)S(1)}, u32[]{:S(2)}, u32[]{:S(2)}) collective-permute-start(f32[24,128]{1,0:T(8,128)S(1)} %reduce_sum.9), channel_id=1, source_target_pairs={{0,2},{2,0},{1,3},{3,1},{4,6},{6,4},{5,7},{7,5},{8,10},{10,8},{9,1... | collective-permute-start | bytes 36872 | tf_op jit(solution)/shard_map/sum_over_columns/ppermute | solution.py:129
  139.9 2.5 %collective-permute-done.17 = f32[24,128]{1,0:T(8,128)S(1)} collective-permute-done((f32[24,128]{1,0:T(8,128)S(1)}, f32[24,128]{1,0:T(8,128)S(1)}, u32[]{:S(2)}, u32[]{:S(2)}) %collective-permute-start.17) | collective-permute-done | bytes 12320 | tf_op jit(solution)/shard_map/sum_over_columns/ppermute | solution.py:129
  (64 shorter events, 14.3 us)
Async XLA Ops:
  0.0 12.4 %collective-permute-start = (f32[512,256]{1,0:T(8,128)}, f32[512,256]{1,0:T(8,128)S(1)}, u32[]{:S(2)}, u32[]{:S(2)}) collective-permute-start(f32[512,256]{1,0:T(8,128)} %refs_4_.1), channel_id=1, source_target_pairs={{0,64},{64,128},{128,192},{192,256},{256,320},{320,384},{384,448},... | collective-permute-start | bytes 1572872 | tf_op jit(solution)/shard_map/vectors_along_z/ppermute | solution.py:155
  4.4 12.0 %collective-permute-start.1 = (f32[512,256]{1,0:T(8,128)}, f32[512,256]{1,0:T(8,128)S(1)}, u32[]{:S(2)}, u32[]{:S(2)}) collective-permute-start(f32[512,256]{1,0:T(8,128)} %refs_4_.1), channel_id=1, source_target_pairs={{64,0},{128,64},{192,128},{256,192},{320,256},{384,320},{448,384},... | collective-permute-start | bytes 1572872 | tf_op jit(solution)/shard_map/vectors_along_z/ppermute | solution.py:156
  5.7 1.9 %copy-start = (f32[48,16384]{1,0:T(8,128)S(1)}, f32[48,16384]{1,0:T(8,128)}, u32[]{:S(2)}) copy-start(f32[48,16384]{1,0:T(8,128)} %slab.1) | copy-start | bytes 9437188
  16.4 16.9 %collective-permute-start.2 = (f32[512,256]{1,0:T(8,128)S(1)}, f32[512,256]{1,0:T(8,128)S(1)}, u32[]{:S(2)}, u32[]{:S(2)}) collective-permute-start(f32[512,256]{1,0:T(8,128)S(1)} %collective-permute-done.1.refs_9_), channel_id=1, source_target_pairs={{64,0},{128,64},{192,128},{256,192},{320,256},{384,320},{448,384},... | collective-permute-start | bytes 1572872 | tf_op jit(solution)/shard_map/vectors_along_z/ppermute | solution.py:156
  18.5 16.9 %collective-permute-start.10 = (f32[512,256]{1,0:T(8,128)S(1)}, f32[512,256]{1,0:T(8,128)S(1)}, u32[]{:S(2)}, u32[]{:S(2)}) collective-permute-start(f32[512,256]{1,0:T(8,128)S(1)} %collective-permute-done.refs_4_), channel_id=1, source_target_pairs={{0,64},{64,128},{128,192},{192,256},{256,320},{320,384},{384,448},... | collective-permute-start | bytes 1572872 | tf_op jit(solution)/shard_map/vectors_along_z/ppermute | solution.py:155
  26.4 20.2 %collective-permute-start.4 = (f32[48,4096]{1,0:T(8,128)S(1)}, f32[48,4096]{1,0:T(8,128)S(1)}, u32[]{:S(2)}, u32[]{:S(2)}) collective-permute-start(f32[48,4096]{1,0:T(8,128)S(1)} %get-tuple-element.31), channel_id=1, source_target_pairs={{0,16},{16,32},{32,48},{48,0},{1,17},{17,33},{33,49},{49,1},{2,18}... | collective-permute-start | bytes 2359304 | tf_op jit(solution)/shard_map/basis_along_y/ppermute | solution.py:129
  33.4 15.1 %collective-permute-start.3 = (f32[512,256]{1,0:T(8,128)S(1)}, f32[512,256]{1,0:T(8,128)S(1)}, u32[]{:S(2)}, u32[]{:S(2)}) collective-permute-start(f32[512,256]{1,0:T(8,128)S(1)} %collective-permute-done.2.refs_9_), channel_id=1, source_target_pairs={{64,0},{128,64},{192,128},{256,192},{320,256},{384,320},{448,384},... | collective-permute-start | bytes 1572872 | tf_op jit(solution)/shard_map/vectors_along_z/ppermute | solution.py:156
  35.4 15.1 %collective-permute-start.11 = (f32[512,256]{1,0:T(8,128)S(1)}, f32[512,256]{1,0:T(8,128)S(1)}, u32[]{:S(2)}, u32[]{:S(2)}) collective-permute-start(f32[512,256]{1,0:T(8,128)S(1)} %collective-permute-done.10.refs_4_), channel_id=1, source_target_pairs={{0,64},{64,128},{128,192},{192,256},{256,320},{320,384},{384,448},... | collective-permute-start | bytes 1572872 | tf_op jit(solution)/shard_map/vectors_along_z/ppermute | solution.py:155
  41.2 0.8 copy-start.8
  42.0 19.0 %collective-permute-start.6 = (f32[48,4096]{1,0:T(8,128)S(1)}, f32[48,4096]{1,0:T(8,128)S(1)}, u32[]{:S(2)}, u32[]{:S(2)}) collective-permute-start(f32[48,4096]{1,0:T(8,128)S(1)} %get-tuple-element.35), channel_id=1, source_target_pairs={{0,48},{16,0},{32,16},{48,32},{1,49},{17,1},{33,17},{49,33},{2,50}... | collective-permute-start | bytes 2359304 | tf_op jit(solution)/shard_map/basis_along_y/ppermute | solution.py:129
  48.5 12.7 %collective-permute-start.5 = (f32[512,256]{1,0:T(8,128)S(1)}, f32[512,256]{1,0:T(8,128)S(1)}, u32[]{:S(2)}, u32[]{:S(2)}) collective-permute-start(f32[512,256]{1,0:T(8,128)S(1)} %collective-permute-done.3.refs_9_), channel_id=1, source_target_pairs={{64,0},{128,64},{192,128},{256,192},{320,256},{384,320},{448,384},... | collective-permute-start | bytes 1572872 | tf_op jit(solution)/shard_map/vectors_along_z/ppermute | solution.py:156
  50.5 12.7 %collective-permute-start.12 = (f32[512,256]{1,0:T(8,128)S(1)}, f32[512,256]{1,0:T(8,128)S(1)}, u32[]{:S(2)}, u32[]{:S(2)}) collective-permute-start(f32[512,256]{1,0:T(8,128)S(1)} %collective-permute-done.11.refs_4_), channel_id=1, source_target_pairs={{0,64},{64,128},{128,192},{192,256},{256,320},{320,384},{384,448},... | collective-permute-start | bytes 1572872 | tf_op jit(solution)/shard_map/vectors_along_z/ppermute | solution.py:155
  61.1 12.1 %collective-permute-start.7 = (f32[512,256]{1,0:T(8,128)S(1)}, f32[512,256]{1,0:T(8,128)S(1)}, u32[]{:S(2)}, u32[]{:S(2)}) collective-permute-start(f32[512,256]{1,0:T(8,128)S(1)} %collective-permute-done.5.refs_9_), channel_id=1, source_target_pairs={{64,0},{128,64},{192,128},{256,192},{320,256},{384,320},{448,384},... | collective-permute-start | bytes 1572872 | tf_op jit(solution)/shard_map/vectors_along_z/ppermute | solution.py:156
  63.2 12.1 %collective-permute-start.13 = (f32[512,256]{1,0:T(8,128)S(1)}, f32[512,256]{1,0:T(8,128)S(1)}, u32[]{:S(2)}, u32[]{:S(2)}) collective-permute-start(f32[512,256]{1,0:T(8,128)S(1)} %collective-permute-done.12.refs_4_), channel_id=1, source_target_pairs={{0,64},{64,128},{128,192},{192,256},{256,320},{320,384},{384,448},... | collective-permute-start | bytes 1572872 | tf_op jit(solution)/shard_map/vectors_along_z/ppermute | solution.py:155
  68.4 18.1 %collective-permute-start.9 = (f32[48,4096]{1,0:T(8,128)S(1)}, f32[48,4096]{1,0:T(8,128)S(1)}, u32[]{:S(2)}, u32[]{:S(2)}) collective-permute-start(f32[48,4096]{1,0:T(8,128)S(1)} %get-tuple-element.39), channel_id=1, source_target_pairs={{0,32},{16,48},{32,0},{48,16},{1,33},{17,49},{33,1},{49,17},{2,34}... | collective-permute-start | bytes 2359304 | tf_op jit(solution)/shard_map/basis_along_y/ppermute | solution.py:129
  73.2 13.2 %collective-permute-start.8 = (f32[512,256]{1,0:T(8,128)S(1)}, f32[512,256]{1,0:T(8,128)}, u32[]{:S(2)}, u32[]{:S(2)}) collective-permute-start(f32[512,256]{1,0:T(8,128)S(1)} %collective-permute-done.7.refs_9_), channel_id=1, source_target_pairs={{64,0},{128,64},{192,128},{256,192},{320,256},{384,320},{448,384},... | collective-permute-start | bytes 1572872 | tf_op jit(solution)/shard_map/vectors_along_z/ppermute | solution.py:156
  74.5 0.8 copy-start.18
  75.3 12.4 %collective-permute-start.14 = (f32[512,256]{1,0:T(8,128)S(1)}, f32[512,256]{1,0:T(8,128)}, u32[]{:S(2)}, u32[]{:S(2)}) collective-permute-start(f32[512,256]{1,0:T(8,128)S(1)} %collective-permute-done.13.refs_4_), channel_id=1, source_target_pairs={{0,64},{64,128},{128,192},{192,256},{256,320},{320,384},{384,448},... | collective-permute-start | bytes 1572872 | tf_op jit(solution)/shard_map/vectors_along_z/ppermute | solution.py:155
  86.5 17.4 %collective-permute-start.16 = (f32[512,256]{1,0:T(8,128)}, f32[512,256]{1,0:T(8,128)}, u32[]{:S(2)}, u32[]{:S(2)}) collective-permute-start(f32[512,256]{1,0:T(8,128)} %collective-permute-done.8.refs_9_), channel_id=1, source_target_pairs={{64,0},{128,64},{192,128},{256,192},{320,256},{384,320},{448,384},... | collective-permute-start | bytes 1572872 | tf_op jit(solution)/shard_map/vectors_along_z/ppermute | solution.py:156
  87.8 16.1 %collective-permute-start.15 = (f32[512,256]{1,0:T(8,128)}, f32[512,256]{1,0:T(8,128)}, u32[]{:S(2)}, u32[]{:S(2)}) collective-permute-start(f32[512,256]{1,0:T(8,128)} %collective-permute-done.14.refs_4_), channel_id=1, source_target_pairs={{0,64},{64,128},{128,192},{192,256},{256,320},{320,384},{384,448},... | collective-permute-start | bytes 1572872 | tf_op jit(solution)/shard_map/vectors_along_z/ppermute | solution.py:155
  93.6 1.0 copy-start.1
  94.7 1.0 copy-start.3
  94.7 1.2 copy-start.5
  95.9 1.0 copy-start.7
  95.9 1.2 copy-start.9
  97.1 1.0 copy-start.11
  97.1 1.2 copy-start.13
  98.3 1.0 copy-start.15
  98.3 1.2 copy-start.17
  99.5 1.0 copy-start.19
  99.5 1.2 copy-start.21
  129.3 13.2 %collective-permute-start.17 = (f32[24,128]{1,0:T(8,128)S(1)}, f32[24,128]{1,0:T(8,128)S(1)}, u32[]{:S(2)}, u32[]{:S(2)}) collective-permute-start(f32[24,128]{1,0:T(8,128)S(1)} %reduce_sum.9), channel_id=1, source_target_pairs={{0,2},{2,0},{1,3},{3,1},{4,6},{6,4},{5,7},{7,5},{8,10},{10,8},{9,1... | collective-permute-start | bytes 36872 | tf_op jit(solution)/shard_map/sum_over_columns/ppermute | solution.py:129
  (8 other events, 6.3 us)

commit v5 on v4

--- a/solution.py
+++ b/solution.py
@@ -46,19 +46,20 @@
     return dot(a_high, b_high) + (dot(a_high, b_low) + dot(a_low, b_high))
 
 
-def add_kernel(offsets, first, last, info, *refs):
+def add_kernel(sources, first, last, info, *refs):
     total = refs[-1]
     out = refs[-2] if last else total
     if first:
         total[...] = jnp.zeros_like(total)
     else:
-        total[...] = refs[len(offsets) * (Y + 1)][...]
+        total[...] = refs[len(sources) * (Y + 1)][...]
     split, z, y, col = (info[i] for i in range(4))
-    for i, off in enumerate(offsets):
+    for i, source in enumerate(sources):
         basis, vec = refs[i * (Y + 1) : i * (Y + 1) + Y], refs[i * (Y + 1) + Y]
         chunk = vec.shape[0]
-        valid = (z + off >= 0) & (z + off < Z)
-        start = ((col * Z + z + off) * Y + y) * chunk
+        at = source(z)
+        valid = (at >= 0) & (at < Z)
+        start = ((col * Z + at) * Y + y) * chunk
         one_side = (start + chunk <= split) | (start >= split)
 
         @pl.when(valid & one_side)
@@ -93,12 +94,12 @@
 def add_chunks(info, basis, pieces, total, last=False):
     rows, chunk, cols = basis[0].shape[0], pieces[0][0].shape[0], pieces[0][0].shape[1]
     specs, args = [], []
-    for vec, off in pieces:
-        specs += [
-            pl.BlockSpec(
-                (rows, chunk), functools.partial(lambda off, g, s: (0, jnp.clip(s[1] + off, 0, Z - 1)), off)
-            )
-        ] * Y
+    for vec, source in pieces:
+
+        def index(g, s, source=source):
+            return 0, jnp.clip(source(s[1]), 0, Z - 1)
+
+        specs += [pl.BlockSpec((rows, chunk), index)] * Y
         specs.append(pl.BlockSpec((chunk, cols), lambda g, s: (0, 0)))
         args += [*basis, vec]
     shape = (2, Y * rows, cols)
@@ -109,7 +110,7 @@
     out = (Y * X * 2, rows // 2, cols // 2) if last else shape
     flops = len(pieces) * 6 * Y * rows * chunk * cols
     return pl.pallas_call(
-        functools.partial(add_kernel, [off for _, off in pieces], total is None, last),
+        functools.partial(add_kernel, [source for _, source in pieces], total is None, last),
         out_shape=jax.ShapeDtypeStruct(out, F32),
         grid_spec=pltpu.PrefetchScalarGridSpec(
             num_scalar_prefetch=1,
@@ -135,30 +136,46 @@
     at = {axis: lax.axis_index(axis) for axis in AXES}
     col = (at["x"] * 2 + at["half"]) * 2 + at["core"]
     info = jnp.stack([split_at[0], at["z"], at["y"], col])
-    up = [(i, i + 1) for i in range(Z - 1)]
-    down = [(i + 1, i) for i in range(Z - 1)]
+    mid = Z // 2
+
+    def near(off):
+        return lambda z: z + off
+
+    def far(step):
+        return lambda z: jnp.where(z < mid, z + step, z - step)
 
     with jax.named_scope("basis_by_y"):
         packed = pack(slab, chunk)
-    below, above = [vectors], [vectors]
+    below, above, beyond = vectors, vectors, None
     basis = [packed[0], None, None, None]
+    pieces = [(vectors, near(0))]
     for step in range(1, Z):
-        if step == 2:
-            below[-1], above[-1], packed = lax.optimization_barrier((below[-1], above[-1], packed))
-        ready = {4: (1,), 5: (3,), 7: (2,)}.get(step, ())
+        ready = {3: (1,), 4: (3,), 6: (2,)}.get(step, ())
         for k in ready:
             with jax.named_scope("basis_along_y"):
                 basis[k] = shift(packed[k], "y", Y, k)
-        if ready:
-            above[-1], basis = lax.optimization_barrier((above[-1], basis))
+        if step == mid + 1:
+            beyond = jnp.where(at["z"] < mid, above, below)
+        if step == 2:
+            above, packed = lax.optimization_barrier((above, packed))
+        if ready and beyond is None:
+            above, basis = lax.optimization_barrier((above, basis))
+        elif ready:
+            beyond, basis = lax.optimization_barrier((beyond, basis))
+        up = [(i, i + 1) for i in range(step - 1, Z - 1)]
+        down = [(i + 1, i) for i in range(Z - step)]
         with jax.named_scope("vectors_along_z"):
-            below.append(lax.ppermute(below[-1], "z", up))
-            above.append(lax.ppermute(above[-1], "z", down))
+            if step <= mid:
+                below, above = lax.ppermute(below, "z", up), lax.ppermute(above, "z", down)
+                pieces += [(below, near(-step)), (above, near(step))]
+            else:
+                beyond = lax.ppermute(beyond, "z", up + down)
+                pieces.append((beyond, far(step)))
 
-    total = add_chunks(info, basis, [(vectors, 0)], None)
-    for step in range(1, Z):
-        pieces = [(below[step], -step), (above[step], step)]
-        total = add_chunks(info, basis, pieces, total, step == Z - 1)
+    total = None
+    for n, m in ((0, 3), (3, 5), (5, 7), (7, 9), (9, 11)):
+        total = add_chunks(info, basis, pieces[n:m], total)
+    total = add_chunks(info, basis, pieces[11:], total, last=True)
 
     with jax.named_scope("sum_over_columns"):
         got = lax.all_to_all(total, ("y", "x", "core"), 0, 0, tiled=True)

time: 146 us -> 145 us (level)
  starting transfers between devices: 68.7 us -> 45.5 us
  waiting for transfers between devices: 27.2 us -> 50.2 us
  local copies, waits for them, and re-layouts: 12.6 us -> 10.6 us
    ppermute x14 -> x11, waiting for transfers between devices: 14.4 us -> 42.5 us  [the longest x4 27.8 us: local(): lax.ppermute(above, 'z', down)]
    ppermute x14 -> x11, starting transfers between devices: 45.4 us -> 17.7 us  [the longest x4 8.7 us: local(): lax.ppermute(below, 'z', up)]
    ppermute x4, waiting for transfers between devices: 12.8 us -> 7.74 us  [shift(): return lax.ppermute(a, axis, [(i, (i + by) % size) for i in range(size)])]
    ppermute x4, starting transfers between devices: 23.3 us -> 27.8 us  [shift(): return lax.ppermute(a, axis, [(i, (i + by) % size) for i in range(size)])]
    unnamed x44 -> x26, local copies, waits for them, and re-layouts: 11.9 us -> 9.87 us
    pallas_call x8 -> x6, Pallas kernels: 10.3 us -> 11.1 us  [add_chunks(): pl.pallas_call(functools.partial(add_kernel, [source for _, source in pie...]
  transfers between devices with their start and end apart: 18 -> 15, of which waited for: 8 -> 9; matrix products, arithmetic and copies ran while one was open for 0% -> 1% of each run, Pallas kernels for 6% -> 6%
where the time goes in v5:
time: 145 us; the launch traced here: 143 us
  waiting for transfers between devices  50.2 us (35%)
  starting transfers between devices  45.5 us (31%)
  blocking collectives  22.7 us (16%)
  Pallas kernels  11.3 us (8%)
  local copies, waits for them, and re-layouts  10.6 us (7%)
    ppermute x4, starting transfers between devices, shift(): return lax.ppermute(a, axis, [(i, (i + by) % size) for i in range(size)])  27.8 us
    ppermute x4, waiting for transfers between devices, local(): lax.ppermute(above, 'z', down)  27.8 us
    all_to_all x1, blocking collectives, local(): got = lax.all_to_all(total, ('y', 'x', 'core'), 0, 0, tiled=True)  22.7 us
    ppermute x3, waiting for transfers between devices, local(): beyond = lax.ppermute(beyond, 'z', up + down)  14.7 us
    pallas_call x6, Pallas kernels, add_chunks(): pl.pallas_call(functools.partial(add_kernel, [source for _, source in pie...  11.1 us
    unnamed x26, local copies, waits for them, and re-layouts  9.87 us
    ppermute x4, starting transfers between devices, local(): lax.ppermute(below, 'z', up)  8.7 us
    ppermute x4, waiting for transfers between devices, shift(): return lax.ppermute(a, axis, [(i, (i + by) % size) for i in range(size)])  7.74 us
  transfers between devices with their start and end apart: 15, of which 9 were waited for; matrix products, arithmetic and copies ran while one was open for 1% of the time, Pallas kernels for 6%

profile of v5, /device:TPU:1, one launch (start us, length us, event | category | flops | bytes accessed | tf_op | source)
XLA Modules:
  0.0 142.7 jit_solution(519459509798814105)
XLA Ops:
  0.0 1.3 collective-permute-start
  1.3 5.0 %collective-permute-start.6 = (f32[512,256]{1,0:T(8,128)}, f32[512,256]{1,0:T(8,128)S(1)}, u32[]{:S(2)}, u32[]{:S(2)}) collective-permute-start(f32[512,256]{1,0:T(8,128)} %refs_4_.1), channel_id=1, source_target_pairs={{0,64},{64,128},{128,192},{192,256},{256,320},{320,384},{384,448},... | collective-permute-start | bytes 1572872 | tf_op jit(solution)/shard_map/vectors_along_z/ppermute | solution.py:169
  6.3 1.9 %copy-done = f32[48,16384]{1,0:T(8,128)S(1)} copy-done((f32[48,16384]{1,0:T(8,128)S(1)}, f32[48,16384]{1,0:T(8,128)}, u32[]{:S(2)}) %copy-start) | copy-done | bytes 3145752
  9.3 1.8 %collective-permute-done.refs_14_ = f32[512,256]{1,0:T(8,128)S(1)} collective-permute-done((f32[512,256]{1,0:T(8,128)}, f32[512,256]{1,0:T(8,128)S(1)}, u32[]{:S(2)}, u32[]{:S(2)}) %collective-permute-start) | collective-permute-done | bytes 524320 | tf_op jit(solution)/shard_map/vectors_along_z/ppermute | solution.py:169
  11.1 8.2 %collective-permute-start.2 = (f32[48,4096]{1,0:T(8,128)S(1)}, f32[48,4096]{1,0:T(8,128)S(1)}, u32[]{:S(2)}, u32[]{:S(2)}) collective-permute-start(f32[48,4096]{1,0:T(8,128)S(1)} %get-tuple-element.30), channel_id=1, source_target_pairs={{0,16},{16,32},{32,48},{48,0},{1,17},{17,33},{33,49},{49,1},{2,18}... | collective-permute-start | bytes 2359304 | tf_op jit(solution)/shard_map/basis_along_y/ppermute | solution.py:130
  20.8 1.3 collective-permute-start.1
  22.9 3.3 %collective-permute-start.4 = (f32[48,4096]{1,0:T(8,128)S(1)}, f32[48,4096]{1,0:T(8,128)S(1)}, u32[]{:S(2)}, u32[]{:S(2)}) collective-permute-start(f32[48,4096]{1,0:T(8,128)S(1)} %get-tuple-element.34), channel_id=1, source_target_pairs={{0,48},{16,0},{32,16},{48,32},{1,49},{17,1},{33,17},{49,33},{2,50}... | collective-permute-start | bytes 2359304 | tf_op jit(solution)/shard_map/basis_along_y/ppermute | solution.py:130
  26.3 1.5 %collective-permute-start.8 = (f32[512,256]{1,0:T(8,128)S(1)}, f32[512,256]{1,0:T(8,128)}, u32[]{:S(2)}, u32[]{:S(2)}) collective-permute-start(f32[512,256]{1,0:T(8,128)S(1)} %collective-permute-done.7.refs_4_), channel_id=1, source_target_pairs={{128,192},{192,256},{256,320},{320,384},{384,448},{129,193},{193,2... | collective-permute-start | bytes 1572872 | tf_op jit(solution)/shard_map/vectors_along_z/ppermute | solution.py:169
  28.6 9.0 %collective-permute-done.1.refs_9_ = f32[512,256]{1,0:T(8,128)S(1)} collective-permute-done((f32[512,256]{1,0:T(8,128)S(1)}, f32[512,256]{1,0:T(8,128)S(1)}, u32[]{:S(2)}, u32[]{:S(2)}) %collective-permute-start.1) | collective-permute-done | bytes 524320 | tf_op jit(solution)/shard_map/vectors_along_z/ppermute | solution.py:169
  37.6 1.3 collective-permute-start.3
  39.7 1.5 %collective-permute-start.9 = (f32[512,256]{1,0:T(8,128)}, f32[512,256]{1,0:T(8,128)}, u32[]{:S(2)}, u32[]{:S(2)}) collective-permute-start(f32[512,256]{1,0:T(8,128)} %collective-permute-done.8.refs_4_), channel_id=1, source_target_pairs={{192,256},{256,320},{320,384},{384,448},{193,257},{257,321},{321,3... | collective-permute-start | bytes 1572872 | tf_op jit(solution)/shard_map/vectors_along_z/ppermute | solution.py:169
  42.2 9.9 %collective-permute-done.3.refs_9_ = f32[512,256]{1,0:T(8,128)} collective-permute-done((f32[512,256]{1,0:T(8,128)S(1)}, f32[512,256]{1,0:T(8,128)}, u32[]{:S(2)}, u32[]{:S(2)}) %collective-permute-start.3) | collective-permute-done | bytes 524320 | tf_op jit(solution)/shard_map/vectors_along_z/ppermute | solution.py:169
  52.1 1.3 collective-permute-start.5
  53.4 4.5 %collective-permute-start.11 = (f32[48,4096]{1,0:T(8,128)}, f32[48,4096]{1,0:T(8,128)S(1)}, u32[]{:S(2)}, u32[]{:S(2)}) collective-permute-start(f32[48,4096]{1,0:T(8,128)} %copy-done.12), channel_id=1, source_target_pairs={{0,32},{16,48},{32,0},{48,16},{1,33},{17,49},{33,1},{49,17},{2,34}... | collective-permute-start | bytes 2359304 | tf_op jit(solution)/shard_map/basis_along_y/ppermute | solution.py:130
  57.9 7.1 %collective-permute-done.5.refs_9_ = f32[512,256]{1,0:T(8,128)} collective-permute-done((f32[512,256]{1,0:T(8,128)}, f32[512,256]{1,0:T(8,128)}, u32[]{:S(2)}, u32[]{:S(2)}) %collective-permute-start.5) | collective-permute-done | bytes 524320 | tf_op jit(solution)/shard_map/vectors_along_z/ppermute | solution.py:169
  65.1 1.1 broadcast_select_fusion
  66.2 1.3 collective-permute-start.10
  67.5 5.4 %collective-permute-done.11.refs_2_.refs_7_.refs_12_ = f32[48,4096]{1,0:T(8,128)S(1)} collective-permute-done((f32[48,4096]{1,0:T(8,128)}, f32[48,4096]{1,0:T(8,128)S(1)}, u32[]{:S(2)}, u32[]{:S(2)}) %collective-permute-start.11) | collective-permute-done | bytes 786464 | tf_op jit(solution)/shard_map/basis_along_y/ppermute | solution.py:130
  72.8 5.4 %collective-permute-done.10.refs_4_ = f32[512,256]{1,0:T(8,128)S(1)} collective-permute-done((f32[512,256]{1,0:T(8,128)S(1)}, f32[512,256]{1,0:T(8,128)S(1)}, u32[]{:S(2)}, u32[]{:S(2)}) %collective-permute-start.10) | collective-permute-done | bytes 524320 | tf_op jit(solution)/shard_map/vectors_along_z/ppermute | solution.py:172
  78.2 1.3 collective-permute-start.12
  80.3 9.3 %collective-permute-done.12.refs_9_ = f32[512,256]{1,0:T(8,128)} collective-permute-done((f32[512,256]{1,0:T(8,128)S(1)}, f32[512,256]{1,0:T(8,128)}, u32[]{:S(2)}, u32[]{:S(2)}) %collective-permute-start.12) | collective-permute-done | bytes 524320 | tf_op jit(solution)/shard_map/vectors_along_z/ppermute | solution.py:172
  89.6 1.3 collective-permute-start.13
  91.6 1.0 copy-done.1
  92.6 1.0 copy-done.3
  94.7 1.3 add_chunks.6.refs_10_
  97.1 2.2 %add_chunks.8.refs_10_ = f32[2,192,256]{2,1,0:T(8,128)S(1)} custom-call(s32[4]{0:T(128)S(1)} %pad_add_fusion.info, f32[48,4096]{1,0:T(8,128)S(1)} %get-tuple-element.40.refs_0_.refs_5_.refs_10_, f32[48,4096]{1,0:T(8,128)S(1)} %collective-permute-done.2.refs_1_.refs_6_.refs_11_, ...), custom_call_target="tpu_custom_call", output_to_operand_aliasing={{}: (11, {})} | custom-call | flops 301989888 | bytes 4194304 | tf_op jit(solution)/shard_map/add_chunks/pallas_call | solution.py:112
  99.3 2.2 %add_chunks.9.refs_10_ = f32[2,192,256]{2,1,0:T(8,128)S(1)} custom-call(s32[4]{0:T(128)S(1)} %pad_add_fusion.info, f32[48,4096]{1,0:T(8,128)S(1)} %get-tuple-element.40.refs_0_.refs_5_.refs_10_, f32[48,4096]{1,0:T(8,128)S(1)} %collective-permute-done.2.refs_1_.refs_6_.refs_11_, ...), custom_call_target="tpu_custom_call", output_to_operand_aliasing={{}: (11, {})} | custom-call | flops 301989888 | bytes 4194304 | tf_op jit(solution)/shard_map/add_chunks/pallas_call | solution.py:112
  101.4 2.3 %add_chunks.10.refs_5_ = f32[2,192,256]{2,1,0:T(8,128)S(1)} custom-call(s32[4]{0:T(128)S(1)} %pad_add_fusion.info, f32[48,4096]{1,0:T(8,128)S(1)} %get-tuple-element.40.refs_0_.refs_5_.refs_10_, f32[48,4096]{1,0:T(8,128)S(1)} %collective-permute-done.2.refs_1_.refs_6_.refs_11_, ...), custom_call_target="tpu_custom_call", output_to_operand_aliasing={{}: (11, {})} | custom-call | flops 301989888 | bytes 4194304 | tf_op jit(solution)/shard_map/add_chunks/pallas_call | solution.py:112
  103.8 2.1 %add_chunks.11 = f32[32,24,128]{2,1,0:T(8,128)S(1)} custom-call(s32[4]{0:T(128)S(1)} %pad_add_fusion.info, f32[48,4096]{1,0:T(8,128)S(1)} %get-tuple-element.40.refs_0_.refs_5_.refs_10_, f32[48,4096]{1,0:T(8,128)S(1)} %collective-permute-done.2.refs_1_.refs_6_.refs_11_, f32[48,4096]{1,0:T(8,128)S(1)} %collective-permute-done.11.refs_2_.refs_7_.refs_12_, ...), custom_call_target="tpu_custom_call" | custom-call | flops 150994944 | bytes 4194304 | tf_op jit(solution)/shard_map/add_chunks/pallas_call | solution.py:112
  105.9 22.7 %all_to_all.5 = f32[32,24,128]{2,1,0:T(8,128)S(1)} all-to-all(f32[32,24,128]{2,1,0:T(8,128)S(1)} %add_chunks.11), channel_id=1, replica_groups=mesh['z'=8,'y'=4,'x'=4,'half'=2,'core'=2] {'y','x','core'}, dimensions={0} | all-to-all | bytes 786432 | tf_op jit(solution)/shard_map/sum_over_columns/all_to_all | solution.py:181
  128.7 11.8 %collective-permute-start.14 = (f32[24,128]{1,0:T(8,128)S(1)}, f32[24,128]{1,0:T(8,128)S(1)}, u32[]{:S(2)}, u32[]{:S(2)}) collective-permute-start(f32[24,128]{1,0:T(8,128)S(1)} %reduce_sum.9), channel_id=1, source_target_pairs={{0,2},{2,0},{1,3},{3,1},{4,6},{6,4},{5,7},{7,5},{8,10},{10,8},{9,1... | collective-permute-start | bytes 36872 | tf_op jit(solution)/shard_map/sum_over_columns/ppermute | solution.py:130
  140.5 1.3 collective-permute-done.14
  (39 shorter events, 9.8 us)
Async XLA Ops:
  0.0 11.1 %collective-permute-start = (f32[512,256]{1,0:T(8,128)}, f32[512,256]{1,0:T(8,128)S(1)}, u32[]{:S(2)}, u32[]{:S(2)}) collective-permute-start(f32[512,256]{1,0:T(8,128)} %refs_4_.1), channel_id=1, source_target_pairs={{64,0},{128,64},{192,128},{256,192},{320,256},{384,320},{448,384},... | collective-permute-start | bytes 1572872 | tf_op jit(solution)/shard_map/vectors_along_z/ppermute | solution.py:169
  1.3 18.0 %collective-permute-start.6 = (f32[512,256]{1,0:T(8,128)}, f32[512,256]{1,0:T(8,128)S(1)}, u32[]{:S(2)}, u32[]{:S(2)}) collective-permute-start(f32[512,256]{1,0:T(8,128)} %refs_4_.1), channel_id=1, source_target_pairs={{0,64},{64,128},{128,192},{192,256},{256,320},{320,384},{384,448},... | collective-permute-start | bytes 1572872 | tf_op jit(solution)/shard_map/vectors_along_z/ppermute | solution.py:169
  6.3 1.9 %copy-start = (f32[48,16384]{1,0:T(8,128)S(1)}, f32[48,16384]{1,0:T(8,128)}, u32[]{:S(2)}) copy-start(f32[48,16384]{1,0:T(8,128)} %slab.1) | copy-start | bytes 9437188
  8.4 0.9 copy-start.12
  11.1 26.4 %collective-permute-start.2 = (f32[48,4096]{1,0:T(8,128)S(1)}, f32[48,4096]{1,0:T(8,128)S(1)}, u32[]{:S(2)}, u32[]{:S(2)}) collective-permute-start(f32[48,4096]{1,0:T(8,128)S(1)} %get-tuple-element.30), channel_id=1, source_target_pairs={{0,16},{16,32},{32,48},{48,0},{1,17},{17,33},{33,49},{49,1},{2,18}... | collective-permute-start | bytes 2359304 | tf_op jit(solution)/shard_map/basis_along_y/ppermute | solution.py:130
  19.3 6.9 %collective-permute-start.7 = (f32[512,256]{1,0:T(8,128)S(1)}, f32[512,256]{1,0:T(8,128)S(1)}, u32[]{:S(2)}, u32[]{:S(2)}) collective-permute-start(f32[512,256]{1,0:T(8,128)S(1)} %collective-permute-done.6.refs_9_), channel_id=1, source_target_pairs={{64,128},{128,192},{192,256},{256,320},{320,384},{384,448},{65,129... | collective-permute-start | bytes 1572872 | tf_op jit(solution)/shard_map/vectors_along_z/ppermute | solution.py:169
  20.0 0.8 copy-start.4
  20.8 16.7 %collective-permute-start.1 = (f32[512,256]{1,0:T(8,128)S(1)}, f32[512,256]{1,0:T(8,128)S(1)}, u32[]{:S(2)}, u32[]{:S(2)}) collective-permute-start(f32[512,256]{1,0:T(8,128)S(1)} %collective-permute-done.refs_14_), channel_id=1, source_target_pairs={{64,0},{128,64},{192,128},{256,192},{320,256},{384,320},{65,1},{12... | collective-permute-start | bytes 1572872 | tf_op jit(solution)/shard_map/vectors_along_z/ppermute | solution.py:169
  22.1 0.8 copy-start.2
  22.9 19.3 %collective-permute-start.4 = (f32[48,4096]{1,0:T(8,128)S(1)}, f32[48,4096]{1,0:T(8,128)S(1)}, u32[]{:S(2)}, u32[]{:S(2)}) collective-permute-start(f32[48,4096]{1,0:T(8,128)S(1)} %get-tuple-element.34), channel_id=1, source_target_pairs={{0,48},{16,0},{32,16},{48,32},{1,49},{17,1},{33,17},{49,33},{2,50}... | collective-permute-start | bytes 2359304 | tf_op jit(solution)/shard_map/basis_along_y/ppermute | solution.py:130
  26.3 13.4 %collective-permute-start.8 = (f32[512,256]{1,0:T(8,128)S(1)}, f32[512,256]{1,0:T(8,128)}, u32[]{:S(2)}, u32[]{:S(2)}) collective-permute-start(f32[512,256]{1,0:T(8,128)S(1)} %collective-permute-done.7.refs_4_), channel_id=1, source_target_pairs={{128,192},{192,256},{256,320},{320,384},{384,448},{129,193},{193,2... | collective-permute-start | bytes 1572872 | tf_op jit(solution)/shard_map/vectors_along_z/ppermute | solution.py:169
  27.8 0.8 copy-start.6
  37.6 14.5 %collective-permute-start.3 = (f32[512,256]{1,0:T(8,128)S(1)}, f32[512,256]{1,0:T(8,128)}, u32[]{:S(2)}, u32[]{:S(2)}) collective-permute-start(f32[512,256]{1,0:T(8,128)S(1)} %collective-permute-done.1.refs_9_), channel_id=1, source_target_pairs={{64,0},{128,64},{192,128},{256,192},{320,256},{65,1},{129,65},{193... | collective-permute-start | bytes 1572872 | tf_op jit(solution)/shard_map/vectors_along_z/ppermute | solution.py:169
  38.9 0.8 copy-start.8
  39.7 18.2 %collective-permute-start.9 = (f32[512,256]{1,0:T(8,128)}, f32[512,256]{1,0:T(8,128)}, u32[]{:S(2)}, u32[]{:S(2)}) collective-permute-start(f32[512,256]{1,0:T(8,128)} %collective-permute-done.8.refs_4_), channel_id=1, source_target_pairs={{192,256},{256,320},{320,384},{384,448},{193,257},{257,321},{321,3... | collective-permute-start | bytes 1572872 | tf_op jit(solution)/shard_map/vectors_along_z/ppermute | solution.py:169
  52.1 13.0 %collective-permute-start.5 = (f32[512,256]{1,0:T(8,128)}, f32[512,256]{1,0:T(8,128)}, u32[]{:S(2)}, u32[]{:S(2)}) collective-permute-start(f32[512,256]{1,0:T(8,128)} %collective-permute-done.3.refs_9_), channel_id=1, source_target_pairs={{64,0},{128,64},{192,128},{256,192},{65,1},{129,65},{193,129},{257... | collective-permute-start | bytes 1572872 | tf_op jit(solution)/shard_map/vectors_along_z/ppermute | solution.py:169
  53.4 19.5 %collective-permute-start.11 = (f32[48,4096]{1,0:T(8,128)}, f32[48,4096]{1,0:T(8,128)S(1)}, u32[]{:S(2)}, u32[]{:S(2)}) collective-permute-start(f32[48,4096]{1,0:T(8,128)} %copy-done.12), channel_id=1, source_target_pairs={{0,32},{16,48},{32,0},{48,16},{1,33},{17,49},{33,1},{49,17},{2,34}... | collective-permute-start | bytes 2359304 | tf_op jit(solution)/shard_map/basis_along_y/ppermute | solution.py:130
  66.2 12.1 %collective-permute-start.10 = (f32[512,256]{1,0:T(8,128)S(1)}, f32[512,256]{1,0:T(8,128)S(1)}, u32[]{:S(2)}, u32[]{:S(2)}) collective-permute-start(f32[512,256]{1,0:T(8,128)S(1)} %broadcast_select_fusion), channel_id=1, source_target_pairs={{256,320},{320,384},{384,448},{64,0},{128,64},{192,128},{257,321},... | collective-permute-start | bytes 1572872 | tf_op jit(solution)/shard_map/vectors_along_z/ppermute | solution.py:172
  78.2 11.3 %collective-permute-start.12 = (f32[512,256]{1,0:T(8,128)S(1)}, f32[512,256]{1,0:T(8,128)}, u32[]{:S(2)}, u32[]{:S(2)}) collective-permute-start(f32[512,256]{1,0:T(8,128)S(1)} %collective-permute-done.10.refs_4_), channel_id=1, source_target_pairs={{320,384},{384,448},{64,0},{128,64},{321,385},{385,449},{65,1},{12... | collective-permute-start | bytes 1572872 | tf_op jit(solution)/shard_map/vectors_along_z/ppermute | solution.py:172
  79.5 0.8 copy-start.10
  89.6 14.2 %collective-permute-start.13 = (f32[512,256]{1,0:T(8,128)}, f32[512,256]{1,0:T(8,128)}, u32[]{:S(2)}, u32[]{:S(2)}) collective-permute-start(f32[512,256]{1,0:T(8,128)} %collective-permute-done.12.refs_9_), channel_id=1, source_target_pairs={{384,448},{64,0},{385,449},{65,1},{386,450},{66,2},{387,451},{67,3... | collective-permute-start | bytes 1572872 | tf_op jit(solution)/shard_map/vectors_along_z/ppermute | solution.py:172
  91.6 1.0 copy-start.1
  92.6 1.0 copy-start.3
  93.7 1.0 copy-start.5
  94.7 1.4 copy-start.7
  94.7 1.4 copy-start.9
  99.3 2.2 %copy-start.11 = (f32[512,256]{1,0:T(8,128)S(1)}, f32[512,256]{1,0:T(8,128)}, u32[]{:S(2)}) copy-start(f32[512,256]{1,0:T(8,128)} %copy-done.10) | copy-start | bytes 1572868
  128.7 13.2 %collective-permute-start.14 = (f32[24,128]{1,0:T(8,128)S(1)}, f32[24,128]{1,0:T(8,128)S(1)}, u32[]{:S(2)}, u32[]{:S(2)}) collective-permute-start(f32[24,128]{1,0:T(8,128)S(1)} %reduce_sum.9), channel_id=1, source_target_pairs={{0,2},{2,0},{1,3},{3,1},{4,6},{6,4},{5,7},{7,5},{8,10},{10,8},{9,1... | collective-permute-start | bytes 36872 | tf_op jit(solution)/shard_map/sum_over_columns/ppermute | solution.py:130

commit v6 on v5

--- a/solution.py
+++ b/solution.py
@@ -146,11 +146,11 @@
 
     with jax.named_scope("basis_by_y"):
         packed = pack(slab, chunk)
-    below, above, beyond = vectors, vectors, None
+    below, above, beyond, total = vectors, vectors, None, None
     basis = [packed[0], None, None, None]
     pieces = [(vectors, near(0))]
     for step in range(1, Z):
-        ready = {3: (1,), 4: (3,), 6: (2,)}.get(step, ())
+        ready = {4: (1, 3), 6: (2,)}.get(step, ())
         for k in ready:
             with jax.named_scope("basis_along_y"):
                 basis[k] = shift(packed[k], "y", Y, k)
@@ -162,6 +162,10 @@
             above, basis = lax.optimization_barrier((above, basis))
         elif ready:
             beyond, basis = lax.optimization_barrier((beyond, basis))
+        if step == Z - 1:
+            for n, m in ((0, 3), (3, 5), (5, 7), (7, 9)):
+                total = add_chunks(info, basis, pieces[n:m], total)
+            beyond, total = lax.optimization_barrier((beyond, total))
         up = [(i, i + 1) for i in range(step - 1, Z - 1)]
         down = [(i + 1, i) for i in range(Z - step)]
         with jax.named_scope("vectors_along_z"):
@@ -172,9 +176,7 @@
                 beyond = lax.ppermute(beyond, "z", up + down)
                 pieces.append((beyond, far(step)))
 
-    total = None
-    for n, m in ((0, 3), (3, 5), (5, 7), (7, 9), (9, 11)):
-        total = add_chunks(info, basis, pieces[n:m], total)
+    total = add_chunks(info, basis, pieces[9:11], total)
     total = add_chunks(info, basis, pieces[11:], total, last=True)
 
     with jax.named_scope("sum_over_columns"):

time: 145 us -> 141 us (0.972); the launches traced: 143 us -> 141 us
    ppermute x4, waiting for transfers between devices: 27.8 us -> 16 us  [local(): lax.ppermute(above, 'z', down)]
    ppermute x4, waiting for transfers between devices: 7.74 us -> 13.6 us  [shift(): return lax.ppermute(a, axis, [(i, (i + by) % size) for i in range(size)])]
    ppermute x3, waiting for transfers between devices: 14.7 us -> 20.4 us  [local(): beyond = lax.ppermute(beyond, 'z', up + down)]
    unnamed x26 -> x22, local copies, waits for them, and re-layouts: 9.87 us -> 9.06 us
  transfers between devices with their start and end apart: 15 -> 15, of which waited for: 9 -> 11; matrix products, arithmetic and copies ran while one was open for 1% -> 1% of each run, Pallas kernels for 6% -> 7%
where the time goes in v6:
time: 141 us
  waiting for transfers between devices  50 us (35%)
  starting transfers between devices  45.5 us (32%)
  blocking collectives  22.7 us (16%)
  Pallas kernels  10.4 us (7%)
  local copies, waits for them, and re-layouts  9.83 us (7%)
    ppermute x4, starting transfers between devices, shift(): return lax.ppermute(a, axis, [(i, (i + by) % size) for i in range(size)])  27.9 us
    all_to_all x1, blocking collectives, local(): got = lax.all_to_all(total, ('y', 'x', 'core'), 0, 0, tiled=True)  22.7 us
    ppermute x3, waiting for transfers between devices, local(): beyond = lax.ppermute(beyond, 'z', up + down)  20.4 us
    ppermute x4, waiting for transfers between devices, local(): lax.ppermute(above, 'z', down)  16 us
    ppermute x4, waiting for transfers between devices, shift(): return lax.ppermute(a, axis, [(i, (i + by) % size) for i in range(size)])  13.6 us
    pallas_call x6, Pallas kernels, add_chunks(): pl.pallas_call(functools.partial(add_kernel, [source for _, source in pie...  10.2 us
    unnamed x22, local copies, waits for them, and re-layouts  9.06 us
    ppermute x4, starting transfers between devices, local(): lax.ppermute(below, 'z', up)  8.62 us
  transfers between devices with their start and end apart: 15, of which 11 were waited for; matrix products, arithmetic and copies ran while one was open for 1% of the time, Pallas kernels for 7%

profile of v6, /device:TPU:1, one launch (start us, length us, event | category | flops | bytes accessed | tf_op | source)
XLA Modules:
  0.0 140.6 jit_solution(9816642328803901928)
XLA Ops:
  0.0 1.3 collective-permute-start
  1.3 5.0 %collective-permute-start.6 = (f32[512,256]{1,0:T(8,128)}, f32[512,256]{1,0:T(8,128)S(1)}, u32[]{:S(2)}, u32[]{:S(2)}) collective-permute-start(f32[512,256]{1,0:T(8,128)} %refs_4_.1), channel_id=1, source_target_pairs={{0,64},{64,128},{128,192},{192,256},{256,320},{320,384},{384,448},... | collective-permute-start | bytes 1572872 | tf_op jit(solution)/shard_map/vectors_along_z/ppermute | solution.py:173
  6.3 1.9 %copy-done = f32[48,16384]{1,0:T(8,128)S(1)} copy-done((f32[48,16384]{1,0:T(8,128)S(1)}, f32[48,16384]{1,0:T(8,128)}, u32[]{:S(2)}) %copy-start) | copy-done | bytes 3145752
  9.3 1.8 %collective-permute-done.refs_14_ = f32[512,256]{1,0:T(8,128)S(1)} collective-permute-done((f32[512,256]{1,0:T(8,128)}, f32[512,256]{1,0:T(8,128)S(1)}, u32[]{:S(2)}, u32[]{:S(2)}) %collective-permute-start) | collective-permute-done | bytes 524320 | tf_op jit(solution)/shard_map/vectors_along_z/ppermute | solution.py:173
  11.1 1.3 collective-permute-start.1
  14.7 8.2 %collective-permute-start.3 = (f32[48,4096]{1,0:T(8,128)S(1)}, f32[48,4096]{1,0:T(8,128)S(1)}, u32[]{:S(2)}, u32[]{:S(2)}) collective-permute-start(f32[48,4096]{1,0:T(8,128)S(1)} %get-tuple-element.29), channel_id=1, source_target_pairs={{0,16},{16,32},{32,48},{48,0},{1,17},{17,33},{33,49},{49,1},{2,18}... | collective-permute-start | bytes 2359304 | tf_op jit(solution)/shard_map/basis_along_y/ppermute | solution.py:130
  22.9 3.4 %collective-permute-start.4 = (f32[48,4096]{1,0:T(8,128)S(1)}, f32[48,4096]{1,0:T(8,128)S(1)}, u32[]{:S(2)}, u32[]{:S(2)}) collective-permute-start(f32[48,4096]{1,0:T(8,128)S(1)} %get-tuple-element.30), channel_id=1, source_target_pairs={{0,48},{16,0},{32,16},{48,32},{1,49},{17,1},{33,17},{49,33},{2,50}... | collective-permute-start | bytes 2359304 | tf_op jit(solution)/shard_map/basis_along_y/ppermute | solution.py:130
  26.2 3.5 %collective-permute-done.1.refs_9_ = f32[512,256]{1,0:T(8,128)S(1)} collective-permute-done((f32[512,256]{1,0:T(8,128)S(1)}, f32[512,256]{1,0:T(8,128)S(1)}, u32[]{:S(2)}, u32[]{:S(2)}) %collective-permute-start.1) | collective-permute-done | bytes 524320 | tf_op jit(solution)/shard_map/vectors_along_z/ppermute | solution.py:173
  29.7 1.3 collective-permute-start.2
  31.8 1.4 %collective-permute-start.8 = (f32[512,256]{1,0:T(8,128)S(1)}, f32[512,256]{1,0:T(8,128)}, u32[]{:S(2)}, u32[]{:S(2)}) collective-permute-start(f32[512,256]{1,0:T(8,128)S(1)} %collective-permute-done.7.refs_4_), channel_id=1, source_target_pairs={{128,192},{192,256},{256,320},{320,384},{384,448},{129,193},{193,2... | collective-permute-start | bytes 1572872 | tf_op jit(solution)/shard_map/vectors_along_z/ppermute | solution.py:173
  34.1 5.8 %collective-permute-done.3.refs_1_.refs_6_.refs_11_ = f32[48,4096]{1,0:T(8,128)S(1)} collective-permute-done((f32[48,4096]{1,0:T(8,128)S(1)}, f32[48,4096]{1,0:T(8,128)S(1)}, u32[]{:S(2)}, u32[]{:S(2)}) %collective-permute-start.3) | collective-permute-done | bytes 786464 | tf_op jit(solution)/shard_map/basis_along_y/ppermute | solution.py:130
  39.9 2.4 %collective-permute-done.4.refs_3_.refs_8_.refs_13_ = f32[48,4096]{1,0:T(8,128)S(1)} collective-permute-done((f32[48,4096]{1,0:T(8,128)S(1)}, f32[48,4096]{1,0:T(8,128)S(1)}, u32[]{:S(2)}, u32[]{:S(2)}) %collective-permute-start.4) | collective-permute-done | bytes 786464 | tf_op jit(solution)/shard_map/basis_along_y/ppermute | solution.py:130
  42.3 1.8 %collective-permute-done.2.refs_9_ = f32[512,256]{1,0:T(8,128)} collective-permute-done((f32[512,256]{1,0:T(8,128)S(1)}, f32[512,256]{1,0:T(8,128)}, u32[]{:S(2)}, u32[]{:S(2)}) %collective-permute-start.2) | collective-permute-done | bytes 524320 | tf_op jit(solution)/shard_map/vectors_along_z/ppermute | solution.py:173
  44.1 1.5 %collective-permute-start.9 = (f32[512,256]{1,0:T(8,128)}, f32[512,256]{1,0:T(8,128)}, u32[]{:S(2)}, u32[]{:S(2)}) collective-permute-start(f32[512,256]{1,0:T(8,128)} %collective-permute-done.8.refs_4_), channel_id=1, source_target_pairs={{192,256},{256,320},{320,384},{384,448},{193,257},{257,321},{321,3... | collective-permute-start | bytes 1572872 | tf_op jit(solution)/shard_map/vectors_along_z/ppermute | solution.py:173
  45.6 1.3 collective-permute-start.5
  46.9 4.8 %collective-permute-start.11 = (f32[48,4096]{1,0:T(8,128)}, f32[48,4096]{1,0:T(8,128)S(1)}, u32[]{:S(2)}, u32[]{:S(2)}) collective-permute-start(f32[48,4096]{1,0:T(8,128)} %copy-done.10), channel_id=1, source_target_pairs={{0,32},{16,48},{32,0},{48,16},{1,33},{17,49},{33,1},{49,17},{2,34}... | collective-permute-start | bytes 2359304 | tf_op jit(solution)/shard_map/basis_along_y/ppermute | solution.py:130
  51.7 8.8 %collective-permute-done.5.refs_9_ = f32[512,256]{1,0:T(8,128)} collective-permute-done((f32[512,256]{1,0:T(8,128)}, f32[512,256]{1,0:T(8,128)}, u32[]{:S(2)}, u32[]{:S(2)}) %collective-permute-start.5) | collective-permute-done | bytes 524320 | tf_op jit(solution)/shard_map/vectors_along_z/ppermute | solution.py:173
  60.6 1.1 broadcast_select_fusion
  61.7 1.3 collective-permute-start.10
  63.0 3.7 %collective-permute-done.11.refs_2_.refs_7_.refs_12_ = f32[48,4096]{1,0:T(8,128)S(1)} collective-permute-done((f32[48,4096]{1,0:T(8,128)}, f32[48,4096]{1,0:T(8,128)S(1)}, u32[]{:S(2)}, u32[]{:S(2)}) %collective-permute-start.11) | collective-permute-done | bytes 786464 | tf_op jit(solution)/shard_map/basis_along_y/ppermute | solution.py:130
  66.7 8.5 %collective-permute-done.10.refs_4_ = f32[512,256]{1,0:T(8,128)} collective-permute-done((f32[512,256]{1,0:T(8,128)S(1)}, f32[512,256]{1,0:T(8,128)}, u32[]{:S(2)}, u32[]{:S(2)}) %collective-permute-start.10) | collective-permute-done | bytes 524320 | tf_op jit(solution)/shard_map/vectors_along_z/ppermute | solution.py:176
  75.2 1.3 collective-permute-start.12
  80.4 1.3 add_chunks.6.refs_10_
  82.8 2.2 %add_chunks.8.refs_10_ = f32[2,192,256]{2,1,0:T(8,128)S(1)} custom-call(s32[4]{0:T(128)S(1)} %pad_add_fusion.info, f32[48,4096]{1,0:T(8,128)S(1)} %get-tuple-element.36.refs_0_.refs_5_.refs_10_, f32[48,4096]{1,0:T(8,128)S(1)} %collective-permute-done.3.refs_1_.refs_6_.refs_11_, ...), custom_call_target="tpu_custom_call", output_to_operand_aliasing={{}: (11, {})} | custom-call | flops 301989888 | bytes 4194304 | tf_op jit(solution)/shard_map/add_chunks/pallas_call | solution.py:112
  84.9 2.2 %add_chunks.9.refs_10_ = f32[2,192,256]{2,1,0:T(8,128)S(1)} custom-call(s32[4]{0:T(128)S(1)} %pad_add_fusion.info, f32[48,4096]{1,0:T(8,128)S(1)} %get-tuple-element.36.refs_0_.refs_5_.refs_10_, f32[48,4096]{1,0:T(8,128)S(1)} %collective-permute-done.3.refs_1_.refs_6_.refs_11_, ...), custom_call_target="tpu_custom_call", output_to_operand_aliasing={{}: (11, {})} | custom-call | flops 301989888 | bytes 4194304 | tf_op jit(solution)/shard_map/add_chunks/pallas_call | solution.py:112
  87.1 3.6 %collective-permute-done.12.refs_9_ = f32[512,256]{1,0:T(8,128)} collective-permute-done((f32[512,256]{1,0:T(8,128)}, f32[512,256]{1,0:T(8,128)}, u32[]{:S(2)}, u32[]{:S(2)}) %collective-permute-start.12) | collective-permute-done | bytes 524320 | tf_op jit(solution)/shard_map/vectors_along_z/ppermute | solution.py:176
  90.7 1.3 collective-permute-start.13
  92.0 2.5 %add_chunks.10.refs_5_ = f32[2,192,256]{2,1,0:T(8,128)S(1)} custom-call(s32[4]{0:T(128)S(1)} %pad_add_fusion.info, f32[48,4096]{1,0:T(8,128)S(1)} %get-tuple-element.36.refs_0_.refs_5_.refs_10_, f32[48,4096]{1,0:T(8,128)S(1)} %collective-permute-done.3.refs_1_.refs_6_.refs_11_, ...), custom_call_target="tpu_custom_call", output_to_operand_aliasing={{}: (11, {})} | custom-call | flops 301989888 | bytes 4194304 | tf_op jit(solution)/shard_map/add_chunks/pallas_call | solution.py:112
  94.4 8.3 %collective-permute-done.13.refs_4_ = f32[512,256]{1,0:T(8,128)S(1)} collective-permute-done((f32[512,256]{1,0:T(8,128)}, f32[512,256]{1,0:T(8,128)S(1)}, u32[]{:S(2)}, u32[]{:S(2)}) %collective-permute-start.13) | collective-permute-done | bytes 524320 | tf_op jit(solution)/shard_map/vectors_along_z/ppermute | solution.py:176
  103.9 22.7 %all_to_all.5 = f32[32,24,128]{2,1,0:T(8,128)S(1)} all-to-all(f32[32,24,128]{2,1,0:T(8,128)S(1)} %add_chunks.11), channel_id=1, replica_groups=mesh['z'=8,'y'=4,'x'=4,'half'=2,'core'=2] {'y','x','core'}, dimensions={0} | all-to-all | bytes 786432 | tf_op jit(solution)/shard_map/sum_over_columns/all_to_all | solution.py:183
  126.6 11.5 %collective-permute-start.14 = (f32[24,128]{1,0:T(8,128)S(1)}, f32[24,128]{1,0:T(8,128)S(1)}, u32[]{:S(2)}, u32[]{:S(2)}) collective-permute-start(f32[24,128]{1,0:T(8,128)S(1)} %reduce_sum.9), channel_id=1, source_target_pairs={{0,2},{2,0},{1,3},{3,1},{4,6},{6,4},{5,7},{7,5},{8,10},{10,8},{9,1... | collective-permute-start | bytes 36872 | tf_op jit(solution)/shard_map/sum_over_columns/ppermute | solution.py:130
  138.2 1.6 %collective-permute-done.14 = f32[24,128]{1,0:T(8,128)S(1)} collective-permute-done((f32[24,128]{1,0:T(8,128)S(1)}, f32[24,128]{1,0:T(8,128)S(1)}, u32[]{:S(2)}, u32[]{:S(2)}) %collective-permute-start.14) | collective-permute-done | bytes 12320 | tf_op jit(solution)/shard_map/sum_over_columns/ppermute | solution.py:130
  (35 shorter events, 11.1 us)
Async XLA Ops:
  0.0 11.1 %collective-permute-start = (f32[512,256]{1,0:T(8,128)}, f32[512,256]{1,0:T(8,128)S(1)}, u32[]{:S(2)}, u32[]{:S(2)}) collective-permute-start(f32[512,256]{1,0:T(8,128)} %refs_4_.1), channel_id=1, source_target_pairs={{64,0},{128,64},{192,128},{256,192},{320,256},{384,320},{448,384},... | collective-permute-start | bytes 1572872 | tf_op jit(solution)/shard_map/vectors_along_z/ppermute | solution.py:173
  1.3 11.9 %collective-permute-start.6 = (f32[512,256]{1,0:T(8,128)}, f32[512,256]{1,0:T(8,128)S(1)}, u32[]{:S(2)}, u32[]{:S(2)}) collective-permute-start(f32[512,256]{1,0:T(8,128)} %refs_4_.1), channel_id=1, source_target_pairs={{0,64},{64,128},{128,192},{192,256},{256,320},{320,384},{384,448},... | collective-permute-start | bytes 1572872 | tf_op jit(solution)/shard_map/vectors_along_z/ppermute | solution.py:173
  6.3 1.9 %copy-start = (f32[48,16384]{1,0:T(8,128)S(1)}, f32[48,16384]{1,0:T(8,128)}, u32[]{:S(2)}) copy-start(f32[48,16384]{1,0:T(8,128)} %slab.1) | copy-start | bytes 9437188
  8.4 0.9 copy-start.10
  11.1 18.6 %collective-permute-start.1 = (f32[512,256]{1,0:T(8,128)S(1)}, f32[512,256]{1,0:T(8,128)S(1)}, u32[]{:S(2)}, u32[]{:S(2)}) collective-permute-start(f32[512,256]{1,0:T(8,128)S(1)} %collective-permute-done.refs_14_), channel_id=1, source_target_pairs={{64,0},{128,64},{192,128},{256,192},{320,256},{384,320},{65,1},{12... | collective-permute-start | bytes 1572872 | tf_op jit(solution)/shard_map/vectors_along_z/ppermute | solution.py:173
  12.4 0.8 copy-start.2
  13.2 18.6 %collective-permute-start.7 = (f32[512,256]{1,0:T(8,128)S(1)}, f32[512,256]{1,0:T(8,128)S(1)}, u32[]{:S(2)}, u32[]{:S(2)}) collective-permute-start(f32[512,256]{1,0:T(8,128)S(1)} %collective-permute-done.6.refs_9_), channel_id=1, source_target_pairs={{64,128},{128,192},{192,256},{256,320},{320,384},{384,448},{65,129... | collective-permute-start | bytes 1572872 | tf_op jit(solution)/shard_map/vectors_along_z/ppermute | solution.py:173
  13.9 0.8 copy-start.4
  14.7 25.2 %collective-permute-start.3 = (f32[48,4096]{1,0:T(8,128)S(1)}, f32[48,4096]{1,0:T(8,128)S(1)}, u32[]{:S(2)}, u32[]{:S(2)}) collective-permute-start(f32[48,4096]{1,0:T(8,128)S(1)} %get-tuple-element.29), channel_id=1, source_target_pairs={{0,16},{16,32},{32,48},{48,0},{1,17},{17,33},{33,49},{49,1},{2,18}... | collective-permute-start | bytes 2359304 | tf_op jit(solution)/shard_map/basis_along_y/ppermute | solution.py:130
  22.9 19.4 %collective-permute-start.4 = (f32[48,4096]{1,0:T(8,128)S(1)}, f32[48,4096]{1,0:T(8,128)S(1)}, u32[]{:S(2)}, u32[]{:S(2)}) collective-permute-start(f32[48,4096]{1,0:T(8,128)S(1)} %get-tuple-element.30), channel_id=1, source_target_pairs={{0,48},{16,0},{32,16},{48,32},{1,49},{17,1},{33,17},{49,33},{2,50}... | collective-permute-start | bytes 2359304 | tf_op jit(solution)/shard_map/basis_along_y/ppermute | solution.py:130
  29.7 14.4 %collective-permute-start.2 = (f32[512,256]{1,0:T(8,128)S(1)}, f32[512,256]{1,0:T(8,128)}, u32[]{:S(2)}, u32[]{:S(2)}) collective-permute-start(f32[512,256]{1,0:T(8,128)S(1)} %collective-permute-done.1.refs_9_), channel_id=1, source_target_pairs={{64,0},{128,64},{192,128},{256,192},{320,256},{65,1},{129,65},{193... | collective-permute-start | bytes 1572872 | tf_op jit(solution)/shard_map/vectors_along_z/ppermute | solution.py:173
  31.0 0.8 copy-start.6
  31.8 12.3 %collective-permute-start.8 = (f32[512,256]{1,0:T(8,128)S(1)}, f32[512,256]{1,0:T(8,128)}, u32[]{:S(2)}, u32[]{:S(2)}) collective-permute-start(f32[512,256]{1,0:T(8,128)S(1)} %collective-permute-done.7.refs_4_), channel_id=1, source_target_pairs={{128,192},{192,256},{256,320},{320,384},{384,448},{129,193},{193,2... | collective-permute-start | bytes 1572872 | tf_op jit(solution)/shard_map/vectors_along_z/ppermute | solution.py:173
  33.3 0.8 copy-start.8
  44.1 7.6 %collective-permute-start.9 = (f32[512,256]{1,0:T(8,128)}, f32[512,256]{1,0:T(8,128)}, u32[]{:S(2)}, u32[]{:S(2)}) collective-permute-start(f32[512,256]{1,0:T(8,128)} %collective-permute-done.8.refs_4_), channel_id=1, source_target_pairs={{192,256},{256,320},{320,384},{384,448},{193,257},{257,321},{321,3... | collective-permute-start | bytes 1572872 | tf_op jit(solution)/shard_map/vectors_along_z/ppermute | solution.py:173
  45.6 15.0 %collective-permute-start.5 = (f32[512,256]{1,0:T(8,128)}, f32[512,256]{1,0:T(8,128)}, u32[]{:S(2)}, u32[]{:S(2)}) collective-permute-start(f32[512,256]{1,0:T(8,128)} %collective-permute-done.2.refs_9_), channel_id=1, source_target_pairs={{64,0},{128,64},{192,128},{256,192},{65,1},{129,65},{193,129},{257... | collective-permute-start | bytes 1572872 | tf_op jit(solution)/shard_map/vectors_along_z/ppermute | solution.py:173
  46.9 19.8 %collective-permute-start.11 = (f32[48,4096]{1,0:T(8,128)}, f32[48,4096]{1,0:T(8,128)S(1)}, u32[]{:S(2)}, u32[]{:S(2)}) collective-permute-start(f32[48,4096]{1,0:T(8,128)} %copy-done.10), channel_id=1, source_target_pairs={{0,32},{16,48},{32,0},{48,16},{1,33},{17,49},{33,1},{49,17},{2,34}... | collective-permute-start | bytes 2359304 | tf_op jit(solution)/shard_map/basis_along_y/ppermute | solution.py:130
  61.7 13.5 %collective-permute-start.10 = (f32[512,256]{1,0:T(8,128)S(1)}, f32[512,256]{1,0:T(8,128)}, u32[]{:S(2)}, u32[]{:S(2)}) collective-permute-start(f32[512,256]{1,0:T(8,128)S(1)} %broadcast_select_fusion), channel_id=1, source_target_pairs={{256,320},{320,384},{384,448},{64,0},{128,64},{192,128},{257,321},... | collective-permute-start | bytes 1572872 | tf_op jit(solution)/shard_map/vectors_along_z/ppermute | solution.py:176
  75.2 15.4 %collective-permute-start.12 = (f32[512,256]{1,0:T(8,128)}, f32[512,256]{1,0:T(8,128)}, u32[]{:S(2)}, u32[]{:S(2)}) collective-permute-start(f32[512,256]{1,0:T(8,128)} %collective-permute-done.10.refs_4_), channel_id=1, source_target_pairs={{320,384},{384,448},{64,0},{128,64},{321,385},{385,449},{65,1},{12... | collective-permute-start | bytes 1572872 | tf_op jit(solution)/shard_map/vectors_along_z/ppermute | solution.py:176
  77.2 1.0 copy-start.1
  78.3 1.0 copy-start.3
  79.3 1.0 copy-start.5
  80.4 1.4 copy-start.7
  80.4 1.4 copy-start.9
  90.7 12.1 %collective-permute-start.13 = (f32[512,256]{1,0:T(8,128)}, f32[512,256]{1,0:T(8,128)S(1)}, u32[]{:S(2)}, u32[]{:S(2)}) collective-permute-start(f32[512,256]{1,0:T(8,128)} %collective-permute-done.12.refs_9_), channel_id=1, source_target_pairs={{384,448},{64,0},{385,449},{65,1},{386,450},{66,2},{387,451},{67,3... | collective-permute-start | bytes 1572872 | tf_op jit(solution)/shard_map/vectors_along_z/ppermute | solution.py:176
  126.6 13.2 %collective-permute-start.14 = (f32[24,128]{1,0:T(8,128)S(1)}, f32[24,128]{1,0:T(8,128)S(1)}, u32[]{:S(2)}, u32[]{:S(2)}) collective-permute-start(f32[24,128]{1,0:T(8,128)S(1)} %reduce_sum.9), channel_id=1, source_target_pairs={{0,2},{2,0},{1,3},{3,1},{4,6},{6,4},{5,7},{7,5},{8,10},{10,8},{9,1... | collective-permute-start | bytes 36872 | tf_op jit(solution)/shard_map/sum_over_columns/ppermute | solution.py:130

commit v7 on v6

v7 whole, which is shorter than its diff:
```python
import functools

import jax
import jax.numpy as jnp
from jax import lax
from jax.experimental import pallas as pl
from jax.experimental.pallas import tpu as pltpu
from jax.sharding import Mesh, PartitionSpec as P

AXES = ("z", "y", "x", "half", "core")
SIZES = (8, 4, 4, 2, 2)
Z, Y, X = SIZES[:3]
PARTS = 2
F32, BF16 = jnp.float32, jnp.bfloat16


def pack_kernel(chunk, slab, *outs):
    y = lax.axis_index("y")
    for k in range(Y):
        to = y ^ k
        for z in range(Z):
            start = pl.multiple_of((z * Y + to) * chunk, chunk)
            outs[k][:, z * chunk : (z + 1) * chunk] = slab[:, pl.ds(start, chunk)]


def pack(slab, chunk):
    rows = slab.shape[0]
    return pl.pallas_call(
        functools.partial(pack_kernel, chunk),
        out_shape=[jax.ShapeDtypeStruct((rows, Z * chunk), F32)] * Y,
        in_specs=[pl.BlockSpec(memory_space=pltpu.VMEM)],
        out_specs=[pl.BlockSpec(memory_space=pltpu.VMEM)] * Y,
        compiler_params=pltpu.CompilerParams(vmem_limit_bytes=14 << 20),
        name="pack_slab",
    )(slab)


def halves(a):
    high = a.astype(BF16)
    return high, (a - high.astype(F32)).astype(BF16)


def product(a, b):
    a_high, a_low = halves(a)
    b_high, b_low = halves(b)
    dot = functools.partial(jnp.dot, preferred_element_type=F32)
    return dot(a_high, b_high) + (dot(a_high, b_low) + dot(a_low, b_high))


def add_kernel(sources, first, last, info, *refs):
    total = refs[-1]
    out, send = refs[-3:-1] if last else (total, None)
    if first:
        total[...] = jnp.zeros_like(total)
    else:
        total[...] = refs[len(sources) * (Y + 1)][...]
    split, z, y, col, core = (info[i] for i in range(5))
    for i, source in enumerate(sources):
        basis, vec = refs[i * (Y + 1) : i * (Y + 1) + Y], refs[i * (Y + 1) + Y]
        source, part, parts = source
        chunk = vec.shape[0]
        at = source(z)
        valid = (at >= 0) & (at < Z)
        start = (((col * Z + at) * Y + y) * parts + part) * chunk
        one_side = (start + chunk <= split) | (start >= split)

        @pl.when(valid & one_side)
        def _():
            lhs = jnp.concatenate([b[...] for b in basis], axis=0)
            side = (start >= split).astype(jnp.int32)
            total[side] += product(lhs, vec[...])

        @pl.when(valid & jnp.logical_not(one_side))
        def _():
            lhs = jnp.concatenate([b[...] for b in basis], axis=0)
            at = start + lax.broadcasted_iota(jnp.int32, lhs.shape, 1)
            left = jnp.where(at < split, lhs, 0.0)
            right = jnp.where(at < split, 0.0, lhs)
            total[0] += product(left, vec[...])
            total[1] += product(right, vec[...])

    if last:
        rows, wide = total.shape[1] // Y, out.shape[2]
        low = lax.broadcasted_iota(jnp.int32, out.shape[1:], 1) % (wide // 2) < wide // 4
        for k in range(Y):
            to = y ^ k
            for x in range(X):
                cols = slice((x % 2) * wide, (x % 2 + 1) * wide)
                top = total[x // 2, k * rows : k * rows + rows // 2, cols]
                bottom = total[x // 2, k * rows + rows // 2 : (k + 1) * rows, cols]
                at = to * X + x
                mine, other = jnp.where(low, top, pltpu.roll(bottom, wide // 4, 1)), jnp.where(low, pltpu.roll(top, wide - wide // 4, 1), bottom)
                out[at] = jnp.where(core == 0, mine, other)
                send[at] = jnp.where(core == 0, other, mine)


def add_chunks(info, basis, pieces, total, last=False):
    rows, cols = basis[0].shape[0], pieces[0][0].shape[1]
    specs, args, sources = [], [], []
    for vec, source, part in pieces:
        chunk = vec.shape[0]
        parts = basis[0].shape[1] // Z // chunk

        def index(g, s, source=source, part=part, parts=parts):
            return 0, jnp.clip(source(s[1]), 0, Z - 1) * parts + part

        sources.append((source, part, parts))
        specs += [pl.BlockSpec((rows, chunk), index)] * Y
        specs.append(pl.BlockSpec((chunk, cols), lambda g, s: (0, 0)))
        args += [*basis, vec]
    shape = (2, Y * rows, cols)
    whole = pl.BlockSpec(shape, lambda g, s: (0, 0, 0))
    if total is not None:
        specs.append(whole)
        args.append(total)
    out = (Y * X, rows // 2, cols // 2) if last else shape
    flops = sum(6 * Y * rows * vec.size for vec, _, _ in pieces)
    return pl.pallas_call(
        functools.partial(add_kernel, sources, total is None, last),
        out_shape=[jax.ShapeDtypeStruct(out, F32)] * 2 if last else jax.ShapeDtypeStruct(out, F32),
        grid_spec=pltpu.PrefetchScalarGridSpec(
            num_scalar_prefetch=1,
            grid=(1,),
            in_specs=specs,
            out_specs=[pl.BlockSpec(out, lambda g, s: (0, 0, 0))] * 2 if last else pl.BlockSpec(out, lambda g, s: (0, 0, 0)),
            scratch_shapes=[pltpu.VMEM(shape, F32)] if last else [],
        ),
        input_output_aliases={} if total is None or last else {len(args): 0},
        compiler_params=pltpu.CompilerParams(vmem_limit_bytes=12 << 20),
        cost_estimate=pl.CostEstimate(flops=flops, bytes_accessed=4 << 20, transcendentals=0),
        name="add_chunks",
    )(info, *args)


def select_kernel(info, even, odd, *outs):
    z = info[1]
    first = (z < Z // 2) == (z % 2 == 0)
    part = outs[0].shape[0]
    for taken, vec in ((first, even), (jnp.logical_not(first), odd)):

        @pl.when(taken)
        def _(vec=vec):
            for i, out in enumerate(outs):
                out[...] = vec[i * part : (i + 1) * part]


def select(info, even, odd):
    vmem = pl.BlockSpec(memory_space=pltpu.VMEM)
    return pl.pallas_call(
        select_kernel,
        out_shape=[jax.ShapeDtypeStruct((even.shape[0] // PARTS, even.shape[1]), F32)] * PARTS,
        in_specs=[pl.BlockSpec(memory_space=pltpu.SMEM), vmem, vmem],
        out_specs=[vmem] * PARTS,
        compiler_params=pltpu.CompilerParams(vmem_limit_bytes=4 << 20),
        name="select",
    )(info, even, odd)


def shift(a, axis, size, by):
    return lax.ppermute(a, axis, [(i, (i + by) % size) for i in range(size)])


def local(split_at, slab, vectors):
    chunk = vectors.shape[0]
    rows = slab.shape[0]
    at = {axis: lax.axis_index(axis) for axis in AXES}
    col = (at["x"] * 2 + at["half"]) * 2 + at["core"]
    info = jnp.stack([split_at[0], at["z"], at["y"], col, at["core"]])
    mid = Z // 2

    def turn(off):
        return lambda z: jnp.where(z % 2 == 0, z + off, z - off)

    def far(step):
        return lambda z: jnp.where(z < mid, z + step, z - step)

    with jax.named_scope("basis_by_y"):
        slab, info = lax.optimization_barrier((slab, info))
        packed = pack(slab, chunk)
    even, odd, beyond, total = vectors, vectors, None, None
    basis = [packed[0], None, None, None]
    pieces = [(vectors, lambda z: z, 0)]
    for step in range(1, Z):
        ready = {4: (1, 3), 6: (2,)}.get(step, ())
        for k in ready:
            with jax.named_scope("basis_along_y"):
                basis[k] = lax.ppermute(packed[k], "y", [(i, i ^ k) for i in range(Y)])
        if step == mid + 1:
            beyond = list(select(info, even, odd))
        if step == 2:
            odd, packed = lax.optimization_barrier((odd, packed))
        if ready and beyond is None:
            even, basis = lax.optimization_barrier((even, basis))
        elif ready:
            beyond[0], basis = lax.optimization_barrier((beyond[0], basis))
        if step == Z - 1:
            for n, m in ((0, 3), (3, 5), (5, 7), (7, 9)):
                total = add_chunks(info, basis, pieces[n:m], total)
            beyond[0], total = lax.optimization_barrier((beyond[0], total))
        up = [(i, i + 1) for i in range(step - 1, Z - 1)]
        down = [(i + 1, i) for i in range(Z - step)]
        with jax.named_scope("vectors_along_z"):
            if step <= mid:
                pairs = [[p for p in up + down if min(p) % 2 == parity] for parity in range(2)]
                even, odd = lax.ppermute(odd, "z", pairs[0]), lax.ppermute(even, "z", pairs[1])
                pieces += [(even, turn(step), 0), (odd, turn(-step), 0)]
            else:
                beyond = [lax.ppermute(b, "z", up + down) for b in beyond]
                pieces += [(b, far(step), i) for i, b in enumerate(beyond)]

    total = add_chunks(info, basis, pieces[9:-1], total)
    total = add_chunks(info, basis, pieces[-1:], total, last=True)

    with jax.named_scope("sum_over_columns"):
        mine, other = total
        mine = mine + shift(other, "core", 2, 1)
        got = lax.all_to_all(mine, ("y", "x"), 0, 0, tiled=True)
        mine = jnp.sum(got, axis=0)
        mine = mine + shift(mine, "half", 2, 1)
        wide = mine.shape[1] // 4
        mine = lax.dynamic_slice(mine, (0, at["half"] * 2 * wide), (rows // 2, 2 * wide))
        return jnp.concatenate([mine[:, :wide], mine[:, wide:]], axis=0)


def solution(mesh):
    split_mesh = Mesh(mesh.devices.reshape(SIZES), AXES)
    placed = (P(), P(("z", "y"), ("x", "half", "core")), P(("x", "half", "core", "z", "y"), None))
    return jax.shard_map(
        local, mesh=split_mesh, in_specs=placed,
        out_specs=P(("z", "y"), ("x", "half", "core")), check_vma=False,
    )
```

time: 141 us -> 133 us (0.943)
  blocking collectives: 22.7 us -> 13.1 us
  starting transfers between devices: 45.5 us -> 54.7 us
  local copies, waits for them, and re-layouts: 9.83 us -> 2.74 us
  Pallas kernels: 10.4 us -> 8.08 us
  waiting for transfers between devices: 50 us -> 52.2 us
    ppermute x11 -> x17, starting transfers between devices: 17.6 us -> 34.9 us  [the longest x3 16.2 us: local(): basis[k] = lax.ppermute(packed[k], 'y', [(i, i ^ k) for i in range(Y)])]
    ppermute x11 -> x17, waiting for transfers between devices: 36.4 us -> 49.4 us  [the longest x4 22.2 us: local(): lax.ppermute(odd, 'z', pairs[0])]
    ppermute x4 -> x2, waiting for transfers between devices: 13.6 us -> 2.87 us  [shift(): return lax.ppermute(a, axis, [(i, (i + by) % size) for i in range(size)])]
    all_to_all x1, blocking collectives: 22.7 us -> 13.1 us  [local(): got = lax.all_to_all(mine, ('y', 'x'), 0, 0, tiled=True)]
    ppermute x4 -> x2, starting transfers between devices: 27.9 us -> 19.9 us  [shift(): return lax.ppermute(a, axis, [(i, (i + by) % size) for i in range(size)])]
    unnamed x22 -> x4, local copies, waits for them, and re-layouts: 9.06 us -> 1.89 us
    pallas_call x6 -> x7, Pallas kernels: 10.2 us -> 7.88 us  [the longest x6 7.29 us: add_chunks(): pl.pallas_call(functools.partial(add_kernel, sources, total is None, last...]
  transfers between devices with their start and end apart: 15 -> 19, of which waited for: 11 -> 15; matrix products, arithmetic and copies ran while one was open for 1% -> 0% of each run, Pallas kernels for 7% -> 5%
where the time goes in v7:
time: 133 us; the launch traced here: 132 us
  starting transfers between devices  54.7 us (41%)
  waiting for transfers between devices  52.2 us (39%)
  blocking collectives  13.1 us (10%)
  Pallas kernels  8.08 us (6%)
  local copies, waits for them, and re-layouts  2.74 us (2%)
    ppermute x4, waiting for transfers between devices, local(): lax.ppermute(odd, 'z', pairs[0])  22.2 us
    ppermute x2, starting transfers between devices, shift(): return lax.ppermute(a, axis, [(i, (i + by) % size) for i in range(size)])  19.9 us
    ppermute x3, starting transfers between devices, local(): basis[k] = lax.ppermute(packed[k], 'y', [(i, i ^ k) for i in range(Y)])  16.2 us
    ppermute x6, waiting for transfers between devices, local(): beyond = [lax.ppermute(b, 'z', up + down) for b in beyond]  16.1 us
    all_to_all x1, blocking collectives, local(): got = lax.all_to_all(mine, ('y', 'x'), 0, 0, tiled=True)  13.1 us
    ppermute x3, waiting for transfers between devices, local(): basis[k] = lax.ppermute(packed[k], 'y', [(i, i ^ k) for i in range(Y)])  11 us
    ppermute x4, starting transfers between devices, local(): lax.ppermute(odd, 'z', pairs[0])  8.24 us
    ppermute x6, starting transfers between devices, local(): beyond = [lax.ppermute(b, 'z', up + down) for b in beyond]  7.71 us
  transfers between devices with their start and end apart: 19, of which 15 were waited for; matrix products, arithmetic and copies ran while one was open for 0% of the time, Pallas kernels for 5%

profile of v7, /device:TPU:1, one launch (start us, length us, event | category | flops | bytes accessed | tf_op | source)
XLA Modules:
  0.0 132.0 jit_solution(9229785915613688728)
XLA Ops:
  0.0 4.4 %collective-permute-start.4 = (f32[512,256]{1,0:T(8,128)}, f32[512,256]{1,0:T(8,128)S(1)}, u32[]{:S(2)}, u32[]{:S(2)}) collective-permute-start(f32[512,256]{1,0:T(8,128)} %refs_4_.1), channel_id=1, source_target_pairs={{0,64},{128,192},{256,320},{384,448},{64,0},{192,128},{320,256},{4... | collective-permute-start | bytes 1572872 | tf_op jit(solution)/shard_map/vectors_along_z/ppermute | solution.py:205
  5.8 1.9 %copy-done = f32[48,16384]{1,0:T(8,128)S(1)} copy-done((f32[48,16384]{1,0:T(8,128)S(1)}, f32[48,16384]{1,0:T(8,128)}, u32[]{:S(2)}) %copy-start) | copy-done | bytes 3145752
  7.9 3.8 %collective-permute-done.4.refs_9_ = f32[512,256]{1,0:T(8,128)S(1)} collective-permute-done((f32[512,256]{1,0:T(8,128)}, f32[512,256]{1,0:T(8,128)S(1)}, u32[]{:S(2)}, u32[]{:S(2)}) %collective-permute-start.4) | collective-permute-done | bytes 524320 | tf_op jit(solution)/shard_map/vectors_along_z/ppermute | solution.py:205
  12.4 1.3 collective-permute-start.1
  13.7 7.6 %collective-permute-start.7 = (f32[48,4096]{1,0:T(8,128)S(1)}, f32[48,4096]{1,0:T(8,128)S(1)}, u32[]{:S(2)}, u32[]{:S(2)}) collective-permute-start(f32[48,4096]{1,0:T(8,128)S(1)} %get-tuple-element.37), channel_id=1, source_target_pairs={{0,16},{16,0},{32,48},{48,32},{1,17},{17,1},{33,49},{49,33},{2,18}... | collective-permute-start | bytes 2359304 | tf_op jit(solution)/shard_map/basis_along_y/ppermute | solution.py:187
  21.3 3.8 %collective-permute-start.8 = (f32[48,4096]{1,0:T(8,128)S(1)}, f32[48,4096]{1,0:T(8,128)S(1)}, u32[]{:S(2)}, u32[]{:S(2)}) collective-permute-start(f32[48,4096]{1,0:T(8,128)S(1)} %get-tuple-element.38), channel_id=1, source_target_pairs={{0,48},{16,32},{32,16},{48,0},{1,49},{17,33},{33,17},{49,1},{2,50}... | collective-permute-start | bytes 2359304 | tf_op jit(solution)/shard_map/basis_along_y/ppermute | solution.py:187
  25.2 1.3 collective-permute-start.6
  26.5 6.7 %collective-permute-done.1.refs_4_ = f32[512,256]{1,0:T(8,128)S(1)} collective-permute-done((f32[512,256]{1,0:T(8,128)S(1)}, f32[512,256]{1,0:T(8,128)S(1)}, u32[]{:S(2)}, u32[]{:S(2)}) %collective-permute-start.1) | collective-permute-done | bytes 524320 | tf_op jit(solution)/shard_map/vectors_along_z/ppermute | solution.py:205
  33.9 2.9 %collective-permute-done.7.refs_1_.refs_6_.refs_11_.refs_16_.refs_21_ = f32[48,4096]{1,0:T(8,128)S(1)} collective-permute-done((f32[48,4096]{1,0:T(8,128)S(1)}, f32[48,4096]{1,0:T(8,128)S(1)}, u32[]{:S(2)}, u32[]{:S(2)}) %collective-permute-start.7) | collective-permute-done | bytes 786464 | tf_op jit(solution)/shard_map/basis_along_y/ppermute | solution.py:187
  36.8 5.0 %collective-permute-done.8.refs_3_.refs_8_.refs_13_.refs_18_.refs_23_ = f32[48,4096]{1,0:T(8,128)S(1)} collective-permute-done((f32[48,4096]{1,0:T(8,128)S(1)}, f32[48,4096]{1,0:T(8,128)S(1)}, u32[]{:S(2)}, u32[]{:S(2)}) %collective-permute-start.8) | collective-permute-done | bytes 786464 | tf_op jit(solution)/shard_map/basis_along_y/ppermute | solution.py:187
  41.8 2.6 %collective-permute-done.6.refs_4_ = f32[512,256]{1,0:T(8,128)S(1)} collective-permute-done((f32[512,256]{1,0:T(8,128)S(1)}, f32[512,256]{1,0:T(8,128)S(1)}, u32[]{:S(2)}, u32[]{:S(2)}) %collective-permute-start.6) | collective-permute-done | bytes 524320 | tf_op jit(solution)/shard_map/vectors_along_z/ppermute | solution.py:205
  45.1 1.3 collective-permute-start.3
  46.4 4.8 %collective-permute-start.11 = (f32[48,4096]{1,0:T(8,128)S(1)}, f32[48,4096]{1,0:T(8,128)S(1)}, u32[]{:S(2)}, u32[]{:S(2)}) collective-permute-start(f32[48,4096]{1,0:T(8,128)S(1)} %get-tuple-element.43), channel_id=1, source_target_pairs={{0,32},{16,48},{32,0},{48,16},{1,33},{17,49},{33,1},{49,17},{2,34}... | collective-permute-start | bytes 2359304 | tf_op jit(solution)/shard_map/basis_along_y/ppermute | solution.py:187
  51.3 9.1 %collective-permute-done.3.even.refs_4_ = f32[512,256]{1,0:T(8,128)S(1)} collective-permute-done((f32[512,256]{1,0:T(8,128)S(1)}, f32[512,256]{1,0:T(8,128)S(1)}, u32[]{:S(2)}, u32[]{:S(2)}) %collective-permute-start.3) | collective-permute-done | bytes 524320 | tf_op jit(solution)/shard_map/vectors_along_z/ppermute | solution.py:205
  61.0 1.3 collective-permute-start.10
  62.3 1.3 collective-permute-start.12
  63.6 3.1 %collective-permute-done.11.refs_2_.refs_7_.refs_12_.refs_17_.refs_22_ = f32[48,4096]{1,0:T(8,128)S(1)} collective-permute-done((f32[48,4096]{1,0:T(8,128)S(1)}, f32[48,4096]{1,0:T(8,128)S(1)}, u32[]{:S(2)}, u32[]{:S(2)}) %collective-permute-start.11) | collective-permute-done | bytes 786464 | tf_op jit(solution)/shard_map/basis_along_y/ppermute | solution.py:187
  66.6 1.7 %collective-permute-done.10.refs_4_ = f32[256,256]{1,0:T(8,128)S(1)} collective-permute-done((f32[256,256]{1,0:T(8,128)S(1)}, f32[256,256]{1,0:T(8,128)S(1)}, u32[]{:S(2)}, u32[]{:S(2)}) %collective-permute-start.10) | collective-permute-done | bytes 262176 | tf_op jit(solution)/shard_map/vectors_along_z/ppermute | solution.py:208
  68.4 1.3 collective-permute-start.15
  69.7 3.0 %collective-permute-done.12.refs_9_ = f32[256,256]{1,0:T(8,128)S(1)} collective-permute-done((f32[256,256]{1,0:T(8,128)S(1)}, f32[256,256]{1,0:T(8,128)S(1)}, u32[]{:S(2)}, u32[]{:S(2)}) %collective-permute-start.12) | collective-permute-done | bytes 262176 | tf_op jit(solution)/shard_map/vectors_along_z/ppermute | solution.py:208
  72.7 1.3 collective-permute-start.13
  74.0 1.3 %add_chunks.6.refs_10_ = f32[2,192,256]{2,1,0:T(8,128)S(1)} custom-call(s32[5]{0:T(128)S(1)} %stack.19.info, f32[48,4096]{1,0:T(8,128)S(1)} %get-tuple-element.45.refs_0_.refs_5_.refs_10_.refs_15_.refs_20_, f32[48,4096]{1,0:T(8,128)S(1)} %collective-permute-done.7.refs_1_.refs_6_.refs_11_.refs_16_.refs_21_, ...), custom_call_target="tpu_custom_call" | custom-call | flops 452984832 | bytes 4194304 | tf_op jit(solution)/shard_map/add_chunks/pallas_call | solution.py:118
  79.3 1.3 collective-permute-start.16
  80.6 2.0 %collective-permute-done.13.refs_19_ = f32[256,256]{1,0:T(8,128)S(1)} collective-permute-done((f32[256,256]{1,0:T(8,128)S(1)}, f32[256,256]{1,0:T(8,128)S(1)}, u32[]{:S(2)}, u32[]{:S(2)}) %collective-permute-start.13) | collective-permute-done | bytes 262176 | tf_op jit(solution)/shard_map/vectors_along_z/ppermute | solution.py:208
  82.6 1.3 collective-permute-start.14
  83.9 5.2 %collective-permute-done.16.refs_24_ = f32[256,256]{1,0:T(8,128)S(1)} collective-permute-done((f32[256,256]{1,0:T(8,128)S(1)}, f32[256,256]{1,0:T(8,128)S(1)}, u32[]{:S(2)}, u32[]{:S(2)}) %collective-permute-start.16) | collective-permute-done | bytes 262176 | tf_op jit(solution)/shard_map/vectors_along_z/ppermute | solution.py:208
  89.1 1.9 %add_chunks.10.refs_5_ = f32[2,192,256]{2,1,0:T(8,128)S(1)} custom-call(s32[5]{0:T(128)S(1)} %stack.19.info, f32[48,4096]{1,0:T(8,128)S(1)} %get-tuple-element.45.refs_0_.refs_5_.refs_10_.refs_15_.refs_20_, f32[48,4096]{1,0:T(8,128)S(1)} %collective-permute-done.7.refs_1_.refs_6_.refs_11_.refs_16_.refs_21_, ...), custom_call_target="tpu_custom_call", output_to_operand_aliasing={{}: (26, {})} | custom-call | flops 377487360 | bytes 4194304 | tf_op jit(solution)/shard_map/add_chunks/pallas_call | solution.py:118
  91.0 3.2 %collective-permute-done.14.refs_4_ = f32[256,256]{1,0:T(8,128)S(1)} collective-permute-done((f32[256,256]{1,0:T(8,128)S(1)}, f32[256,256]{1,0:T(8,128)S(1)}, u32[]{:S(2)}, u32[]{:S(2)}) %collective-permute-start.14) | collective-permute-done | bytes 262176 | tf_op jit(solution)/shard_map/vectors_along_z/ppermute | solution.py:208
  95.2 8.5 %collective-permute-start.17 = (f32[16,24,128]{2,1,0:T(8,128)S(1)}, f32[16,24,128]{2,1,0:T(8,128)S(1)}, u32[]{:S(2)}, u32[]{:S(2)}) collective-permute-start(f32[16,24,128]{2,1,0:T(8,128)S(1)} %get-tuple-element.54), channel_id=1, source_target_pairs={{0,1},{1,0},{2,3},{3,2},{4,5},{5,4},{6,7},{7,6},{8,9},{9,8},{10,11... | collective-permute-start | bytes 589832 | tf_op jit(solution)/shard_map/sum_over_columns/ppermute | solution.py:160
  104.8 13.1 %all_to_all.5 = f32[16,24,128]{2,1,0:T(8,128)S(1)} all-to-all(f32[16,24,128]{2,1,0:T(8,128)S(1)} %add.17), channel_id=1, replica_groups=mesh['z'=8,'y'=4,'x'=4,'half'=2,'core'=2] {'y','x'}, dimensions={0} | all-to-all | bytes 393216 | tf_op jit(solution)/shard_map/sum_over_columns/all_to_all | solution.py:217
  118.0 11.3 %collective-permute-start.18 = (f32[24,128]{1,0:T(8,128)S(1)}, f32[24,128]{1,0:T(8,128)S(1)}, u32[]{:S(2)}, u32[]{:S(2)}) collective-permute-start(f32[24,128]{1,0:T(8,128)S(1)} %reduce_sum.9), channel_id=1, source_target_pairs={{0,2},{2,0},{1,3},{3,1},{4,6},{6,4},{5,7},{7,5},{8,10},{10,8},{9,1... | collective-permute-start | bytes 36872 | tf_op jit(solution)/shard_map/sum_over_columns/ppermute | solution.py:160
  129.3 1.8 %collective-permute-done.18 = f32[24,128]{1,0:T(8,128)S(1)} collective-permute-done((f32[24,128]{1,0:T(8,128)S(1)}, f32[24,128]{1,0:T(8,128)S(1)}, u32[]{:S(2)}, u32[]{:S(2)}) %collective-permute-start.18) | collective-permute-done | bytes 12320 | tf_op jit(solution)/shard_map/sum_over_columns/ppermute | solution.py:160
  (26 shorter events, 10.5 us)
Async XLA Ops:
  0.0 11.7 %collective-permute-start.4 = (f32[512,256]{1,0:T(8,128)}, f32[512,256]{1,0:T(8,128)S(1)}, u32[]{:S(2)}, u32[]{:S(2)}) collective-permute-start(f32[512,256]{1,0:T(8,128)} %refs_4_.1), channel_id=1, source_target_pairs={{0,64},{128,192},{256,320},{384,448},{64,0},{192,128},{320,256},{4... | collective-permute-start | bytes 1572872 | tf_op jit(solution)/shard_map/vectors_along_z/ppermute | solution.py:205
  4.4 8.1 %collective-permute-start = (f32[512,256]{1,0:T(8,128)}, f32[512,256]{1,0:T(8,128)S(1)}, u32[]{:S(2)}, u32[]{:S(2)}) collective-permute-start(f32[512,256]{1,0:T(8,128)} %refs_4_.1), channel_id=1, source_target_pairs={{64,128},{192,256},{320,384},{128,64},{256,192},{384,320},{65,129}... | collective-permute-start | bytes 1572872 | tf_op jit(solution)/shard_map/vectors_along_z/ppermute | solution.py:205
  5.8 1.9 %copy-start = (f32[48,16384]{1,0:T(8,128)S(1)}, f32[48,16384]{1,0:T(8,128)}, u32[]{:S(2)}) copy-start(f32[48,16384]{1,0:T(8,128)} %slab) | copy-start | bytes 9437188
  7.7 66.3 %copy-start.1 = (f32[512,256]{1,0:T(8,128)S(1)}, f32[512,256]{1,0:T(8,128)}, u32[]{:S(2)}) copy-start(f32[512,256]{1,0:T(8,128)} %refs_4_.1) | copy-start | bytes 1572868
  11.7 13.4 %collective-permute-start.5 = (f32[512,256]{1,0:T(8,128)S(1)}, f32[512,256]{1,0:T(8,128)S(1)}, u32[]{:S(2)}, u32[]{:S(2)}) collective-permute-start(f32[512,256]{1,0:T(8,128)S(1)} %collective-permute-done.4.refs_9_), channel_id=1, source_target_pairs={{64,128},{192,256},{320,384},{128,64},{256,192},{384,320},{65,129}... | collective-permute-start | bytes 1572872 | tf_op jit(solution)/shard_map/vectors_along_z/ppermute | solution.py:205
  12.4 20.8 %collective-permute-start.1 = (f32[512,256]{1,0:T(8,128)S(1)}, f32[512,256]{1,0:T(8,128)S(1)}, u32[]{:S(2)}, u32[]{:S(2)}) collective-permute-start(f32[512,256]{1,0:T(8,128)S(1)} %collective-permute-done.refs_14_), channel_id=1, source_target_pairs={{128,192},{256,320},{384,448},{64,0},{192,128},{320,256},{129,193}... | collective-permute-start | bytes 1572872 | tf_op jit(solution)/shard_map/vectors_along_z/ppermute | solution.py:205
  13.7 23.1 %collective-permute-start.7 = (f32[48,4096]{1,0:T(8,128)S(1)}, f32[48,4096]{1,0:T(8,128)S(1)}, u32[]{:S(2)}, u32[]{:S(2)}) collective-permute-start(f32[48,4096]{1,0:T(8,128)S(1)} %get-tuple-element.37), channel_id=1, source_target_pairs={{0,16},{16,0},{32,48},{48,32},{1,17},{17,1},{33,49},{49,33},{2,18}... | collective-permute-start | bytes 2359304 | tf_op jit(solution)/shard_map/basis_along_y/ppermute | solution.py:187
  21.3 20.5 %collective-permute-start.8 = (f32[48,4096]{1,0:T(8,128)S(1)}, f32[48,4096]{1,0:T(8,128)S(1)}, u32[]{:S(2)}, u32[]{:S(2)}) collective-permute-start(f32[48,4096]{1,0:T(8,128)S(1)} %get-tuple-element.38), channel_id=1, source_target_pairs={{0,48},{16,32},{32,16},{48,0},{1,49},{17,33},{33,17},{49,1},{2,50}... | collective-permute-start | bytes 2359304 | tf_op jit(solution)/shard_map/basis_along_y/ppermute | solution.py:187
  25.2 19.3 %collective-permute-start.6 = (f32[512,256]{1,0:T(8,128)S(1)}, f32[512,256]{1,0:T(8,128)S(1)}, u32[]{:S(2)}, u32[]{:S(2)}) collective-permute-start(f32[512,256]{1,0:T(8,128)S(1)} %collective-permute-done.5.refs_9_), channel_id=1, source_target_pairs={{128,192},{256,320},{384,448},{64,0},{192,128},{320,256},{129,193}... | collective-permute-start | bytes 1572872 | tf_op jit(solution)/shard_map/vectors_along_z/ppermute | solution.py:205
  33.2 11.9 %collective-permute-start.2 = (f32[512,256]{1,0:T(8,128)S(1)}, f32[512,256]{1,0:T(8,128)S(1)}, u32[]{:S(2)}, u32[]{:S(2)}) collective-permute-start(f32[512,256]{1,0:T(8,128)S(1)} %collective-permute-done.1.refs_4_), channel_id=1, source_target_pairs={{192,256},{320,384},{128,64},{256,192},{193,257},{321,385},{129,65... | collective-permute-start | bytes 1572872 | tf_op jit(solution)/shard_map/vectors_along_z/ppermute | solution.py:205
  44.4 6.8 %collective-permute-start.9 = (f32[512,256]{1,0:T(8,128)S(1)}, f32[512,256]{1,0:T(8,128)S(1)}, u32[]{:S(2)}, u32[]{:S(2)}) collective-permute-start(f32[512,256]{1,0:T(8,128)S(1)} %collective-permute-done.6.refs_4_), channel_id=1, source_target_pairs={{192,256},{320,384},{128,64},{256,192},{193,257},{321,385},{129,65... | collective-permute-start | bytes 1572872 | tf_op jit(solution)/shard_map/vectors_along_z/ppermute | solution.py:205
  45.1 15.2 %collective-permute-start.3 = (f32[512,256]{1,0:T(8,128)S(1)}, f32[512,256]{1,0:T(8,128)S(1)}, u32[]{:S(2)}, u32[]{:S(2)}) collective-permute-start(f32[512,256]{1,0:T(8,128)S(1)} %collective-permute-done.2.refs_9_), channel_id=1, source_target_pairs={{256,320},{384,448},{64,0},{192,128},{257,321},{385,449},{65,1},{1... | collective-permute-start | bytes 1572872 | tf_op jit(solution)/shard_map/vectors_along_z/ppermute | solution.py:205
  46.4 20.2 %collective-permute-start.11 = (f32[48,4096]{1,0:T(8,128)S(1)}, f32[48,4096]{1,0:T(8,128)S(1)}, u32[]{:S(2)}, u32[]{:S(2)}) collective-permute-start(f32[48,4096]{1,0:T(8,128)S(1)} %get-tuple-element.43), channel_id=1, source_target_pairs={{0,32},{16,48},{32,0},{48,16},{1,33},{17,49},{33,1},{49,17},{2,34}... | collective-permute-start | bytes 2359304 | tf_op jit(solution)/shard_map/basis_along_y/ppermute | solution.py:187
  61.0 7.4 %collective-permute-start.10 = (f32[256,256]{1,0:T(8,128)S(1)}, f32[256,256]{1,0:T(8,128)S(1)}, u32[]{:S(2)}, u32[]{:S(2)}) collective-permute-start(f32[256,256]{1,0:T(8,128)S(1)} %get-tuple-element.40), channel_id=1, source_target_pairs={{256,320},{320,384},{384,448},{64,0},{128,64},{192,128},{257,321},... | collective-permute-start | bytes 786440 | tf_op jit(solution)/shard_map/vectors_along_z/ppermute | solution.py:208
  62.3 10.4 %collective-permute-start.12 = (f32[256,256]{1,0:T(8,128)S(1)}, f32[256,256]{1,0:T(8,128)S(1)}, u32[]{:S(2)}, u32[]{:S(2)}) collective-permute-start(f32[256,256]{1,0:T(8,128)S(1)} %get-tuple-element.49), channel_id=1, source_target_pairs={{256,320},{320,384},{384,448},{64,0},{128,64},{192,128},{257,321},... | collective-permute-start | bytes 786440 | tf_op jit(solution)/shard_map/vectors_along_z/ppermute | solution.py:208
  68.4 10.9 %collective-permute-start.15 = (f32[256,256]{1,0:T(8,128)S(1)}, f32[256,256]{1,0:T(8,128)S(1)}, u32[]{:S(2)}, u32[]{:S(2)}) collective-permute-start(f32[256,256]{1,0:T(8,128)S(1)} %collective-permute-done.10.refs_4_), channel_id=1, source_target_pairs={{320,384},{384,448},{64,0},{128,64},{321,385},{385,449},{65,1},{12... | collective-permute-start | bytes 786440 | tf_op jit(solution)/shard_map/vectors_along_z/ppermute | solution.py:208
  72.7 9.9 %collective-permute-start.13 = (f32[256,256]{1,0:T(8,128)S(1)}, f32[256,256]{1,0:T(8,128)S(1)}, u32[]{:S(2)}, u32[]{:S(2)}) collective-permute-start(f32[256,256]{1,0:T(8,128)S(1)} %collective-permute-done.12.refs_9_), channel_id=1, source_target_pairs={{320,384},{384,448},{64,0},{128,64},{321,385},{385,449},{65,1},{12... | collective-permute-start | bytes 786440 | tf_op jit(solution)/shard_map/vectors_along_z/ppermute | solution.py:208
  79.3 9.8 %collective-permute-start.16 = (f32[256,256]{1,0:T(8,128)S(1)}, f32[256,256]{1,0:T(8,128)S(1)}, u32[]{:S(2)}, u32[]{:S(2)}) collective-permute-start(f32[256,256]{1,0:T(8,128)S(1)} %collective-permute-done.15.refs_14_), channel_id=1, source_target_pairs={{384,448},{64,0},{385,449},{65,1},{386,450},{66,2},{387,451},{67,3... | collective-permute-start | bytes 786440 | tf_op jit(solution)/shard_map/vectors_along_z/ppermute | solution.py:208
  82.6 11.7 %collective-permute-start.14 = (f32[256,256]{1,0:T(8,128)S(1)}, f32[256,256]{1,0:T(8,128)S(1)}, u32[]{:S(2)}, u32[]{:S(2)}) collective-permute-start(f32[256,256]{1,0:T(8,128)S(1)} %collective-permute-done.13.refs_19_), channel_id=1, source_target_pairs={{384,448},{64,0},{385,449},{65,1},{386,450},{66,2},{387,451},{67,3... | collective-permute-start | bytes 786440 | tf_op jit(solution)/shard_map/vectors_along_z/ppermute | solution.py:208
  95.2 9.6 %collective-permute-start.17 = (f32[16,24,128]{2,1,0:T(8,128)S(1)}, f32[16,24,128]{2,1,0:T(8,128)S(1)}, u32[]{:S(2)}, u32[]{:S(2)}) collective-permute-start(f32[16,24,128]{2,1,0:T(8,128)S(1)} %get-tuple-element.54), channel_id=1, source_target_pairs={{0,1},{1,0},{2,3},{3,2},{4,5},{5,4},{6,7},{7,6},{8,9},{9,8},{10,11... | collective-permute-start | bytes 589832 | tf_op jit(solution)/shard_map/sum_over_columns/ppermute | solution.py:160
  118.0 13.2 %collective-permute-start.18 = (f32[24,128]{1,0:T(8,128)S(1)}, f32[24,128]{1,0:T(8,128)S(1)}, u32[]{:S(2)}, u32[]{:S(2)}) collective-permute-start(f32[24,128]{1,0:T(8,128)S(1)} %reduce_sum.9), channel_id=1, source_target_pairs={{0,2},{2,0},{1,3},{3,1},{4,6},{6,4},{5,7},{7,5},{8,10},{10,8},{9,1... | collective-permute-start | bytes 36872 | tf_op jit(solution)/shard_map/sum_over_columns/ppermute | solution.py:160

commit v8 on v7

--- a/solution.py
+++ b/solution.py
@@ -49,7 +49,7 @@
 
 def add_kernel(sources, first, last, info, *refs):
     total = refs[-1]
-    out, send = refs[-3:-1] if last else (total, None)
+    out = refs[-2] if last else total
     if first:
         total[...] = jnp.zeros_like(total)
     else:
@@ -88,10 +88,9 @@
                 cols = slice((x % 2) * wide, (x % 2 + 1) * wide)
                 top = total[x // 2, k * rows : k * rows + rows // 2, cols]
                 bottom = total[x // 2, k * rows + rows // 2 : (k + 1) * rows, cols]
-                at = to * X + x
-                mine, other = jnp.where(low, top, pltpu.roll(bottom, wide // 4, 1)), jnp.where(low, pltpu.roll(top, wide - wide // 4, 1), bottom)
-                out[at] = jnp.where(core == 0, mine, other)
-                send[at] = jnp.where(core == 0, other, mine)
+                at = (to * X + x) * 2
+                out[at] = jnp.where(low, top, pltpu.roll(bottom, wide // 4, 1))
+                out[at + 1] = jnp.where(low, pltpu.roll(top, wide - wide // 4, 1), bottom)
 
 
 def add_chunks(info, basis, pieces, total, last=False):
@@ -113,16 +112,16 @@
     if total is not None:
         specs.append(whole)
         args.append(total)
-    out = (Y * X, rows // 2, cols // 2) if last else shape
+    out = (Y * X * 2, rows // 2, cols // 2) if last else shape
     flops = sum(6 * Y * rows * vec.size for vec, _, _ in pieces)
     return pl.pallas_call(
         functools.partial(add_kernel, sources, total is None, last),
-        out_shape=[jax.ShapeDtypeStruct(out, F32)] * 2 if last else jax.ShapeDtypeStruct(out, F32),
+        out_shape=jax.ShapeDtypeStruct(out, F32),
         grid_spec=pltpu.PrefetchScalarGridSpec(
             num_scalar_prefetch=1,
             grid=(1,),
             in_specs=specs,
-            out_specs=[pl.BlockSpec(out, lambda g, s: (0, 0, 0))] * 2 if last else pl.BlockSpec(out, lambda g, s: (0, 0, 0)),
+            out_specs=pl.BlockSpec(out, lambda g, s: (0, 0, 0)),
             scratch_shapes=[pltpu.VMEM(shape, F32)] if last else [],
         ),
         input_output_aliases={} if total is None or last else {len(args): 0},
@@ -154,6 +153,25 @@
         compiler_params=pltpu.CompilerParams(vmem_limit_bytes=4 << 20),
         name="select",
     )(info, even, odd)
+
+
+def finish_kernel(half, mine, other, out):
+    rows, wide = mine.shape[0], out.shape[0]
+    both = mine[...] + other[...]
+    both = jnp.where(half[0] == 0, both, pltpu.roll(both, 2 * wide, 1)).T
+    out[...] = jnp.concatenate([both[:wide], both[wide : 2 * wide]], axis=1)
+
+
+def finish(half, mine, other):
+    vmem = pl.BlockSpec(memory_space=pltpu.VMEM)
+    return pl.pallas_call(
+        finish_kernel,
+        out_shape=jax.ShapeDtypeStruct((mine.shape[1] // 4, 2 * mine.shape[0]), F32),
+        in_specs=[pl.BlockSpec(memory_space=pltpu.SMEM), vmem, vmem],
+        out_specs=vmem,
+        compiler_params=pltpu.CompilerParams(vmem_limit_bytes=4 << 20),
+        name="finish",
+    )(half, mine, other)
 
 
 def shift(a, axis, size, by):
@@ -212,14 +230,9 @@
     total = add_chunks(info, basis, pieces[-1:], total, last=True)
 
     with jax.named_scope("sum_over_columns"):
-        mine, other = total
-        mine = mine + shift(other, "core", 2, 1)
-        got = lax.all_to_all(mine, ("y", "x"), 0, 0, tiled=True)
+        got = lax.all_to_all(total, ("y", "x", "core"), 0, 0, tiled=True)
         mine = jnp.sum(got, axis=0)
-        mine = mine + shift(mine, "half", 2, 1)
-        wide = mine.shape[1] // 4
-        mine = lax.dynamic_slice(mine, (0, at["half"] * 2 * wide), (rows // 2, 2 * wide))
-        return jnp.concatenate([mine[:, :wide], mine[:, wide:]], axis=0)
+        return finish(at["half"][None], mine, shift(mine, "half", 2, 1)).T
 
 
 def solution(mesh):

time: 133 us -> 133 us (level)
  blocking collectives: 13.1 us -> 23 us
  starting transfers between devices: 54.7 us -> 46.2 us
    all_to_all x1, blocking collectives: 13.1 us -> 23 us  [local(): got = lax.all_to_all(total, ('y', 'x', 'core'), 0, 0, tiled=True)]
    ppermute x2 -> x1, starting transfers between devices: 19.9 us -> 11.3 us  [shift(): return lax.ppermute(a, axis, [(i, (i + by) % size) for i in range(size)])]
    ppermute x2 -> x1, waiting for transfers between devices: 2.87 us -> 1.82 us  [shift(): return lax.ppermute(a, axis, [(i, (i + by) % size) for i in range(size)])]
  transfers between devices with their start and end apart: 19 -> 18, of which waited for: 15 -> 14; matrix products, arithmetic and copies ran while one was open for 0% -> 0% of each run, Pallas kernels for 5% -> 5%
where the time goes in v8:
time: 133 us; the launch traced here: 132 us
  waiting for transfers between devices  51.2 us (38%)
  starting transfers between devices  46.2 us (35%)
  blocking collectives  23 us (17%)
  Pallas kernels  8.91 us (7%)
  local copies, waits for them, and re-layouts  1.98 us (1%)
    all_to_all x1, blocking collectives, local(): got = lax.all_to_all(total, ('y', 'x', 'core'), 0, 0, tiled=True)  23 us
    ppermute x4, waiting for transfers between devices, local(): lax.ppermute(odd, 'z', pairs[0])  22.2 us
    ppermute x3, starting transfers between devices, local(): basis[k] = lax.ppermute(packed[k], 'y', [(i, i ^ k) for i in range(Y)])  16.2 us
    ppermute x6, waiting for transfers between devices, local(): beyond = [lax.ppermute(b, 'z', up + down) for b in beyond]  16.1 us
    ppermute x1, starting transfers between devices, shift(): return lax.ppermute(a, axis, [(i, (i + by) % size) for i in range(size)])  11.3 us
    ppermute x3, waiting for transfers between devices, local(): basis[k] = lax.ppermute(packed[k], 'y', [(i, i ^ k) for i in range(Y)])  11 us
    ppermute x4, starting transfers between devices, local(): lax.ppermute(odd, 'z', pairs[0])  8.24 us
    ppermute x6, starting transfers between devices, local(): beyond = [lax.ppermute(b, 'z', up + down) for b in beyond]  7.71 us
  transfers between devices with their start and end apart: 18, of which 14 were waited for; matrix products, arithmetic and copies ran while one was open for 0% of the time, Pallas kernels for 5%

profile of v8, /device:TPU:1, one launch (start us, length us, event | category | flops | bytes accessed | tf_op | source)
XLA Modules:
  0.0 132.3 jit_solution(823126831980798141)
XLA Ops:
  0.0 4.4 %collective-permute-start.4 = (f32[512,256]{1,0:T(8,128)}, f32[512,256]{1,0:T(8,128)S(1)}, u32[]{:S(2)}, u32[]{:S(2)}) collective-permute-start(f32[512,256]{1,0:T(8,128)} %refs_4_.1), channel_id=1, source_target_pairs={{0,64},{128,192},{256,320},{384,448},{64,0},{192,128},{320,256},{4... | collective-permute-start | bytes 1572872 | tf_op jit(solution)/shard_map/vectors_along_z/ppermute | solution.py:223
  5.8 1.9 %copy-done = f32[48,16384]{1,0:T(8,128)S(1)} copy-done((f32[48,16384]{1,0:T(8,128)S(1)}, f32[48,16384]{1,0:T(8,128)}, u32[]{:S(2)}) %copy-start) | copy-done | bytes 3145752
  7.9 3.8 %collective-permute-done.4.refs_9_ = f32[512,256]{1,0:T(8,128)S(1)} collective-permute-done((f32[512,256]{1,0:T(8,128)}, f32[512,256]{1,0:T(8,128)S(1)}, u32[]{:S(2)}, u32[]{:S(2)}) %collective-permute-start.4) | collective-permute-done | bytes 524320 | tf_op jit(solution)/shard_map/vectors_along_z/ppermute | solution.py:223
  12.4 1.3 collective-permute-start.1
  13.7 7.6 %collective-permute-start.7 = (f32[48,4096]{1,0:T(8,128)S(1)}, f32[48,4096]{1,0:T(8,128)S(1)}, u32[]{:S(2)}, u32[]{:S(2)}) collective-permute-start(f32[48,4096]{1,0:T(8,128)S(1)} %get-tuple-element.35), channel_id=1, source_target_pairs={{0,16},{16,0},{32,48},{48,32},{1,17},{17,1},{33,49},{49,33},{2,18}... | collective-permute-start | bytes 2359304 | tf_op jit(solution)/shard_map/basis_along_y/ppermute | solution.py:205
  21.3 3.8 %collective-permute-start.8 = (f32[48,4096]{1,0:T(8,128)S(1)}, f32[48,4096]{1,0:T(8,128)S(1)}, u32[]{:S(2)}, u32[]{:S(2)}) collective-permute-start(f32[48,4096]{1,0:T(8,128)S(1)} %get-tuple-element.36), channel_id=1, source_target_pairs={{0,48},{16,32},{32,16},{48,0},{1,49},{17,33},{33,17},{49,1},{2,50}... | collective-permute-start | bytes 2359304 | tf_op jit(solution)/shard_map/basis_along_y/ppermute | solution.py:205
  25.2 1.3 collective-permute-start.6
  26.5 6.7 %collective-permute-done.1.refs_4_ = f32[512,256]{1,0:T(8,128)S(1)} collective-permute-done((f32[512,256]{1,0:T(8,128)S(1)}, f32[512,256]{1,0:T(8,128)S(1)}, u32[]{:S(2)}, u32[]{:S(2)}) %collective-permute-start.1) | collective-permute-done | bytes 524320 | tf_op jit(solution)/shard_map/vectors_along_z/ppermute | solution.py:223
  33.9 2.9 %collective-permute-done.7.refs_1_.refs_6_.refs_11_.refs_16_.refs_21_ = f32[48,4096]{1,0:T(8,128)S(1)} collective-permute-done((f32[48,4096]{1,0:T(8,128)S(1)}, f32[48,4096]{1,0:T(8,128)S(1)}, u32[]{:S(2)}, u32[]{:S(2)}) %collective-permute-start.7) | collective-permute-done | bytes 786464 | tf_op jit(solution)/shard_map/basis_along_y/ppermute | solution.py:205
  36.8 5.0 %collective-permute-done.8.refs_3_.refs_8_.refs_13_.refs_18_.refs_23_ = f32[48,4096]{1,0:T(8,128)S(1)} collective-permute-done((f32[48,4096]{1,0:T(8,128)S(1)}, f32[48,4096]{1,0:T(8,128)S(1)}, u32[]{:S(2)}, u32[]{:S(2)}) %collective-permute-start.8) | collective-permute-done | bytes 786464 | tf_op jit(solution)/shard_map/basis_along_y/ppermute | solution.py:205
  41.8 2.6 %collective-permute-done.6.refs_4_ = f32[512,256]{1,0:T(8,128)S(1)} collective-permute-done((f32[512,256]{1,0:T(8,128)S(1)}, f32[512,256]{1,0:T(8,128)S(1)}, u32[]{:S(2)}, u32[]{:S(2)}) %collective-permute-start.6) | collective-permute-done | bytes 524320 | tf_op jit(solution)/shard_map/vectors_along_z/ppermute | solution.py:223
  45.1 1.3 collective-permute-start.3
  46.4 4.8 %collective-permute-start.11 = (f32[48,4096]{1,0:T(8,128)S(1)}, f32[48,4096]{1,0:T(8,128)S(1)}, u32[]{:S(2)}, u32[]{:S(2)}) collective-permute-start(f32[48,4096]{1,0:T(8,128)S(1)} %get-tuple-element.41), channel_id=1, source_target_pairs={{0,32},{16,48},{32,0},{48,16},{1,33},{17,49},{33,1},{49,17},{2,34}... | collective-permute-start | bytes 2359304 | tf_op jit(solution)/shard_map/basis_along_y/ppermute | solution.py:205
  51.3 9.1 %collective-permute-done.3.even.refs_4_ = f32[512,256]{1,0:T(8,128)S(1)} collective-permute-done((f32[512,256]{1,0:T(8,128)S(1)}, f32[512,256]{1,0:T(8,128)S(1)}, u32[]{:S(2)}, u32[]{:S(2)}) %collective-permute-start.3) | collective-permute-done | bytes 524320 | tf_op jit(solution)/shard_map/vectors_along_z/ppermute | solution.py:223
  61.0 1.3 collective-permute-start.10
  62.3 1.3 collective-permute-start.12
  63.6 3.1 %collective-permute-done.11.refs_2_.refs_7_.refs_12_.refs_17_.refs_22_ = f32[48,4096]{1,0:T(8,128)S(1)} collective-permute-done((f32[48,4096]{1,0:T(8,128)S(1)}, f32[48,4096]{1,0:T(8,128)S(1)}, u32[]{:S(2)}, u32[]{:S(2)}) %collective-permute-start.11) | collective-permute-done | bytes 786464 | tf_op jit(solution)/shard_map/basis_along_y/ppermute | solution.py:205
  66.6 1.7 %collective-permute-done.10.refs_4_ = f32[256,256]{1,0:T(8,128)S(1)} collective-permute-done((f32[256,256]{1,0:T(8,128)S(1)}, f32[256,256]{1,0:T(8,128)S(1)}, u32[]{:S(2)}, u32[]{:S(2)}) %collective-permute-start.10) | collective-permute-done | bytes 262176 | tf_op jit(solution)/shard_map/vectors_along_z/ppermute | solution.py:226
  68.4 1.3 collective-permute-start.15
  69.7 3.0 %collective-permute-done.12.refs_9_ = f32[256,256]{1,0:T(8,128)S(1)} collective-permute-done((f32[256,256]{1,0:T(8,128)S(1)}, f32[256,256]{1,0:T(8,128)S(1)}, u32[]{:S(2)}, u32[]{:S(2)}) %collective-permute-start.12) | collective-permute-done | bytes 262176 | tf_op jit(solution)/shard_map/vectors_along_z/ppermute | solution.py:226
  72.7 1.3 collective-permute-start.13
  74.0 1.3 %add_chunks.6.refs_10_ = f32[2,192,256]{2,1,0:T(8,128)S(1)} custom-call(s32[5]{0:T(128)S(1)} %stack.19.info, f32[48,4096]{1,0:T(8,128)S(1)} %get-tuple-element.43.refs_0_.refs_5_.refs_10_.refs_15_.refs_20_, f32[48,4096]{1,0:T(8,128)S(1)} %collective-permute-done.7.refs_1_.refs_6_.refs_11_.refs_16_.refs_21_, ...), custom_call_target="tpu_custom_call" | custom-call | flops 452984832 | bytes 4194304 | tf_op jit(solution)/shard_map/add_chunks/pallas_call | solution.py:117
  75.3 1.0 add_chunks.7.refs_10_
  79.3 1.3 collective-permute-start.16
  80.6 2.0 %collective-permute-done.13.refs_19_ = f32[256,256]{1,0:T(8,128)S(1)} collective-permute-done((f32[256,256]{1,0:T(8,128)S(1)}, f32[256,256]{1,0:T(8,128)S(1)}, u32[]{:S(2)}, u32[]{:S(2)}) %collective-permute-start.13) | collective-permute-done | bytes 262176 | tf_op jit(solution)/shard_map/vectors_along_z/ppermute | solution.py:226
  82.6 1.3 collective-permute-start.14
  83.9 5.2 %collective-permute-done.16.refs_24_ = f32[256,256]{1,0:T(8,128)S(1)} collective-permute-done((f32[256,256]{1,0:T(8,128)S(1)}, f32[256,256]{1,0:T(8,128)S(1)}, u32[]{:S(2)}, u32[]{:S(2)}) %collective-permute-start.16) | collective-permute-done | bytes 262176 | tf_op jit(solution)/shard_map/vectors_along_z/ppermute | solution.py:226
  89.1 1.9 %add_chunks.10.refs_5_ = f32[2,192,256]{2,1,0:T(8,128)S(1)} custom-call(s32[5]{0:T(128)S(1)} %stack.19.info, f32[48,4096]{1,0:T(8,128)S(1)} %get-tuple-element.43.refs_0_.refs_5_.refs_10_.refs_15_.refs_20_, f32[48,4096]{1,0:T(8,128)S(1)} %collective-permute-done.7.refs_1_.refs_6_.refs_11_.refs_16_.refs_21_, ...), custom_call_target="tpu_custom_call", output_to_operand_aliasing={{}: (26, {})} | custom-call | flops 377487360 | bytes 4194304 | tf_op jit(solution)/shard_map/add_chunks/pallas_call | solution.py:117
  91.0 3.2 %collective-permute-done.14.refs_4_ = f32[256,256]{1,0:T(8,128)S(1)} collective-permute-done((f32[256,256]{1,0:T(8,128)S(1)}, f32[256,256]{1,0:T(8,128)S(1)}, u32[]{:S(2)}, u32[]{:S(2)}) %collective-permute-start.14) | collective-permute-done | bytes 262176 | tf_op jit(solution)/shard_map/vectors_along_z/ppermute | solution.py:226
  95.2 23.0 %all_to_all.5 = f32[32,24,128]{2,1,0:T(8,128)S(1)} all-to-all(f32[32,24,128]{2,1,0:T(8,128)S(1)} %add_chunks.11), channel_id=1, replica_groups=mesh['z'=8,'y'=4,'x'=4,'half'=2,'core'=2] {'y','x','core'}, dimensions={0} | all-to-all | bytes 786432 | tf_op jit(solution)/shard_map/sum_over_columns/all_to_all | solution.py:233
  118.3 11.3 %collective-permute-start.17 = (f32[24,128]{1,0:T(8,128)S(1)}, f32[24,128]{1,0:T(8,128)S(1)}, u32[]{:S(2)}, u32[]{:S(2)}) collective-permute-start(f32[24,128]{1,0:T(8,128)S(1)} %reduce_sum.9.mine), channel_id=1, source_target_pairs={{0,2},{2,0},{1,3},{3,1},{4,6},{6,4},{5,7},{7,5},{8,10},{10,8},{9,1... | collective-permute-start | bytes 36872 | tf_op jit(solution)/shard_map/sum_over_columns/ppermute | solution.py:178
  129.7 1.8 %collective-permute-done.17.other = f32[24,128]{1,0:T(8,128)S(1)} collective-permute-done((f32[24,128]{1,0:T(8,128)S(1)}, f32[24,128]{1,0:T(8,128)S(1)}, u32[]{:S(2)}, u32[]{:S(2)}) %collective-permute-start.17) | collective-permute-done | bytes 12320 | tf_op jit(solution)/shard_map/sum_over_columns/ppermute | solution.py:178
  (20 shorter events, 8.4 us)
Async XLA Ops:
  0.0 11.7 %collective-permute-start.4 = (f32[512,256]{1,0:T(8,128)}, f32[512,256]{1,0:T(8,128)S(1)}, u32[]{:S(2)}, u32[]{:S(2)}) collective-permute-start(f32[512,256]{1,0:T(8,128)} %refs_4_.1), channel_id=1, source_target_pairs={{0,64},{128,192},{256,320},{384,448},{64,0},{192,128},{320,256},{4... | collective-permute-start | bytes 1572872 | tf_op jit(solution)/shard_map/vectors_along_z/ppermute | solution.py:223
  4.4 8.1 %collective-permute-start = (f32[512,256]{1,0:T(8,128)}, f32[512,256]{1,0:T(8,128)S(1)}, u32[]{:S(2)}, u32[]{:S(2)}) collective-permute-start(f32[512,256]{1,0:T(8,128)} %refs_4_.1), channel_id=1, source_target_pairs={{64,128},{192,256},{320,384},{128,64},{256,192},{384,320},{65,129}... | collective-permute-start | bytes 1572872 | tf_op jit(solution)/shard_map/vectors_along_z/ppermute | solution.py:223
  5.8 1.9 %copy-start = (f32[48,16384]{1,0:T(8,128)S(1)}, f32[48,16384]{1,0:T(8,128)}, u32[]{:S(2)}) copy-start(f32[48,16384]{1,0:T(8,128)} %slab) | copy-start | bytes 9437188
  7.7 66.3 %copy-start.1 = (f32[512,256]{1,0:T(8,128)S(1)}, f32[512,256]{1,0:T(8,128)}, u32[]{:S(2)}) copy-start(f32[512,256]{1,0:T(8,128)} %refs_4_.1) | copy-start | bytes 1572868
  11.7 13.4 %collective-permute-start.5 = (f32[512,256]{1,0:T(8,128)S(1)}, f32[512,256]{1,0:T(8,128)S(1)}, u32[]{:S(2)}, u32[]{:S(2)}) collective-permute-start(f32[512,256]{1,0:T(8,128)S(1)} %collective-permute-done.4.refs_9_), channel_id=1, source_target_pairs={{64,128},{192,256},{320,384},{128,64},{256,192},{384,320},{65,129}... | collective-permute-start | bytes 1572872 | tf_op jit(solution)/shard_map/vectors_along_z/ppermute | solution.py:223
  12.4 20.8 %collective-permute-start.1 = (f32[512,256]{1,0:T(8,128)S(1)}, f32[512,256]{1,0:T(8,128)S(1)}, u32[]{:S(2)}, u32[]{:S(2)}) collective-permute-start(f32[512,256]{1,0:T(8,128)S(1)} %collective-permute-done.refs_14_), channel_id=1, source_target_pairs={{128,192},{256,320},{384,448},{64,0},{192,128},{320,256},{129,193}... | collective-permute-start | bytes 1572872 | tf_op jit(solution)/shard_map/vectors_along_z/ppermute | solution.py:223
  13.7 23.1 %collective-permute-start.7 = (f32[48,4096]{1,0:T(8,128)S(1)}, f32[48,4096]{1,0:T(8,128)S(1)}, u32[]{:S(2)}, u32[]{:S(2)}) collective-permute-start(f32[48,4096]{1,0:T(8,128)S(1)} %get-tuple-element.35), channel_id=1, source_target_pairs={{0,16},{16,0},{32,48},{48,32},{1,17},{17,1},{33,49},{49,33},{2,18}... | collective-permute-start | bytes 2359304 | tf_op jit(solution)/shard_map/basis_along_y/ppermute | solution.py:205
  21.3 20.5 %collective-permute-start.8 = (f32[48,4096]{1,0:T(8,128)S(1)}, f32[48,4096]{1,0:T(8,128)S(1)}, u32[]{:S(2)}, u32[]{:S(2)}) collective-permute-start(f32[48,4096]{1,0:T(8,128)S(1)} %get-tuple-element.36), channel_id=1, source_target_pairs={{0,48},{16,32},{32,16},{48,0},{1,49},{17,33},{33,17},{49,1},{2,50}... | collective-permute-start | bytes 2359304 | tf_op jit(solution)/shard_map/basis_along_y/ppermute | solution.py:205
  25.2 19.3 %collective-permute-start.6 = (f32[512,256]{1,0:T(8,128)S(1)}, f32[512,256]{1,0:T(8,128)S(1)}, u32[]{:S(2)}, u32[]{:S(2)}) collective-permute-start(f32[512,256]{1,0:T(8,128)S(1)} %collective-permute-done.5.refs_9_), channel_id=1, source_target_pairs={{128,192},{256,320},{384,448},{64,0},{192,128},{320,256},{129,193}... | collective-permute-start | bytes 1572872 | tf_op jit(solution)/shard_map/vectors_along_z/ppermute | solution.py:223
  33.2 11.9 %collective-permute-start.2 = (f32[512,256]{1,0:T(8,128)S(1)}, f32[512,256]{1,0:T(8,128)S(1)}, u32[]{:S(2)}, u32[]{:S(2)}) collective-permute-start(f32[512,256]{1,0:T(8,128)S(1)} %collective-permute-done.1.refs_4_), channel_id=1, source_target_pairs={{192,256},{320,384},{128,64},{256,192},{193,257},{321,385},{129,65... | collective-permute-start | bytes 1572872 | tf_op jit(solution)/shard_map/vectors_along_z/ppermute | solution.py:223
  44.4 6.8 %collective-permute-start.9 = (f32[512,256]{1,0:T(8,128)S(1)}, f32[512,256]{1,0:T(8,128)S(1)}, u32[]{:S(2)}, u32[]{:S(2)}) collective-permute-start(f32[512,256]{1,0:T(8,128)S(1)} %collective-permute-done.6.refs_4_), channel_id=1, source_target_pairs={{192,256},{320,384},{128,64},{256,192},{193,257},{321,385},{129,65... | collective-permute-start | bytes 1572872 | tf_op jit(solution)/shard_map/vectors_along_z/ppermute | solution.py:223
  45.1 15.2 %collective-permute-start.3 = (f32[512,256]{1,0:T(8,128)S(1)}, f32[512,256]{1,0:T(8,128)S(1)}, u32[]{:S(2)}, u32[]{:S(2)}) collective-permute-start(f32[512,256]{1,0:T(8,128)S(1)} %collective-permute-done.2.refs_9_), channel_id=1, source_target_pairs={{256,320},{384,448},{64,0},{192,128},{257,321},{385,449},{65,1},{1... | collective-permute-start | bytes 1572872 | tf_op jit(solution)/shard_map/vectors_along_z/ppermute | solution.py:223
  46.4 20.2 %collective-permute-start.11 = (f32[48,4096]{1,0:T(8,128)S(1)}, f32[48,4096]{1,0:T(8,128)S(1)}, u32[]{:S(2)}, u32[]{:S(2)}) collective-permute-start(f32[48,4096]{1,0:T(8,128)S(1)} %get-tuple-element.41), channel_id=1, source_target_pairs={{0,32},{16,48},{32,0},{48,16},{1,33},{17,49},{33,1},{49,17},{2,34}... | collective-permute-start | bytes 2359304 | tf_op jit(solution)/shard_map/basis_along_y/ppermute | solution.py:205
  61.0 7.4 %collective-permute-start.10 = (f32[256,256]{1,0:T(8,128)S(1)}, f32[256,256]{1,0:T(8,128)S(1)}, u32[]{:S(2)}, u32[]{:S(2)}) collective-permute-start(f32[256,256]{1,0:T(8,128)S(1)} %get-tuple-element.38), channel_id=1, source_target_pairs={{256,320},{320,384},{384,448},{64,0},{128,64},{192,128},{257,321},... | collective-permute-start | bytes 786440 | tf_op jit(solution)/shard_map/vectors_along_z/ppermute | solution.py:226
  62.3 10.4 %collective-permute-start.12 = (f32[256,256]{1,0:T(8,128)S(1)}, f32[256,256]{1,0:T(8,128)S(1)}, u32[]{:S(2)}, u32[]{:S(2)}) collective-permute-start(f32[256,256]{1,0:T(8,128)S(1)} %get-tuple-element.47), channel_id=1, source_target_pairs={{256,320},{320,384},{384,448},{64,0},{128,64},{192,128},{257,321},... | collective-permute-start | bytes 786440 | tf_op jit(solution)/shard_map/vectors_along_z/ppermute | solution.py:226
  68.4 10.9 %collective-permute-start.15 = (f32[256,256]{1,0:T(8,128)S(1)}, f32[256,256]{1,0:T(8,128)S(1)}, u32[]{:S(2)}, u32[]{:S(2)}) collective-permute-start(f32[256,256]{1,0:T(8,128)S(1)} %collective-permute-done.10.refs_4_), channel_id=1, source_target_pairs={{320,384},{384,448},{64,0},{128,64},{321,385},{385,449},{65,1},{12... | collective-permute-start | bytes 786440 | tf_op jit(solution)/shard_map/vectors_along_z/ppermute | solution.py:226
  72.7 9.9 %collective-permute-start.13 = (f32[256,256]{1,0:T(8,128)S(1)}, f32[256,256]{1,0:T(8,128)S(1)}, u32[]{:S(2)}, u32[]{:S(2)}) collective-permute-start(f32[256,256]{1,0:T(8,128)S(1)} %collective-permute-done.12.refs_9_), channel_id=1, source_target_pairs={{320,384},{384,448},{64,0},{128,64},{321,385},{385,449},{65,1},{12... | collective-permute-start | bytes 786440 | tf_op jit(solution)/shard_map/vectors_along_z/ppermute | solution.py:226
  79.3 9.8 %collective-permute-start.16 = (f32[256,256]{1,0:T(8,128)S(1)}, f32[256,256]{1,0:T(8,128)S(1)}, u32[]{:S(2)}, u32[]{:S(2)}) collective-permute-start(f32[256,256]{1,0:T(8,128)S(1)} %collective-permute-done.15.refs_14_), channel_id=1, source_target_pairs={{384,448},{64,0},{385,449},{65,1},{386,450},{66,2},{387,451},{67,3... | collective-permute-start | bytes 786440 | tf_op jit(solution)/shard_map/vectors_along_z/ppermute | solution.py:226
  82.6 11.7 %collective-permute-start.14 = (f32[256,256]{1,0:T(8,128)S(1)}, f32[256,256]{1,0:T(8,128)S(1)}, u32[]{:S(2)}, u32[]{:S(2)}) collective-permute-start(f32[256,256]{1,0:T(8,128)S(1)} %collective-permute-done.13.refs_19_), channel_id=1, source_target_pairs={{384,448},{64,0},{385,449},{65,1},{386,450},{66,2},{387,451},{67,3... | collective-permute-start | bytes 786440 | tf_op jit(solution)/shard_map/vectors_along_z/ppermute | solution.py:226
  118.3 13.2 %collective-permute-start.17 = (f32[24,128]{1,0:T(8,128)S(1)}, f32[24,128]{1,0:T(8,128)S(1)}, u32[]{:S(2)}, u32[]{:S(2)}) collective-permute-start(f32[24,128]{1,0:T(8,128)S(1)} %reduce_sum.9.mine), channel_id=1, source_target_pairs={{0,2},{2,0},{1,3},{3,1},{4,6},{6,4},{5,7},{7,5},{8,10},{10,8},{9,1... | collective-permute-start | bytes 36872 | tf_op jit(solution)/shard_map/sum_over_columns/ppermute | solution.py:178

commit v9 on v8

--- a/solution.py
+++ b/solution.py
@@ -147,9 +147,9 @@
     vmem = pl.BlockSpec(memory_space=pltpu.VMEM)
     return pl.pallas_call(
         select_kernel,
-        out_shape=[jax.ShapeDtypeStruct((even.shape[0] // PARTS, even.shape[1]), F32)] * PARTS,
+        out_shape=jax.ShapeDtypeStruct(even.shape, F32),
         in_specs=[pl.BlockSpec(memory_space=pltpu.SMEM), vmem, vmem],
-        out_specs=[vmem] * PARTS,
+        out_specs=vmem,
         compiler_params=pltpu.CompilerParams(vmem_limit_bytes=4 << 20),
         name="select",
     )(info, even, odd)
@@ -174,6 +174,24 @@
     )(half, mine, other)
 
 
+def cut_kernel(vec, *outs):
+    part = outs[0].shape[0]
+    for i, out in enumerate(outs):
+        out[...] = vec[i * part : (i + 1) * part]
+
+
+def cut(vec):
+    vmem = pl.BlockSpec(memory_space=pltpu.VMEM)
+    return pl.pallas_call(
+        cut_kernel,
+        out_shape=[jax.ShapeDtypeStruct((vec.shape[0] // PARTS, vec.shape[1]), F32)] * PARTS,
+        in_specs=[vmem],
+        out_specs=[vmem] * PARTS,
+        compiler_params=pltpu.CompilerParams(vmem_limit_bytes=4 << 20),
+        name="cut",
+    )(vec)
+
+
 def shift(a, axis, size, by):
     return lax.ppermute(a, axis, [(i, (i + by) % size) for i in range(size)])
 
@@ -199,34 +217,39 @@
     basis = [packed[0], None, None, None]
     pieces = [(vectors, lambda z: z, 0)]
     for step in range(1, Z):
-        ready = {4: (1, 3), 6: (2,)}.get(step, ())
+        ready = {4: (1, 3), 7: (2,)}.get(step, ())
         for k in ready:
             with jax.named_scope("basis_along_y"):
                 basis[k] = lax.ppermute(packed[k], "y", [(i, i ^ k) for i in range(Y)])
         if step == mid + 1:
-            beyond = list(select(info, even, odd))
+            beyond = [select(info, e, o) for e, o in zip(even, odd)]
         if step == 2:
             odd, packed = lax.optimization_barrier((odd, packed))
         if ready and beyond is None:
             even, basis = lax.optimization_barrier((even, basis))
         elif ready:
             beyond[0], basis = lax.optimization_barrier((beyond[0], basis))
-        if step == Z - 1:
-            for n, m in ((0, 3), (3, 5), (5, 7), (7, 9)):
-                total = add_chunks(info, basis, pieces[n:m], total)
-            beyond[0], total = lax.optimization_barrier((beyond[0], total))
         up = [(i, i + 1) for i in range(step - 1, Z - 1)]
         down = [(i + 1, i) for i in range(Z - step)]
         with jax.named_scope("vectors_along_z"):
             if step <= mid:
                 pairs = [[p for p in up + down if min(p) % 2 == parity] for parity in range(2)]
-                even, odd = lax.ppermute(odd, "z", pairs[0]), lax.ppermute(even, "z", pairs[1])
-                pieces += [(even, turn(step), 0), (odd, turn(-step), 0)]
+                if step < mid:
+                    even, odd = lax.ppermute(odd, "z", pairs[0]), lax.ppermute(even, "z", pairs[1])
+                    pieces += [(even, turn(step), 0), (odd, turn(-step), 0)]
+                else:
+                    evens, odds = cut(even), cut(odd)
+                    even, odd = [], []
+                    for i in range(PARTS):
+                        even.append(lax.ppermute(odds[i], "z", pairs[0]))
+                        odd.append(lax.ppermute(evens[i], "z", pairs[1]))
+                        pieces += [(even[i], turn(step), i), (odd[i], turn(-step), i)]
             else:
                 beyond = [lax.ppermute(b, "z", up + down) for b in beyond]
                 pieces += [(b, far(step), i) for i, b in enumerate(beyond)]
 
-    total = add_chunks(info, basis, pieces[9:-1], total)
+    for n, m in ((0, 3), (3, 5), (5, 7), (7, 11), (11, -1)):
+        total = add_chunks(info, basis, pieces[n:m], total)
     total = add_chunks(info, basis, pieces[-1:], total, last=True)
 
     with jax.named_scope("sum_over_columns"):

time: 133 us -> 132 us (level)
  starting transfers between devices: 46.2 us -> 49.2 us
  blocking collectives: 23 us -> 20.5 us
  waiting for transfers between devices: 51.2 us -> 48.8 us
    ppermute x4 -> x3, waiting for transfers between devices: 22.2 us -> 13.2 us  [local(): lax.ppermute(odd, 'z', pairs[0])]
    ppermute x0 -> x4, waiting for transfers between devices: none -> 7.38 us  [the longest x2 7.38 us: local(): even.append(lax.ppermute(odds[i], 'z', pairs[0]))]
    ppermute x0 -> x4, starting transfers between devices: none -> 3.94 us  [the longest x2 2.58 us: local(): even.append(lax.ppermute(odds[i], 'z', pairs[0]))]
    ppermute x6, waiting for transfers between devices: 16.1 us -> 19.2 us  [local(): beyond = [lax.ppermute(b, 'z', up + down) for b in beyond]]
    ppermute x3, waiting for transfers between devices: 11 us -> 7.96 us  [local(): basis[k] = lax.ppermute(packed[k], 'y', [(i, i ^ k) for i in range(Y)])]
    all_to_all x1, blocking collectives: 23 us -> 20.5 us  [local(): got = lax.all_to_all(total, ('y', 'x', 'core'), 0, 0, tiled=True)]
    ppermute x4 -> x3, starting transfers between devices: 8.24 us -> 6.95 us  [local(): lax.ppermute(odd, 'z', pairs[0])]
    ppermute x4 -> x3, starting transfers between devices: 2.74 us -> 2.06 us  [local(): lax.ppermute(even, 'z', pairs[1])]
  transfers between devices with their start and end apart: 18 -> 20, of which waited for: 14 -> 13; matrix products, arithmetic and copies ran while one was open for 0% -> 0% of each run, Pallas kernels for 5% -> 6%
where the time goes in v9:
time: 132 us; the launch traced here: 131 us
  starting transfers between devices  49.2 us (37%)
  waiting for transfers between devices  48.8 us (37%)
  blocking collectives  20.5 us (16%)
  Pallas kernels  9.75 us (7%)
  local copies, waits for them, and re-layouts  1.98 us (2%)
    all_to_all x1, blocking collectives, local(): got = lax.all_to_all(total, ('y', 'x', 'core'), 0, 0, tiled=True)  20.5 us
    ppermute x6, waiting for transfers between devices, local(): beyond = [lax.ppermute(b, 'z', up + down) for b in beyond]  19.2 us
    ppermute x3, starting transfers between devices, local(): basis[k] = lax.ppermute(packed[k], 'y', [(i, i ^ k) for i in range(Y)])  16.2 us
    ppermute x3, waiting for transfers between devices, local(): lax.ppermute(odd, 'z', pairs[0])  13.2 us
    ppermute x1, starting transfers between devices, shift(): return lax.ppermute(a, axis, [(i, (i + by) % size) for i in range(size)])  12.3 us
    ppermute x3, waiting for transfers between devices, local(): basis[k] = lax.ppermute(packed[k], 'y', [(i, i ^ k) for i in range(Y)])  7.96 us
    ppermute x6, starting transfers between devices, local(): beyond = [lax.ppermute(b, 'z', up + down) for b in beyond]  7.71 us
    pallas_call x6, Pallas kernels, add_chunks(): pl.pallas_call(functools.partial(add_kernel, sources, total is None, last...  7.51 us
  transfers between devices with their start and end apart: 20, of which 13 were waited for; matrix products, arithmetic and copies ran while one was open for 0% of the time, Pallas kernels for 6%

profile of v9, /device:TPU:1, one launch (start us, length us, event | category | flops | bytes accessed | tf_op | source)
XLA Modules:
  0.0 131.1 jit_solution(10811731518898908464)
XLA Ops:
  0.0 4.4 %collective-permute-start.4 = (f32[512,256]{1,0:T(8,128)}, f32[512,256]{1,0:T(8,128)S(1)}, u32[]{:S(2)}, u32[]{:S(2)}) collective-permute-start(f32[512,256]{1,0:T(8,128)} %refs_4_.1), channel_id=1, source_target_pairs={{0,64},{128,192},{256,320},{384,448},{64,0},{192,128},{320,256},{4... | collective-permute-start | bytes 1572872 | tf_op jit(solution)/shard_map/vectors_along_z/ppermute | solution.py:238
  5.8 1.9 %copy-done = f32[48,16384]{1,0:T(8,128)S(1)} copy-done((f32[48,16384]{1,0:T(8,128)S(1)}, f32[48,16384]{1,0:T(8,128)}, u32[]{:S(2)}) %copy-start) | copy-done | bytes 3145752
  7.9 3.8 %collective-permute-done.4.refs_9_ = f32[512,256]{1,0:T(8,128)S(1)} collective-permute-done((f32[512,256]{1,0:T(8,128)}, f32[512,256]{1,0:T(8,128)S(1)}, u32[]{:S(2)}, u32[]{:S(2)}) %collective-permute-start.4) | collective-permute-done | bytes 524320 | tf_op jit(solution)/shard_map/vectors_along_z/ppermute | solution.py:238
  12.4 1.3 collective-permute-start.1
  13.7 7.6 %collective-permute-start.7 = (f32[48,4096]{1,0:T(8,128)S(1)}, f32[48,4096]{1,0:T(8,128)S(1)}, u32[]{:S(2)}, u32[]{:S(2)}) collective-permute-start(f32[48,4096]{1,0:T(8,128)S(1)} %get-tuple-element.36), channel_id=1, source_target_pairs={{0,16},{16,0},{32,48},{48,32},{1,17},{17,1},{33,49},{49,33},{2,18}... | collective-permute-start | bytes 2359304 | tf_op jit(solution)/shard_map/basis_along_y/ppermute | solution.py:223
  21.3 3.8 %collective-permute-start.8 = (f32[48,4096]{1,0:T(8,128)S(1)}, f32[48,4096]{1,0:T(8,128)S(1)}, u32[]{:S(2)}, u32[]{:S(2)}) collective-permute-start(f32[48,4096]{1,0:T(8,128)S(1)} %get-tuple-element.37), channel_id=1, source_target_pairs={{0,48},{16,32},{32,16},{48,0},{1,49},{17,33},{33,17},{49,1},{2,50}... | collective-permute-start | bytes 2359304 | tf_op jit(solution)/shard_map/basis_along_y/ppermute | solution.py:223
  25.2 1.3 collective-permute-start.6
  26.5 6.7 %collective-permute-done.1.refs_4_ = f32[512,256]{1,0:T(8,128)S(1)} collective-permute-done((f32[512,256]{1,0:T(8,128)S(1)}, f32[512,256]{1,0:T(8,128)S(1)}, u32[]{:S(2)}, u32[]{:S(2)}) %collective-permute-start.1) | collective-permute-done | bytes 524320 | tf_op jit(solution)/shard_map/vectors_along_z/ppermute | solution.py:238
  33.9 2.9 %collective-permute-done.7.refs_1_.refs_6_.refs_11_.refs_16_.refs_21_ = f32[48,4096]{1,0:T(8,128)S(1)} collective-permute-done((f32[48,4096]{1,0:T(8,128)S(1)}, f32[48,4096]{1,0:T(8,128)S(1)}, u32[]{:S(2)}, u32[]{:S(2)}) %collective-permute-start.7) | collective-permute-done | bytes 786464 | tf_op jit(solution)/shard_map/basis_along_y/ppermute | solution.py:223
  36.8 5.0 %collective-permute-done.8.refs_3_.refs_8_.refs_13_.refs_18_.refs_23_ = f32[48,4096]{1,0:T(8,128)S(1)} collective-permute-done((f32[48,4096]{1,0:T(8,128)S(1)}, f32[48,4096]{1,0:T(8,128)S(1)}, u32[]{:S(2)}, u32[]{:S(2)}) %collective-permute-start.8) | collective-permute-done | bytes 786464 | tf_op jit(solution)/shard_map/basis_along_y/ppermute | solution.py:223
  41.8 2.6 %collective-permute-done.6.vec.refs_4_ = f32[512,256]{1,0:T(8,128)S(1)} collective-permute-done((f32[512,256]{1,0:T(8,128)S(1)}, f32[512,256]{1,0:T(8,128)S(1)}, u32[]{:S(2)}, u32[]{:S(2)}) %collective-permute-start.6) | collective-permute-done | bytes 524320 | tf_op jit(solution)/shard_map/vectors_along_z/ppermute | solution.py:238
  45.2 1.3 collective-permute-start.3
  46.5 4.8 %collective-permute-start.12 = (f32[48,4096]{1,0:T(8,128)S(1)}, f32[48,4096]{1,0:T(8,128)S(1)}, u32[]{:S(2)}, u32[]{:S(2)}) collective-permute-start(f32[48,4096]{1,0:T(8,128)S(1)} %get-tuple-element.42), channel_id=1, source_target_pairs={{0,32},{16,48},{32,0},{48,16},{1,33},{17,49},{33,1},{49,17},{2,34}... | collective-permute-start | bytes 2359304 | tf_op jit(solution)/shard_map/basis_along_y/ppermute | solution.py:223
  52.0 1.3 collective-permute-start.13
  53.3 1.5 %collective-permute-done.3.even.refs_4_ = f32[256,256]{1,0:T(8,128)S(1)} collective-permute-done((f32[256,256]{1,0:T(8,128)S(1)}, f32[256,256]{1,0:T(8,128)S(1)}, u32[]{:S(2)}, u32[]{:S(2)}) %collective-permute-start.3) | collective-permute-done | bytes 262176 | tf_op jit(solution)/shard_map/vectors_along_z/ppermute | solution.py:244
  55.4 1.3 collective-permute-start.10
  56.8 5.8 %collective-permute-done.13.even.refs_14_ = f32[256,256]{1,0:T(8,128)S(1)} collective-permute-done((f32[256,256]{1,0:T(8,128)S(1)}, f32[256,256]{1,0:T(8,128)S(1)}, u32[]{:S(2)}, u32[]{:S(2)}) %collective-permute-start.13) | collective-permute-done | bytes 262176 | tf_op jit(solution)/shard_map/vectors_along_z/ppermute | solution.py:244
  63.2 1.3 collective-permute-start.15
  64.5 2.9 %collective-permute-done.10.refs_4_ = f32[256,256]{1,0:T(8,128)S(1)} collective-permute-done((f32[256,256]{1,0:T(8,128)S(1)}, f32[256,256]{1,0:T(8,128)S(1)}, u32[]{:S(2)}, u32[]{:S(2)}) %collective-permute-start.10) | collective-permute-done | bytes 262176 | tf_op jit(solution)/shard_map/vectors_along_z/ppermute | solution.py:248
  67.4 1.3 collective-permute-start.11
  68.7 4.8 %collective-permute-done.15.refs_9_ = f32[256,256]{1,0:T(8,128)S(1)} collective-permute-done((f32[256,256]{1,0:T(8,128)S(1)}, f32[256,256]{1,0:T(8,128)S(1)}, u32[]{:S(2)}, u32[]{:S(2)}) %collective-permute-start.15) | collective-permute-done | bytes 262176 | tf_op jit(solution)/shard_map/vectors_along_z/ppermute | solution.py:248
  73.5 1.3 collective-permute-start.16
  74.8 3.9 %collective-permute-done.11.refs_14_ = f32[256,256]{1,0:T(8,128)S(1)} collective-permute-done((f32[256,256]{1,0:T(8,128)S(1)}, f32[256,256]{1,0:T(8,128)S(1)}, u32[]{:S(2)}, u32[]{:S(2)}) %collective-permute-start.11) | collective-permute-done | bytes 262176 | tf_op jit(solution)/shard_map/vectors_along_z/ppermute | solution.py:248
  78.7 1.3 collective-permute-start.18
  80.0 4.6 %collective-permute-done.16.refs_19_ = f32[256,256]{1,0:T(8,128)S(1)} collective-permute-done((f32[256,256]{1,0:T(8,128)S(1)}, f32[256,256]{1,0:T(8,128)S(1)}, u32[]{:S(2)}, u32[]{:S(2)}) %collective-permute-start.16) | collective-permute-done | bytes 262176 | tf_op jit(solution)/shard_map/vectors_along_z/ppermute | solution.py:248
  84.5 1.3 collective-permute-start.17
  85.8 1.3 %add_chunks.6.refs_10_ = f32[2,192,256]{2,1,0:T(8,128)S(1)} custom-call(s32[5]{0:T(128)S(1)} %stack.19.info, f32[48,4096]{1,0:T(8,128)S(1)} %get-tuple-element.44.refs_0_.refs_5_.refs_10_.refs_15_.refs_20_, f32[48,4096]{1,0:T(8,128)S(1)} %collective-permute-done.7.refs_1_.refs_6_.refs_11_.refs_16_.refs_21_, ...), custom_call_target="tpu_custom_call" | custom-call | flops 452984832 | bytes 4194304 | tf_op jit(solution)/shard_map/add_chunks/pallas_call | solution.py:117
  89.2 1.2 add_chunks.9.refs_25_
  90.4 2.0 %add_chunks.10.refs_5_ = f32[2,192,256]{2,1,0:T(8,128)S(1)} custom-call(s32[5]{0:T(128)S(1)} %stack.19.info, f32[48,4096]{1,0:T(8,128)S(1)} %get-tuple-element.44.refs_0_.refs_5_.refs_10_.refs_15_.refs_20_, f32[48,4096]{1,0:T(8,128)S(1)} %collective-permute-done.7.refs_1_.refs_6_.refs_11_.refs_16_.refs_21_, ...), custom_call_target="tpu_custom_call", output_to_operand_aliasing={{}: (26, {})} | custom-call | flops 377487360 | bytes 4194304 | tf_op jit(solution)/shard_map/add_chunks/pallas_call | solution.py:117
  92.4 3.0 %collective-permute-done.17.refs_4_ = f32[256,256]{1,0:T(8,128)S(1)} collective-permute-done((f32[256,256]{1,0:T(8,128)S(1)}, f32[256,256]{1,0:T(8,128)S(1)}, u32[]{:S(2)}, u32[]{:S(2)}) %collective-permute-start.17) | collective-permute-done | bytes 262176 | tf_op jit(solution)/shard_map/vectors_along_z/ppermute | solution.py:248
  96.4 20.5 %all_to_all.5 = f32[32,24,128]{2,1,0:T(8,128)S(1)} all-to-all(f32[32,24,128]{2,1,0:T(8,128)S(1)} %add_chunks.11), channel_id=1, replica_groups=mesh['z'=8,'y'=4,'x'=4,'half'=2,'core'=2] {'y','x','core'}, dimensions={0} | all-to-all | bytes 786432 | tf_op jit(solution)/shard_map/sum_over_columns/all_to_all | solution.py:256
  116.9 12.3 %collective-permute-start.19 = (f32[24,128]{1,0:T(8,128)S(1)}, f32[24,128]{1,0:T(8,128)S(1)}, u32[]{:S(2)}, u32[]{:S(2)}) collective-permute-start(f32[24,128]{1,0:T(8,128)S(1)} %reduce_sum.9.mine), channel_id=1, source_target_pairs={{0,2},{2,0},{1,3},{3,1},{4,6},{6,4},{5,7},{7,5},{8,10},{10,8},{9,1... | collective-permute-start | bytes 36872 | tf_op jit(solution)/shard_map/sum_over_columns/ppermute | solution.py:196
  (27 shorter events, 9.9 us)
Async XLA Ops:
  0.0 11.7 %collective-permute-start.4 = (f32[512,256]{1,0:T(8,128)}, f32[512,256]{1,0:T(8,128)S(1)}, u32[]{:S(2)}, u32[]{:S(2)}) collective-permute-start(f32[512,256]{1,0:T(8,128)} %refs_4_.1), channel_id=1, source_target_pairs={{0,64},{128,192},{256,320},{384,448},{64,0},{192,128},{320,256},{4... | collective-permute-start | bytes 1572872 | tf_op jit(solution)/shard_map/vectors_along_z/ppermute | solution.py:238
  4.4 8.1 %collective-permute-start = (f32[512,256]{1,0:T(8,128)}, f32[512,256]{1,0:T(8,128)S(1)}, u32[]{:S(2)}, u32[]{:S(2)}) collective-permute-start(f32[512,256]{1,0:T(8,128)} %refs_4_.1), channel_id=1, source_target_pairs={{64,128},{192,256},{320,384},{128,64},{256,192},{384,320},{65,129}... | collective-permute-start | bytes 1572872 | tf_op jit(solution)/shard_map/vectors_along_z/ppermute | solution.py:238
  5.8 1.9 %copy-start = (f32[48,16384]{1,0:T(8,128)S(1)}, f32[48,16384]{1,0:T(8,128)}, u32[]{:S(2)}) copy-start(f32[48,16384]{1,0:T(8,128)} %slab) | copy-start | bytes 9437188
  7.7 78.1 %copy-start.1 = (f32[512,256]{1,0:T(8,128)S(1)}, f32[512,256]{1,0:T(8,128)}, u32[]{:S(2)}) copy-start(f32[512,256]{1,0:T(8,128)} %refs_4_.1) | copy-start | bytes 1572868
  11.7 13.4 %collective-permute-start.5 = (f32[512,256]{1,0:T(8,128)S(1)}, f32[512,256]{1,0:T(8,128)S(1)}, u32[]{:S(2)}, u32[]{:S(2)}) collective-permute-start(f32[512,256]{1,0:T(8,128)S(1)} %collective-permute-done.4.refs_9_), channel_id=1, source_target_pairs={{64,128},{192,256},{320,384},{128,64},{256,192},{384,320},{65,129}... | collective-permute-start | bytes 1572872 | tf_op jit(solution)/shard_map/vectors_along_z/ppermute | solution.py:238
  12.4 20.8 %collective-permute-start.1 = (f32[512,256]{1,0:T(8,128)S(1)}, f32[512,256]{1,0:T(8,128)S(1)}, u32[]{:S(2)}, u32[]{:S(2)}) collective-permute-start(f32[512,256]{1,0:T(8,128)S(1)} %collective-permute-done.refs_14_), channel_id=1, source_target_pairs={{128,192},{256,320},{384,448},{64,0},{192,128},{320,256},{129,193}... | collective-permute-start | bytes 1572872 | tf_op jit(solution)/shard_map/vectors_along_z/ppermute | solution.py:238
  13.7 23.1 %collective-permute-start.7 = (f32[48,4096]{1,0:T(8,128)S(1)}, f32[48,4096]{1,0:T(8,128)S(1)}, u32[]{:S(2)}, u32[]{:S(2)}) collective-permute-start(f32[48,4096]{1,0:T(8,128)S(1)} %get-tuple-element.36), channel_id=1, source_target_pairs={{0,16},{16,0},{32,48},{48,32},{1,17},{17,1},{33,49},{49,33},{2,18}... | collective-permute-start | bytes 2359304 | tf_op jit(solution)/shard_map/basis_along_y/ppermute | solution.py:223
  21.3 20.5 %collective-permute-start.8 = (f32[48,4096]{1,0:T(8,128)S(1)}, f32[48,4096]{1,0:T(8,128)S(1)}, u32[]{:S(2)}, u32[]{:S(2)}) collective-permute-start(f32[48,4096]{1,0:T(8,128)S(1)} %get-tuple-element.37), channel_id=1, source_target_pairs={{0,48},{16,32},{32,16},{48,0},{1,49},{17,33},{33,17},{49,1},{2,50}... | collective-permute-start | bytes 2359304 | tf_op jit(solution)/shard_map/basis_along_y/ppermute | solution.py:223
  25.2 19.3 %collective-permute-start.6 = (f32[512,256]{1,0:T(8,128)S(1)}, f32[512,256]{1,0:T(8,128)S(1)}, u32[]{:S(2)}, u32[]{:S(2)}) collective-permute-start(f32[512,256]{1,0:T(8,128)S(1)} %collective-permute-done.5.refs_9_), channel_id=1, source_target_pairs={{128,192},{256,320},{384,448},{64,0},{192,128},{320,256},{129,193}... | collective-permute-start | bytes 1572872 | tf_op jit(solution)/shard_map/vectors_along_z/ppermute | solution.py:238
  33.2 12.0 %collective-permute-start.2 = (f32[512,256]{1,0:T(8,128)S(1)}, f32[512,256]{1,0:T(8,128)S(1)}, u32[]{:S(2)}, u32[]{:S(2)}) collective-permute-start(f32[512,256]{1,0:T(8,128)S(1)} %collective-permute-done.1.refs_4_), channel_id=1, source_target_pairs={{192,256},{320,384},{128,64},{256,192},{193,257},{321,385},{129,65... | collective-permute-start | bytes 1572872 | tf_op jit(solution)/shard_map/vectors_along_z/ppermute | solution.py:238
  44.5 8.9 %collective-permute-start.9 = (f32[256,256]{1,0:T(8,128)S(1)}, f32[256,256]{1,0:T(8,128)S(1)}, u32[]{:S(2)}, u32[]{:S(2)}) collective-permute-start(f32[256,256]{1,0:T(8,128)S(1)} %get-tuple-element.39), channel_id=1, source_target_pairs={{192,256},{320,384},{128,64},{256,192},{193,257},{321,385},{129,65... | collective-permute-start | bytes 786440 | tf_op jit(solution)/shard_map/vectors_along_z/ppermute | solution.py:245
  45.2 9.7 %collective-permute-start.3 = (f32[256,256]{1,0:T(8,128)S(1)}, f32[256,256]{1,0:T(8,128)S(1)}, u32[]{:S(2)}, u32[]{:S(2)}) collective-permute-start(f32[256,256]{1,0:T(8,128)S(1)} %get-tuple-element.35), channel_id=1, source_target_pairs={{256,320},{384,448},{64,0},{192,128},{257,321},{385,449},{65,1},{1... | collective-permute-start | bytes 786440 | tf_op jit(solution)/shard_map/vectors_along_z/ppermute | solution.py:244
  46.5 28.2 %collective-permute-start.12 = (f32[48,4096]{1,0:T(8,128)S(1)}, f32[48,4096]{1,0:T(8,128)S(1)}, u32[]{:S(2)}, u32[]{:S(2)}) collective-permute-start(f32[48,4096]{1,0:T(8,128)S(1)} %get-tuple-element.42), channel_id=1, source_target_pairs={{0,32},{16,48},{32,0},{48,16},{1,33},{17,49},{33,1},{49,17},{2,34}... | collective-permute-start | bytes 2359304 | tf_op jit(solution)/shard_map/basis_along_y/ppermute | solution.py:223
  51.3 5.4 %collective-permute-start.14 = (f32[256,256]{1,0:T(8,128)S(1)}, f32[256,256]{1,0:T(8,128)S(1)}, u32[]{:S(2)}, u32[]{:S(2)}) collective-permute-start(f32[256,256]{1,0:T(8,128)S(1)} %get-tuple-element.49), channel_id=1, source_target_pairs={{192,256},{320,384},{128,64},{256,192},{193,257},{321,385},{129,65... | collective-permute-start | bytes 786440 | tf_op jit(solution)/shard_map/vectors_along_z/ppermute | solution.py:245
  52.0 10.6 %collective-permute-start.13 = (f32[256,256]{1,0:T(8,128)S(1)}, f32[256,256]{1,0:T(8,128)S(1)}, u32[]{:S(2)}, u32[]{:S(2)}) collective-permute-start(f32[256,256]{1,0:T(8,128)S(1)} %get-tuple-element.48), channel_id=1, source_target_pairs={{256,320},{384,448},{64,0},{192,128},{257,321},{385,449},{65,1},{1... | collective-permute-start | bytes 786440 | tf_op jit(solution)/shard_map/vectors_along_z/ppermute | solution.py:244
  55.4 12.0 %collective-permute-start.10 = (f32[256,256]{1,0:T(8,128)S(1)}, f32[256,256]{1,0:T(8,128)S(1)}, u32[]{:S(2)}, u32[]{:S(2)}) collective-permute-start(f32[256,256]{1,0:T(8,128)S(1)} %select.2), channel_id=1, source_target_pairs={{256,320},{320,384},{384,448},{64,0},{128,64},{192,128},{257,321},... | collective-permute-start | bytes 786440 | tf_op jit(solution)/shard_map/vectors_along_z/ppermute | solution.py:248
  63.2 10.3 %collective-permute-start.15 = (f32[256,256]{1,0:T(8,128)S(1)}, f32[256,256]{1,0:T(8,128)S(1)}, u32[]{:S(2)}, u32[]{:S(2)}) collective-permute-start(f32[256,256]{1,0:T(8,128)S(1)} %select.3), channel_id=1, source_target_pairs={{256,320},{320,384},{384,448},{64,0},{128,64},{192,128},{257,321},... | collective-permute-start | bytes 786440 | tf_op jit(solution)/shard_map/vectors_along_z/ppermute | solution.py:248
  67.4 11.2 %collective-permute-start.11 = (f32[256,256]{1,0:T(8,128)S(1)}, f32[256,256]{1,0:T(8,128)S(1)}, u32[]{:S(2)}, u32[]{:S(2)}) collective-permute-start(f32[256,256]{1,0:T(8,128)S(1)} %collective-permute-done.10.refs_4_), channel_id=1, source_target_pairs={{320,384},{384,448},{64,0},{128,64},{321,385},{385,449},{65,1},{12... | collective-permute-start | bytes 786440 | tf_op jit(solution)/shard_map/vectors_along_z/ppermute | solution.py:248
  73.5 11.0 %collective-permute-start.16 = (f32[256,256]{1,0:T(8,128)S(1)}, f32[256,256]{1,0:T(8,128)S(1)}, u32[]{:S(2)}, u32[]{:S(2)}) collective-permute-start(f32[256,256]{1,0:T(8,128)S(1)} %collective-permute-done.15.refs_9_), channel_id=1, source_target_pairs={{320,384},{384,448},{64,0},{128,64},{321,385},{385,449},{65,1},{12... | collective-permute-start | bytes 786440 | tf_op jit(solution)/shard_map/vectors_along_z/ppermute | solution.py:248
  78.7 11.7 %collective-permute-start.18 = (f32[256,256]{1,0:T(8,128)S(1)}, f32[256,256]{1,0:T(8,128)S(1)}, u32[]{:S(2)}, u32[]{:S(2)}) collective-permute-start(f32[256,256]{1,0:T(8,128)S(1)} %collective-permute-done.11.refs_14_), channel_id=1, source_target_pairs={{384,448},{64,0},{385,449},{65,1},{386,450},{66,2},{387,451},{67,3... | collective-permute-start | bytes 786440 | tf_op jit(solution)/shard_map/vectors_along_z/ppermute | solution.py:248
  84.5 10.9 %collective-permute-start.17 = (f32[256,256]{1,0:T(8,128)S(1)}, f32[256,256]{1,0:T(8,128)S(1)}, u32[]{:S(2)}, u32[]{:S(2)}) collective-permute-start(f32[256,256]{1,0:T(8,128)S(1)} %collective-permute-done.16.refs_19_), channel_id=1, source_target_pairs={{384,448},{64,0},{385,449},{65,1},{386,450},{66,2},{387,451},{67,3... | collective-permute-start | bytes 786440 | tf_op jit(solution)/shard_map/vectors_along_z/ppermute | solution.py:248
  116.9 13.4 %collective-permute-start.19 = (f32[24,128]{1,0:T(8,128)S(1)}, f32[24,128]{1,0:T(8,128)S(1)}, u32[]{:S(2)}, u32[]{:S(2)}) collective-permute-start(f32[24,128]{1,0:T(8,128)S(1)} %reduce_sum.9.mine), channel_id=1, source_target_pairs={{0,2},{2,0},{1,3},{3,1},{4,6},{6,4},{5,7},{7,5},{8,10},{10,8},{9,1... | collective-permute-start | bytes 36872 | tf_op jit(solution)/shard_map/sum_over_columns/ppermute | solution.py:196

commit v10 on v9

--- a/solution.py
+++ b/solution.py
@@ -248,7 +248,7 @@
                 beyond = [lax.ppermute(b, "z", up + down) for b in beyond]
                 pieces += [(b, far(step), i) for i, b in enumerate(beyond)]
 
-    for n, m in ((0, 3), (3, 5), (5, 7), (7, 11), (11, -1)):
+    for n, m in ((0, 5), (5, 11), (11, -1)):
         total = add_chunks(info, basis, pieces[n:m], total)
     total = add_chunks(info, basis, pieces[-1:], total, last=True)
 

time: 132 us -> 132 us (level)
    pallas_call x6 -> x4, Pallas kernels: 7.51 us -> 6.35 us  [add_chunks(): pl.pallas_call(functools.partial(add_kernel, sources, total is None, last...]
  transfers between devices with their start and end apart: 20 -> 20, of which waited for: 13 -> 14; matrix products, arithmetic and copies ran while one was open for 0% -> 0% of each run, Pallas kernels for 6% -> 5%
where the time goes in v10:
time: 132 us; the launch traced here: 131 us
  waiting for transfers between devices  49.9 us (38%)
  starting transfers between devices  49.2 us (37%)
  blocking collectives  20.5 us (16%)
  Pallas kernels  8.59 us (7%)
  local copies, waits for them, and re-layouts  1.98 us (2%)
    all_to_all x1, blocking collectives, local(): got = lax.all_to_all(total, ('y', 'x', 'core'), 0, 0, tiled=True)  20.5 us
    ppermute x6, waiting for transfers between devices, local(): beyond = [lax.ppermute(b, 'z', up + down) for b in beyond]  20.4 us
    ppermute x3, starting transfers between devices, local(): basis[k] = lax.ppermute(packed[k], 'y', [(i, i ^ k) for i in range(Y)])  16.2 us
    ppermute x3, waiting for transfers between devices, local(): lax.ppermute(odd, 'z', pairs[0])  13.2 us
    ppermute x1, starting transfers between devices, shift(): return lax.ppermute(a, axis, [(i, (i + by) % size) for i in range(size)])  12.3 us
    ppermute x3, waiting for transfers between devices, local(): basis[k] = lax.ppermute(packed[k], 'y', [(i, i ^ k) for i in range(Y)])  7.96 us
    ppermute x6, starting transfers between devices, local(): beyond = [lax.ppermute(b, 'z', up + down) for b in beyond]  7.71 us
    ppermute x2, waiting for transfers between devices, local(): even.append(lax.ppermute(odds[i], 'z', pairs[0]))  7.38 us
  transfers between devices with their start and end apart: 20, of which 14 were waited for; matrix products, arithmetic and copies ran while one was open for 0% of the time, Pallas kernels for 5%

profile of v10, /device:TPU:1, one launch (start us, length us, event | category | flops | bytes accessed | tf_op | source)
XLA Modules:
  0.0 131.1 jit_solution(2730781718068797050)
XLA Ops:
  0.0 4.4 %collective-permute-start.4 = (f32[512,256]{1,0:T(8,128)}, f32[512,256]{1,0:T(8,128)S(1)}, u32[]{:S(2)}, u32[]{:S(2)}) collective-permute-start(f32[512,256]{1,0:T(8,128)} %refs_4_.1), channel_id=1, source_target_pairs={{0,64},{128,192},{256,320},{384,448},{64,0},{192,128},{320,256},{4... | collective-permute-start | bytes 1572872 | tf_op jit(solution)/shard_map/vectors_along_z/ppermute | solution.py:238
  5.8 1.9 %copy-done = f32[48,16384]{1,0:T(8,128)S(1)} copy-done((f32[48,16384]{1,0:T(8,128)S(1)}, f32[48,16384]{1,0:T(8,128)}, u32[]{:S(2)}) %copy-start) | copy-done | bytes 3145752
  7.9 3.8 %collective-permute-done.4.refs_9_ = f32[512,256]{1,0:T(8,128)S(1)} collective-permute-done((f32[512,256]{1,0:T(8,128)}, f32[512,256]{1,0:T(8,128)S(1)}, u32[]{:S(2)}, u32[]{:S(2)}) %collective-permute-start.4) | collective-permute-done | bytes 524320 | tf_op jit(solution)/shard_map/vectors_along_z/ppermute | solution.py:238
  12.4 1.3 collective-permute-start.1
  13.7 7.6 %collective-permute-start.7 = (f32[48,4096]{1,0:T(8,128)S(1)}, f32[48,4096]{1,0:T(8,128)S(1)}, u32[]{:S(2)}, u32[]{:S(2)}) collective-permute-start(f32[48,4096]{1,0:T(8,128)S(1)} %get-tuple-element.36), channel_id=1, source_target_pairs={{0,16},{16,0},{32,48},{48,32},{1,17},{17,1},{33,49},{49,33},{2,18}... | collective-permute-start | bytes 2359304 | tf_op jit(solution)/shard_map/basis_along_y/ppermute | solution.py:223
  21.3 3.8 %collective-permute-start.8 = (f32[48,4096]{1,0:T(8,128)S(1)}, f32[48,4096]{1,0:T(8,128)S(1)}, u32[]{:S(2)}, u32[]{:S(2)}) collective-permute-start(f32[48,4096]{1,0:T(8,128)S(1)} %get-tuple-element.37), channel_id=1, source_target_pairs={{0,48},{16,32},{32,16},{48,0},{1,49},{17,33},{33,17},{49,1},{2,50}... | collective-permute-start | bytes 2359304 | tf_op jit(solution)/shard_map/basis_along_y/ppermute | solution.py:223
  25.2 1.3 collective-permute-start.6
  26.5 6.7 %collective-permute-done.1.refs_19_ = f32[512,256]{1,0:T(8,128)S(1)} collective-permute-done((f32[512,256]{1,0:T(8,128)S(1)}, f32[512,256]{1,0:T(8,128)S(1)}, u32[]{:S(2)}, u32[]{:S(2)}) %collective-permute-start.1) | collective-permute-done | bytes 524320 | tf_op jit(solution)/shard_map/vectors_along_z/ppermute | solution.py:238
  33.9 2.9 %collective-permute-done.7.refs_1_.refs_6_.refs_11_.refs_16_.refs_21_.refs_26_ = f32[48,4096]{1,0:T(8,128)S(1)} collective-permute-done((f32[48,4096]{1,0:T(8,128)S(1)}, f32[48,4096]{1,0:T(8,128)S(1)}, u32[]{:S(2)}, u32[]{:S(2)}) %collective-permute-start.7) | collective-permute-done | bytes 786464 | tf_op jit(solution)/shard_map/basis_along_y/ppermute | solution.py:223
  36.8 5.0 %collective-permute-done.8.refs_3_.refs_8_.refs_13_.refs_18_.refs_23_.refs_28_ = f32[48,4096]{1,0:T(8,128)S(1)} collective-permute-done((f32[48,4096]{1,0:T(8,128)S(1)}, f32[48,4096]{1,0:T(8,128)S(1)}, u32[]{:S(2)}, u32[]{:S(2)}) %collective-permute-start.8) | collective-permute-done | bytes 786464 | tf_op jit(solution)/shard_map/basis_along_y/ppermute | solution.py:223
  41.8 2.6 %collective-permute-done.6.vec.refs_4_ = f32[512,256]{1,0:T(8,128)S(1)} collective-permute-done((f32[512,256]{1,0:T(8,128)S(1)}, f32[512,256]{1,0:T(8,128)S(1)}, u32[]{:S(2)}, u32[]{:S(2)}) %collective-permute-start.6) | collective-permute-done | bytes 524320 | tf_op jit(solution)/shard_map/vectors_along_z/ppermute | solution.py:238
  45.2 1.3 collective-permute-start.3
  46.5 4.8 %collective-permute-start.12 = (f32[48,4096]{1,0:T(8,128)S(1)}, f32[48,4096]{1,0:T(8,128)S(1)}, u32[]{:S(2)}, u32[]{:S(2)}) collective-permute-start(f32[48,4096]{1,0:T(8,128)S(1)} %get-tuple-element.42), channel_id=1, source_target_pairs={{0,32},{16,48},{32,0},{48,16},{1,33},{17,49},{33,1},{49,17},{2,34}... | collective-permute-start | bytes 2359304 | tf_op jit(solution)/shard_map/basis_along_y/ppermute | solution.py:223
  52.0 1.3 collective-permute-start.13
  53.3 1.5 %collective-permute-done.3.even.refs_14_ = f32[256,256]{1,0:T(8,128)S(1)} collective-permute-done((f32[256,256]{1,0:T(8,128)S(1)}, f32[256,256]{1,0:T(8,128)S(1)}, u32[]{:S(2)}, u32[]{:S(2)}) %collective-permute-start.3) | collective-permute-done | bytes 262176 | tf_op jit(solution)/shard_map/vectors_along_z/ppermute | solution.py:244
  55.4 1.3 collective-permute-start.10
  56.8 5.8 %collective-permute-done.13.even.refs_24_ = f32[256,256]{1,0:T(8,128)S(1)} collective-permute-done((f32[256,256]{1,0:T(8,128)S(1)}, f32[256,256]{1,0:T(8,128)S(1)}, u32[]{:S(2)}, u32[]{:S(2)}) %collective-permute-start.13) | collective-permute-done | bytes 262176 | tf_op jit(solution)/shard_map/vectors_along_z/ppermute | solution.py:244
  63.2 1.3 collective-permute-start.15
  64.5 2.9 %collective-permute-done.10.refs_4_ = f32[256,256]{1,0:T(8,128)S(1)} collective-permute-done((f32[256,256]{1,0:T(8,128)S(1)}, f32[256,256]{1,0:T(8,128)S(1)}, u32[]{:S(2)}, u32[]{:S(2)}) %collective-permute-start.10) | collective-permute-done | bytes 262176 | tf_op jit(solution)/shard_map/vectors_along_z/ppermute | solution.py:248
  67.4 1.3 collective-permute-start.11
  68.7 4.8 %collective-permute-done.15.refs_9_ = f32[256,256]{1,0:T(8,128)S(1)} collective-permute-done((f32[256,256]{1,0:T(8,128)S(1)}, f32[256,256]{1,0:T(8,128)S(1)}, u32[]{:S(2)}, u32[]{:S(2)}) %collective-permute-start.15) | collective-permute-done | bytes 262176 | tf_op jit(solution)/shard_map/vectors_along_z/ppermute | solution.py:248
  73.5 1.3 collective-permute-start.16
  74.8 3.9 %collective-permute-done.11.refs_14_ = f32[256,256]{1,0:T(8,128)S(1)} collective-permute-done((f32[256,256]{1,0:T(8,128)S(1)}, f32[256,256]{1,0:T(8,128)S(1)}, u32[]{:S(2)}, u32[]{:S(2)}) %collective-permute-start.11) | collective-permute-done | bytes 262176 | tf_op jit(solution)/shard_map/vectors_along_z/ppermute | solution.py:248
  78.7 1.3 collective-permute-start.18
  80.0 4.6 %collective-permute-done.16.refs_19_ = f32[256,256]{1,0:T(8,128)S(1)} collective-permute-done((f32[256,256]{1,0:T(8,128)S(1)}, f32[256,256]{1,0:T(8,128)S(1)}, u32[]{:S(2)}, u32[]{:S(2)}) %collective-permute-start.16) | collective-permute-done | bytes 262176 | tf_op jit(solution)/shard_map/vectors_along_z/ppermute | solution.py:248
  84.5 1.3 collective-permute-start.17
  85.8 1.8 %add_chunks.4.refs_30_ = f32[2,192,256]{2,1,0:T(8,128)S(1)} custom-call(s32[5]{0:T(128)S(1)} %stack.19.info, f32[48,4096]{1,0:T(8,128)S(1)} %get-tuple-element.44.refs_0_.refs_5_.refs_10_.refs_15_.refs_20_.refs_25_, f32[48,4096]{1,0:T(8,128)S(1)} %collective-permute-done.7.refs_1_.refs_6_.refs_11_.refs_16_.refs_21_.refs_26_, ...), custom_call_target="tpu_custom_call" | custom-call | flops 754974720 | bytes 4194304 | tf_op jit(solution)/shard_map/add_chunks/pallas_call | solution.py:117
  87.6 1.7 %add_chunks.5.refs_25_ = f32[2,192,256]{2,1,0:T(8,128)S(1)} custom-call(s32[5]{0:T(128)S(1)} %stack.19.info, f32[48,4096]{1,0:T(8,128)S(1)} %get-tuple-element.44.refs_0_.refs_5_.refs_10_.refs_15_.refs_20_.refs_25_, f32[48,4096]{1,0:T(8,128)S(1)} %collective-permute-done.7.refs_1_.refs_6_.refs_11_.refs_16_.refs_21_.refs_26_, ...), custom_call_target="tpu_custom_call", output_to_operand_aliasing={{}: (31, {})} | custom-call | flops 603979776 | bytes 4194304 | tf_op jit(solution)/shard_map/add_chunks/pallas_call | solution.py:117
  89.4 1.9 %add_chunks.6.refs_5_ = f32[2,192,256]{2,1,0:T(8,128)S(1)} custom-call(s32[5]{0:T(128)S(1)} %stack.19.info, f32[48,4096]{1,0:T(8,128)S(1)} %get-tuple-element.44.refs_0_.refs_5_.refs_10_.refs_15_.refs_20_.refs_25_, f32[48,4096]{1,0:T(8,128)S(1)} %collective-permute-done.7.refs_1_.refs_6_.refs_11_.refs_16_.refs_21_.refs_26_, ...), custom_call_target="tpu_custom_call", output_to_operand_aliasing={{}: (26, {})} | custom-call | flops 377487360 | bytes 4194304 | tf_op jit(solution)/shard_map/add_chunks/pallas_call | solution.py:117
  91.4 4.0 %collective-permute-done.17.refs_4_ = f32[256,256]{1,0:T(8,128)S(1)} collective-permute-done((f32[256,256]{1,0:T(8,128)S(1)}, f32[256,256]{1,0:T(8,128)S(1)}, u32[]{:S(2)}, u32[]{:S(2)}) %collective-permute-start.17) | collective-permute-done | bytes 262176 | tf_op jit(solution)/shard_map/vectors_along_z/ppermute | solution.py:248
  96.4 20.5 %all_to_all.5 = f32[32,24,128]{2,1,0:T(8,128)S(1)} all-to-all(f32[32,24,128]{2,1,0:T(8,128)S(1)} %add_chunks.7), channel_id=1, replica_groups=mesh['z'=8,'y'=4,'x'=4,'half'=2,'core'=2] {'y','x','core'}, dimensions={0} | all-to-all | bytes 786432 | tf_op jit(solution)/shard_map/sum_over_columns/all_to_all | solution.py:256
  116.9 12.3 %collective-permute-start.19 = (f32[24,128]{1,0:T(8,128)S(1)}, f32[24,128]{1,0:T(8,128)S(1)}, u32[]{:S(2)}, u32[]{:S(2)}) collective-permute-start(f32[24,128]{1,0:T(8,128)S(1)} %reduce_sum.9.mine), channel_id=1, source_target_pairs={{0,2},{2,0},{1,3},{3,1},{4,6},{6,4},{5,7},{7,5},{8,10},{10,8},{9,1... | collective-permute-start | bytes 36872 | tf_op jit(solution)/shard_map/sum_over_columns/ppermute | solution.py:196
  (25 shorter events, 8.0 us)
Async XLA Ops:
  0.0 11.7 %collective-permute-start.4 = (f32[512,256]{1,0:T(8,128)}, f32[512,256]{1,0:T(8,128)S(1)}, u32[]{:S(2)}, u32[]{:S(2)}) collective-permute-start(f32[512,256]{1,0:T(8,128)} %refs_4_.1), channel_id=1, source_target_pairs={{0,64},{128,192},{256,320},{384,448},{64,0},{192,128},{320,256},{4... | collective-permute-start | bytes 1572872 | tf_op jit(solution)/shard_map/vectors_along_z/ppermute | solution.py:238
  4.4 8.1 %collective-permute-start = (f32[512,256]{1,0:T(8,128)}, f32[512,256]{1,0:T(8,128)S(1)}, u32[]{:S(2)}, u32[]{:S(2)}) collective-permute-start(f32[512,256]{1,0:T(8,128)} %refs_4_.1), channel_id=1, source_target_pairs={{64,128},{192,256},{320,384},{128,64},{256,192},{384,320},{65,129}... | collective-permute-start | bytes 1572872 | tf_op jit(solution)/shard_map/vectors_along_z/ppermute | solution.py:238
  5.8 1.9 %copy-start = (f32[48,16384]{1,0:T(8,128)S(1)}, f32[48,16384]{1,0:T(8,128)}, u32[]{:S(2)}) copy-start(f32[48,16384]{1,0:T(8,128)} %slab) | copy-start | bytes 9437188
  7.7 78.1 %copy-start.1 = (f32[512,256]{1,0:T(8,128)S(1)}, f32[512,256]{1,0:T(8,128)}, u32[]{:S(2)}) copy-start(f32[512,256]{1,0:T(8,128)} %refs_4_.1) | copy-start | bytes 1572868
  11.7 13.4 %collective-permute-start.5 = (f32[512,256]{1,0:T(8,128)S(1)}, f32[512,256]{1,0:T(8,128)S(1)}, u32[]{:S(2)}, u32[]{:S(2)}) collective-permute-start(f32[512,256]{1,0:T(8,128)S(1)} %collective-permute-done.4.refs_9_), channel_id=1, source_target_pairs={{64,128},{192,256},{320,384},{128,64},{256,192},{384,320},{65,129}... | collective-permute-start | bytes 1572872 | tf_op jit(solution)/shard_map/vectors_along_z/ppermute | solution.py:238
  12.4 20.8 %collective-permute-start.1 = (f32[512,256]{1,0:T(8,128)S(1)}, f32[512,256]{1,0:T(8,128)S(1)}, u32[]{:S(2)}, u32[]{:S(2)}) collective-permute-start(f32[512,256]{1,0:T(8,128)S(1)} %collective-permute-done.refs_14_), channel_id=1, source_target_pairs={{128,192},{256,320},{384,448},{64,0},{192,128},{320,256},{129,193}... | collective-permute-start | bytes 1572872 | tf_op jit(solution)/shard_map/vectors_along_z/ppermute | solution.py:238
  13.7 23.1 %collective-permute-start.7 = (f32[48,4096]{1,0:T(8,128)S(1)}, f32[48,4096]{1,0:T(8,128)S(1)}, u32[]{:S(2)}, u32[]{:S(2)}) collective-permute-start(f32[48,4096]{1,0:T(8,128)S(1)} %get-tuple-element.36), channel_id=1, source_target_pairs={{0,16},{16,0},{32,48},{48,32},{1,17},{17,1},{33,49},{49,33},{2,18}... | collective-permute-start | bytes 2359304 | tf_op jit(solution)/shard_map/basis_along_y/ppermute | solution.py:223
  21.3 20.5 %collective-permute-start.8 = (f32[48,4096]{1,0:T(8,128)S(1)}, f32[48,4096]{1,0:T(8,128)S(1)}, u32[]{:S(2)}, u32[]{:S(2)}) collective-permute-start(f32[48,4096]{1,0:T(8,128)S(1)} %get-tuple-element.37), channel_id=1, source_target_pairs={{0,48},{16,32},{32,16},{48,0},{1,49},{17,33},{33,17},{49,1},{2,50}... | collective-permute-start | bytes 2359304 | tf_op jit(solution)/shard_map/basis_along_y/ppermute | solution.py:223
  25.2 19.3 %collective-permute-start.6 = (f32[512,256]{1,0:T(8,128)S(1)}, f32[512,256]{1,0:T(8,128)S(1)}, u32[]{:S(2)}, u32[]{:S(2)}) collective-permute-start(f32[512,256]{1,0:T(8,128)S(1)} %collective-permute-done.5.refs_24_), channel_id=1, source_target_pairs={{128,192},{256,320},{384,448},{64,0},{192,128},{320,256},{129,193}... | collective-permute-start | bytes 1572872 | tf_op jit(solution)/shard_map/vectors_along_z/ppermute | solution.py:238
  33.2 12.0 %collective-permute-start.2 = (f32[512,256]{1,0:T(8,128)S(1)}, f32[512,256]{1,0:T(8,128)S(1)}, u32[]{:S(2)}, u32[]{:S(2)}) collective-permute-start(f32[512,256]{1,0:T(8,128)S(1)} %collective-permute-done.1.refs_19_), channel_id=1, source_target_pairs={{192,256},{320,384},{128,64},{256,192},{193,257},{321,385},{129,65... | collective-permute-start | bytes 1572872 | tf_op jit(solution)/shard_map/vectors_along_z/ppermute | solution.py:238
  44.5 8.9 %collective-permute-start.9 = (f32[256,256]{1,0:T(8,128)S(1)}, f32[256,256]{1,0:T(8,128)S(1)}, u32[]{:S(2)}, u32[]{:S(2)}) collective-permute-start(f32[256,256]{1,0:T(8,128)S(1)} %get-tuple-element.39), channel_id=1, source_target_pairs={{192,256},{320,384},{128,64},{256,192},{193,257},{321,385},{129,65... | collective-permute-start | bytes 786440 | tf_op jit(solution)/shard_map/vectors_along_z/ppermute | solution.py:245
  45.2 9.7 %collective-permute-start.3 = (f32[256,256]{1,0:T(8,128)S(1)}, f32[256,256]{1,0:T(8,128)S(1)}, u32[]{:S(2)}, u32[]{:S(2)}) collective-permute-start(f32[256,256]{1,0:T(8,128)S(1)} %get-tuple-element.35), channel_id=1, source_target_pairs={{256,320},{384,448},{64,0},{192,128},{257,321},{385,449},{65,1},{1... | collective-permute-start | bytes 786440 | tf_op jit(solution)/shard_map/vectors_along_z/ppermute | solution.py:244
  46.5 28.2 %collective-permute-start.12 = (f32[48,4096]{1,0:T(8,128)S(1)}, f32[48,4096]{1,0:T(8,128)S(1)}, u32[]{:S(2)}, u32[]{:S(2)}) collective-permute-start(f32[48,4096]{1,0:T(8,128)S(1)} %get-tuple-element.42), channel_id=1, source_target_pairs={{0,32},{16,48},{32,0},{48,16},{1,33},{17,49},{33,1},{49,17},{2,34}... | collective-permute-start | bytes 2359304 | tf_op jit(solution)/shard_map/basis_along_y/ppermute | solution.py:223
  51.3 5.4 %collective-permute-start.14 = (f32[256,256]{1,0:T(8,128)S(1)}, f32[256,256]{1,0:T(8,128)S(1)}, u32[]{:S(2)}, u32[]{:S(2)}) collective-permute-start(f32[256,256]{1,0:T(8,128)S(1)} %get-tuple-element.49), channel_id=1, source_target_pairs={{192,256},{320,384},{128,64},{256,192},{193,257},{321,385},{129,65... | collective-permute-start | bytes 786440 | tf_op jit(solution)/shard_map/vectors_along_z/ppermute | solution.py:245
  52.0 10.6 %collective-permute-start.13 = (f32[256,256]{1,0:T(8,128)S(1)}, f32[256,256]{1,0:T(8,128)S(1)}, u32[]{:S(2)}, u32[]{:S(2)}) collective-permute-start(f32[256,256]{1,0:T(8,128)S(1)} %get-tuple-element.48), channel_id=1, source_target_pairs={{256,320},{384,448},{64,0},{192,128},{257,321},{385,449},{65,1},{1... | collective-permute-start | bytes 786440 | tf_op jit(solution)/shard_map/vectors_along_z/ppermute | solution.py:244
  55.4 12.0 %collective-permute-start.10 = (f32[256,256]{1,0:T(8,128)S(1)}, f32[256,256]{1,0:T(8,128)S(1)}, u32[]{:S(2)}, u32[]{:S(2)}) collective-permute-start(f32[256,256]{1,0:T(8,128)S(1)} %select.2), channel_id=1, source_target_pairs={{256,320},{320,384},{384,448},{64,0},{128,64},{192,128},{257,321},... | collective-permute-start | bytes 786440 | tf_op jit(solution)/shard_map/vectors_along_z/ppermute | solution.py:248
  63.2 10.3 %collective-permute-start.15 = (f32[256,256]{1,0:T(8,128)S(1)}, f32[256,256]{1,0:T(8,128)S(1)}, u32[]{:S(2)}, u32[]{:S(2)}) collective-permute-start(f32[256,256]{1,0:T(8,128)S(1)} %select.3), channel_id=1, source_target_pairs={{256,320},{320,384},{384,448},{64,0},{128,64},{192,128},{257,321},... | collective-permute-start | bytes 786440 | tf_op jit(solution)/shard_map/vectors_along_z/ppermute | solution.py:248
  67.4 11.2 %collective-permute-start.11 = (f32[256,256]{1,0:T(8,128)S(1)}, f32[256,256]{1,0:T(8,128)S(1)}, u32[]{:S(2)}, u32[]{:S(2)}) collective-permute-start(f32[256,256]{1,0:T(8,128)S(1)} %collective-permute-done.10.refs_4_), channel_id=1, source_target_pairs={{320,384},{384,448},{64,0},{128,64},{321,385},{385,449},{65,1},{12... | collective-permute-start | bytes 786440 | tf_op jit(solution)/shard_map/vectors_along_z/ppermute | solution.py:248
  73.5 11.0 %collective-permute-start.16 = (f32[256,256]{1,0:T(8,128)S(1)}, f32[256,256]{1,0:T(8,128)S(1)}, u32[]{:S(2)}, u32[]{:S(2)}) collective-permute-start(f32[256,256]{1,0:T(8,128)S(1)} %collective-permute-done.15.refs_9_), channel_id=1, source_target_pairs={{320,384},{384,448},{64,0},{128,64},{321,385},{385,449},{65,1},{12... | collective-permute-start | bytes 786440 | tf_op jit(solution)/shard_map/vectors_along_z/ppermute | solution.py:248
  78.7 10.8 %collective-permute-start.18 = (f32[256,256]{1,0:T(8,128)S(1)}, f32[256,256]{1,0:T(8,128)S(1)}, u32[]{:S(2)}, u32[]{:S(2)}) collective-permute-start(f32[256,256]{1,0:T(8,128)S(1)} %collective-permute-done.11.refs_14_), channel_id=1, source_target_pairs={{384,448},{64,0},{385,449},{65,1},{386,450},{66,2},{387,451},{67,3... | collective-permute-start | bytes 786440 | tf_op jit(solution)/shard_map/vectors_along_z/ppermute | solution.py:248
  84.5 10.9 %collective-permute-start.17 = (f32[256,256]{1,0:T(8,128)S(1)}, f32[256,256]{1,0:T(8,128)S(1)}, u32[]{:S(2)}, u32[]{:S(2)}) collective-permute-start(f32[256,256]{1,0:T(8,128)S(1)} %collective-permute-done.16.refs_19_), channel_id=1, source_target_pairs={{384,448},{64,0},{385,449},{65,1},{386,450},{66,2},{387,451},{67,3... | collective-permute-start | bytes 786440 | tf_op jit(solution)/shard_map/vectors_along_z/ppermute | solution.py:248
  116.9 13.4 %collective-permute-start.19 = (f32[24,128]{1,0:T(8,128)S(1)}, f32[24,128]{1,0:T(8,128)S(1)}, u32[]{:S(2)}, u32[]{:S(2)}) collective-permute-start(f32[24,128]{1,0:T(8,128)S(1)} %reduce_sum.9.mine), channel_id=1, source_target_pairs={{0,2},{2,0},{1,3},{3,1},{4,6},{6,4},{5,7},{7,5},{8,10},{10,8},{9,1... | collective-permute-start | bytes 36872 | tf_op jit(solution)/shard_map/sum_over_columns/ppermute | solution.py:196
